TPU v7x, 32 devices: a whole 2x2x4 slice. The times are simulated.
32 devices in a mesh: dp: 16 (over z, x, core), seq: 2 (over y).
Axes of the slice: x: 2, y: 2, z: 4, core: 2. Of those that a mesh axis runs over, the one named last changes fastest.
Arguments:
- inputs: bfloat16 [2, 16, 1024, 896], P(None, 'dp', 'seq'), may hold values from -6 to 6
- cotangent: bfloat16 [2, 16, 1024, 896], P(None, 'dp', 'seq'), may hold values from -6 to 6
- starts: int32 [2, 16, 6], P(None, 'dp'), may hold values from 0 to 1023, as said below
- query_weight: float32 [896, 896], P(('dp', 'seq')), may hold values from -0.1875 to 0.1875
- key_weight: float32 [896, 128], P(('dp', 'seq')), may hold values from -0.1875 to 0.1875
- value_weight: float32 [896, 128], P(('dp', 'seq')), may hold values from -0.1875 to 0.1875
- out_weight: float32 [896, 896], P(None, ('dp', 'seq')), may hold values from -0.5 to 0.5
- gate_weight: float32 [896, 4864], P(('dp', 'seq')), may hold values from -0.1875 to 0.1875
- up_weight: float32 [896, 4864], P(('dp', 'seq')), may hold values from -0.1875 to 0.1875
- down_weight: float32 [4864, 896], P(None, ('dp', 'seq')), may hold values from -0.078125 to 0.078125
- vectors: float32 [2944], P(('dp', 'seq')), may hold values from -1 to 1.6, as said below
- owner_slot: int32 [130], replicated, may hold values from 0 to 159, as said below
- first_moment: float32 [160, 896, 128], P(('dp', 'seq')), may hold values from -48 to 48
- second_moment: float32 [160, 896, 128], P(('dp', 'seq')), may hold values from 2.62144 to 39.3216
- basis_left: float32 [160, 128, 128], P(('dp', 'seq')), may hold values from -0.5 to 0.5
- basis_right: float32 [160, 128, 128], P(('dp', 'seq')), may hold values from -0.5 to 0.5
- vector_first: float32 [2944], P(('dp', 'seq')), may hold values from -160 to 160
- vector_second: float32 [2944], P(('dp', 'seq')), may hold values from 98.304 to 983.04
Outputs:
- output: bfloat16 [2, 16, 1024, 896], P(None, 'dp', 'seq')
- input_grad: float32 [2, 16, 1024, 896], P(None, 'dp', 'seq')
- grad_query: float32 [896, 896], P(('dp', 'seq'))
- grad_key: float32 [896, 128], P(('dp', 'seq'))
- grad_value: float32 [896, 128], P(('dp', 'seq'))
- grad_out: float32 [896, 896], P(None, ('dp', 'seq'))
- grad_gate: float32 [896, 4864], P(('dp', 'seq'))
- grad_up: float32 [896, 4864], P(('dp', 'seq'))
- grad_down: float32 [4864, 896], P(None, ('dp', 'seq'))
- grad_vectors: float32 [2944], P(('dp', 'seq'))
- new_first: float32 [160, 896, 128], P(('dp', 'seq'))
- new_second: float32 [160, 896, 128], P(('dp', 'seq'))
- new_blocks: float32 [160, 896, 128], P(('dp', 'seq'))
- vector_second_new: float32 [2944], P(('dp', 'seq'))
- vector_new: float32 [2944], P(('dp', 'seq'))
Inputs may be any that keep to these rules, and one draw needn't show every extreme that they name: In each stream the first start is 0, the starts rise strictly, and none equals 512. All values differ; block b sits in slot owner_slot[b] % 5 of device owner_slot[b] // 5 along dp+seq. `vectors`: the first 1792 entries are the gains.
All inputs are finite; a program needn't handle non-finite values.
Results may differ from a plain program's by a relative error of at most 0.013.
The roundings to bfloat16 on the way count: a program that leaves them out, or rounds other values in their place, can miss the bound.
Values may be sent and summed in bfloat16 or wider, within the bound.
A program may use at most 320 MiB of HBM per device.

v0:
```python
import math

import jax
import jax.numpy as jnp
from jax import lax
from jax.sharding import PartitionSpec as P

D = 896
QUERY_HEADS = 14
KEY_VALUE_HEADS = 2
HEAD_SIZE = 64
BW = 128
MICRO = 2
STEP = 10
QW = 896
KW = 128


norm_epsilon = 1e-06
rope_theta = 1000000.0
beta_first = 0.9
beta_second = 0.999
adam_epsilon = 1e-08
weight_decay = 0.01
rate_matrix = 0.1
rate_vector = 0.5
masked_value = -1e30


def contract_rows(former, latter):
    return lax.dot_general(
        former, latter, (((0,), (0,)), ((), ())), preferred_element_type=jnp.float32
    )


def contract_cols(former, latter):
    return lax.dot_general(
        former, latter, (((1,), (1,)), ((), ())), preferred_element_type=jnp.float32
    )


def split_vectors(vectors_full):
    gain_attn = vectors_full[:D]
    gain_mlp = vectors_full[D : 2 * D]
    bias_query = vectors_full[2 * D : 2 * D + QW]
    bias_key = vectors_full[2 * D + QW : 2 * D + QW + KW]
    bias_value = vectors_full[2 * D + QW + KW :]
    return (gain_attn, gain_mlp, bias_query, bias_key, bias_value)


def rotary_embedding(values, cosine_values, sine_values):
    half_size = values.shape[-1] // 2
    lower_half = values[..., :half_size]
    upper_half = values[..., half_size:]
    return jnp.concatenate(
        [
            lower_half * cosine_values - upper_half * sine_values,
            upper_half * cosine_values + lower_half * sine_values,
        ],
        axis=-1,
    )


def angle_tables(places, starts):
    before = starts[None, :] <= places[:, None]
    doc_begin = jnp.max(jnp.where(before, starts[None, :], 0), axis=1)
    relative = (places - doc_begin).astype(jnp.float32)
    frequency = jnp.power(rope_theta, -jnp.arange(0, HEAD_SIZE, 2, dtype=jnp.float32) / HEAD_SIZE)
    angles = relative[:, None] * frequency[None, :]
    return (jnp.cos(angles)[:, None, :], jnp.sin(angles)[:, None, :])


def doc_numbers(places, starts):
    return jnp.sum((starts[None, :] <= places[:, None]).astype(jnp.int32), axis=1)


def column_blocks(matrix):
    return matrix.reshape(matrix.shape[0], -1, BW).transpose(1, 0, 2)


def row_blocks(matrix):
    return matrix.reshape(-1, BW, matrix.shape[1]).transpose(0, 2, 1)


def local_blocks(query_m, key_m, value_m, out_m, gate_m, up_m, down_m):
    return jnp.concatenate(
        [
            column_blocks(query_m),
            column_blocks(key_m),
            column_blocks(value_m),
            row_blocks(out_m),
            column_blocks(gate_m),
            column_blocks(up_m),
            row_blocks(down_m),
        ],
        axis=0,
    )


def rotate_into(left_side, tile_view, right_side):
    half_turn = jnp.einsum("sba,stbe->stae", left_side, tile_view, precision=lax.Precision.HIGHEST)
    return jnp.einsum("stae,sef->staf", half_turn, right_side, precision=lax.Precision.HIGHEST)


def rotate_back(left_side, tile_view, right_side):
    half_turn = jnp.einsum("sab,stbe->stae", left_side, tile_view, precision=lax.Precision.HIGHEST)
    return jnp.einsum("stae,sfe->staf", half_turn, right_side, precision=lax.Precision.HIGHEST)


def rotated_adam(
    block_grads, block_weights, first_moment, second_moment, basis_left, basis_right, slot_used
):
    slot_total = block_grads.shape[0]
    tile_view = block_grads.reshape(slot_total, -1, BW, BW)
    rotated = rotate_into(basis_left, tile_view, basis_right).reshape(block_grads.shape)
    first_new = beta_first * first_moment + (1.0 - beta_first) * rotated
    second_new = beta_second * second_moment + (1.0 - beta_second) * rotated * rotated
    step_size = (
        first_new
        / (1.0 - beta_first**STEP)
        / (jnp.sqrt(second_new / (1.0 - beta_second**STEP)) + adam_epsilon)
    )
    turned = rotate_back(
        basis_left, step_size.reshape(slot_total, -1, BW, BW), basis_right
    ).reshape(block_grads.shape)
    updated = block_weights - rate_matrix * (turned + weight_decay * block_weights)
    used_mask = slot_used[:, None, None]
    return (
        jnp.where(used_mask, first_new, 0.0),
        jnp.where(used_mask, second_new, 0.0),
        jnp.where(used_mask, updated, 0.0),
    )


def vector_adam(vectors, grad_vectors, vector_first, vector_second):
    first_new = beta_first * vector_first + (1.0 - beta_first) * grad_vectors
    second_new = beta_second * vector_second + (1.0 - beta_second) * grad_vectors * grad_vectors
    step_size = (
        first_new
        / (1.0 - beta_first**STEP)
        / (jnp.sqrt(second_new / (1.0 - beta_second**STEP)) + adam_epsilon)
    )
    return (second_new, vectors - rate_vector * step_size)


def block_scores(query_block, key_view, block_start, block_rows, doc_all, columns):
    score_scale = 1.0 / math.sqrt(HEAD_SIZE)
    scores = (
        jnp.einsum("ikgd,jkd->kgij", query_block, key_view, preferred_element_type=jnp.float32)
        * score_scale
    )
    rows_here = block_start + jnp.arange(block_rows, dtype=jnp.int32)
    doc_rows = lax.dynamic_slice_in_dim(doc_all, block_start, block_rows, 0)
    allowed = (doc_rows[:, None] == doc_all[None, :]) & (columns[None, :] <= rows_here[:, None])
    return jnp.where(allowed, scores, masked_value)


def head_views(query_heads, key_heads, value_heads):
    length = query_heads.shape[0]
    kv_local = key_heads.shape[1] // HEAD_SIZE
    query_group_width = QUERY_HEADS // KEY_VALUE_HEADS
    query_rows = query_heads.reshape(length, kv_local, query_group_width, HEAD_SIZE)
    key_view = key_heads.reshape(length, kv_local, HEAD_SIZE)
    value_view = value_heads.reshape(length, kv_local, HEAD_SIZE)
    return (query_rows, key_view, value_view)


def attend_forward(query_heads, key_heads, value_heads, doc_all):
    length = query_heads.shape[0]
    block_rows = min(512, length)
    query_rows, key_view, value_view = head_views(query_heads, key_heads, value_heads)
    columns = jnp.arange(length, dtype=jnp.int32)

    def one_block(block_start):
        query_block = lax.dynamic_slice_in_dim(query_rows, block_start, block_rows, 0)
        scores = block_scores(query_block, key_view, block_start, block_rows, doc_all, columns)
        row_max = jnp.max(scores, axis=-1, keepdims=True)
        exp_scores = jnp.exp(scores - row_max)
        row_total = jnp.sum(exp_scores, axis=-1, keepdims=True)
        attn_probs = exp_scores / row_total
        attention_output = jnp.einsum(
            "kgij,jkd->ikgd",
            attn_probs.astype(jnp.bfloat16),
            value_view,
            preferred_element_type=jnp.float32,
        )
        return (
            attention_output.astype(jnp.bfloat16).reshape(block_rows, -1),
            (row_max + jnp.log(row_total))[..., 0],
        )

    block_starts = jnp.arange(0, length, block_rows, dtype=jnp.int32)
    attention_output, log_totals = lax.map(one_block, block_starts)
    return (attention_output.reshape(length, -1), log_totals)


def attend_backward(query_heads, key_heads, value_heads, doc_all, log_totals, d_attended):
    length = query_heads.shape[0]
    block_rows = min(512, length)
    query_rows, key_view, value_view = head_views(query_heads, key_heads, value_heads)
    grad_view = d_attended.reshape(query_rows.shape)
    columns = jnp.arange(length, dtype=jnp.int32)
    score_scale = 1.0 / math.sqrt(HEAD_SIZE)

    def one_block(carried, block_inputs):
        d_key_acc, d_value_acc = carried
        block_start, log_block = block_inputs
        query_block = lax.dynamic_slice_in_dim(query_rows, block_start, block_rows, 0)
        grad_block = lax.dynamic_slice_in_dim(grad_view, block_start, block_rows, 0)
        scores = block_scores(query_block, key_view, block_start, block_rows, doc_all, columns)
        attn_probs = jnp.exp(scores - log_block[..., None])
        d_probs = jnp.einsum(
            "ikgd,jkd->kgij", grad_block, value_view, preferred_element_type=jnp.float32
        )
        row_dot = jnp.sum(attn_probs * d_probs, axis=-1, keepdims=True)
        d_scores = (attn_probs * (d_probs - row_dot)).astype(jnp.bfloat16)
        d_query = (
            jnp.einsum("kgij,jkd->ikgd", d_scores, key_view, preferred_element_type=jnp.float32)
            * score_scale
        )
        d_key_acc = (
            d_key_acc
            + jnp.einsum(
                "kgij,ikgd->jkd", d_scores, query_block, preferred_element_type=jnp.float32
            )
            * score_scale
        )
        d_value_acc = d_value_acc + jnp.einsum(
            "kgij,ikgd->jkd",
            attn_probs.astype(jnp.bfloat16),
            grad_block,
            preferred_element_type=jnp.float32,
        )
        return ((d_key_acc, d_value_acc), d_query.astype(jnp.bfloat16).reshape(block_rows, -1))

    zero_acc = jnp.zeros(key_view.shape, jnp.float32)
    block_starts = jnp.arange(0, length, block_rows, dtype=jnp.int32)
    (d_key_acc, d_value_acc), d_query = lax.scan(
        one_block, (zero_acc, zero_acc), (block_starts, log_totals)
    )
    return (
        d_query.reshape(length, -1),
        d_key_acc.astype(jnp.bfloat16).reshape(length, -1),
        d_value_acc.astype(jnp.bfloat16).reshape(length, -1),
    )


def layer_forward(params_low, tokens, starts_row, seq_index):
    (
        query_weight,
        key_weight,
        value_weight,
        out_weight,
        gate_weight,
        up_weight,
        down_weight,
        vectors_low,
    ) = params_low
    gain_attn, gain_mlp, bias_query, bias_key, bias_value = split_vectors(
        vectors_low.astype(jnp.float32)
    )
    local_rows_count = tokens.shape[0]
    length = local_rows_count * lax.axis_size("seq")
    inputs_f = tokens.astype(jnp.float32)
    inv_attn = lax.rsqrt(jnp.mean(inputs_f * inputs_f, axis=1, keepdims=True) + norm_epsilon)
    normed_low = (inputs_f * inv_attn * gain_attn).astype(jnp.bfloat16)
    places = seq_index * local_rows_count + jnp.arange(local_rows_count, dtype=jnp.int32)
    cosine_values, sine_values = angle_tables(places, starts_row)
    query_lin = jnp.dot(normed_low, query_weight, preferred_element_type=jnp.float32) + bias_query
    key_projected = jnp.dot(normed_low, key_weight, preferred_element_type=jnp.float32) + bias_key
    value_reduced = (
        jnp.dot(normed_low, value_weight, preferred_element_type=jnp.float32) + bias_value
    ).astype(jnp.bfloat16)
    rotated_queries = rotary_embedding(
        query_lin.reshape(local_rows_count, QUERY_HEADS, HEAD_SIZE), cosine_values, sine_values
    )
    rotated_queries = rotated_queries.reshape(local_rows_count, QW).astype(jnp.bfloat16)
    rotated_keys = rotary_embedding(
        key_projected.reshape(local_rows_count, KEY_VALUE_HEADS, HEAD_SIZE),
        cosine_values,
        sine_values,
    )
    rotated_keys = rotated_keys.reshape(local_rows_count, KW).astype(jnp.bfloat16)
    query_heads, key_heads, value_heads = (
        lax.all_to_all(rotated_queries, "seq", split_axis=1, concat_axis=0, tiled=True),
        lax.all_to_all(rotated_keys, "seq", split_axis=1, concat_axis=0, tiled=True),
        lax.all_to_all(value_reduced, "seq", split_axis=1, concat_axis=0, tiled=True),
    )
    doc_all = doc_numbers(jnp.arange(length, dtype=jnp.int32), starts_row)
    attended_heads, log_totals = attend_forward(query_heads, key_heads, value_heads, doc_all)
    attention_output = lax.all_to_all(
        attended_heads, "seq", split_axis=0, concat_axis=1, tiled=True
    )
    residual = inputs_f + jnp.dot(attention_output, out_weight, preferred_element_type=jnp.float32)
    inv_mlp = lax.rsqrt(jnp.mean(residual * residual, axis=1, keepdims=True) + norm_epsilon)
    normed_mlp = (residual * inv_mlp * gain_mlp).astype(jnp.bfloat16)
    gate_act = jnp.dot(normed_mlp, gate_weight, preferred_element_type=jnp.float32)
    up_act = jnp.dot(normed_mlp, up_weight, preferred_element_type=jnp.float32)
    hidden = (jax.nn.silu(gate_act) * up_act).astype(jnp.bfloat16)
    output = residual + jnp.dot(hidden, down_weight, preferred_element_type=jnp.float32)
    kept = (
        inputs_f,
        inv_attn,
        normed_low,
        cosine_values,
        sine_values,
        query_heads,
        key_heads,
        value_heads,
        doc_all,
        log_totals,
        attention_output,
        residual,
        inv_mlp,
        normed_mlp,
        gate_act,
        up_act,
        hidden,
    )
    return (output.astype(jnp.bfloat16), kept)


def layer_backward(params_low, kept, cotangent_rows):
    (
        query_weight,
        key_weight,
        value_weight,
        out_weight,
        gate_weight,
        up_weight,
        down_weight,
        vectors_low,
    ) = params_low
    gain_attn, gain_mlp, bias_query, bias_key, bias_value = split_vectors(
        vectors_low.astype(jnp.float32)
    )
    (
        inputs_f,
        inv_attn,
        normed_low,
        cosine_values,
        sine_values,
        query_heads,
        key_heads,
        value_heads,
        doc_all,
        log_totals,
        attention_output,
        residual,
        inv_mlp,
        normed_mlp,
        gate_act,
        up_act,
        hidden,
    ) = kept
    local_rows_count = inputs_f.shape[0]
    d_output = cotangent_rows.astype(jnp.float32)
    grad_down = contract_rows(hidden, cotangent_rows)
    d_hidden = contract_cols(cotangent_rows, down_weight)
    sigmoid_gate = jax.nn.sigmoid(gate_act)
    silu_gate = gate_act * sigmoid_gate
    d_gate = (d_hidden * up_act * sigmoid_gate * (1.0 + gate_act * (1.0 - sigmoid_gate))).astype(
        jnp.bfloat16
    )
    d_up = (d_hidden * silu_gate).astype(jnp.bfloat16)
    grad_gate = contract_rows(normed_mlp, d_gate)
    grad_up = contract_rows(normed_mlp, d_up)
    d_normed_mlp = contract_cols(d_gate, gate_weight) + contract_cols(d_up, up_weight)
    hat_mlp = residual * inv_mlp
    scaled_mlp = d_normed_mlp * gain_mlp
    d_gain_mlp = jnp.sum(d_normed_mlp * hat_mlp, axis=0)
    d_residual = d_output + inv_mlp * (
        scaled_mlp - hat_mlp * jnp.mean(scaled_mlp * hat_mlp, axis=1, keepdims=True)
    )
    d_residual_low = d_residual.astype(jnp.bfloat16)
    grad_out = contract_rows(attention_output, d_residual_low)
    d_attended = contract_cols(d_residual_low, out_weight).astype(jnp.bfloat16)
    d_attended_heads = lax.all_to_all(d_attended, "seq", split_axis=1, concat_axis=0, tiled=True)
    d_query_heads, d_key_heads, d_value_heads = attend_backward(
        query_heads, key_heads, value_heads, doc_all, log_totals, d_attended_heads
    )
    d_query_rot, rotated_key_gradient, d_value = (
        lax.all_to_all(d_query_heads, "seq", split_axis=0, concat_axis=1, tiled=True),
        lax.all_to_all(d_key_heads, "seq", split_axis=0, concat_axis=1, tiled=True),
        lax.all_to_all(d_value_heads, "seq", split_axis=0, concat_axis=1, tiled=True),
    )
    d_query_lin = rotary_embedding(
        d_query_rot.astype(jnp.float32).reshape(local_rows_count, QUERY_HEADS, HEAD_SIZE),
        cosine_values,
        -sine_values,
    )
    d_query_lin = d_query_lin.reshape(local_rows_count, QW).astype(jnp.bfloat16)
    d_key_lin = rotary_embedding(
        rotated_key_gradient.astype(jnp.float32).reshape(
            local_rows_count, KEY_VALUE_HEADS, HEAD_SIZE
        ),
        cosine_values,
        -sine_values,
    )
    d_key_lin = d_key_lin.reshape(local_rows_count, KW).astype(jnp.bfloat16)
    grad_query = contract_rows(normed_low, d_query_lin)
    grad_key = contract_rows(normed_low, d_key_lin)
    grad_value = contract_rows(normed_low, d_value)
    d_normed = (
        contract_cols(d_query_lin, query_weight)
        + contract_cols(d_key_lin, key_weight)
        + contract_cols(d_value, value_weight)
    )
    hat_attn = inputs_f * inv_attn
    scaled_attn = d_normed * gain_attn
    d_gain_attn = jnp.sum(d_normed * hat_attn, axis=0)
    input_grad = d_residual + inv_attn * (
        scaled_attn - hat_attn * jnp.mean(scaled_attn * hat_attn, axis=1, keepdims=True)
    )
    grad_vectors = jnp.concatenate(
        [
            d_gain_attn,
            d_gain_mlp,
            jnp.sum(d_query_lin.astype(jnp.float32), axis=0),
            jnp.sum(d_key_lin.astype(jnp.float32), axis=0),
            jnp.sum(d_value.astype(jnp.float32), axis=0),
        ]
    )
    return (
        input_grad,
        (grad_query, grad_key, grad_value, grad_out, grad_gate, grad_up, grad_down, grad_vectors),
    )


def on_device(
    inputs,
    cotangent,
    starts,
    query_weight,
    key_weight,
    value_weight,
    out_weight,
    gate_weight,
    up_weight,
    down_weight,
    vectors,
    owner_slot,
    first_moment,
    second_moment,
    basis_left,
    basis_right,
    vector_first,
    vector_second,
):
    query_low = query_weight.astype(jnp.bfloat16)
    key_low = key_weight.astype(jnp.bfloat16)
    value_reduced = value_weight.astype(jnp.bfloat16)
    out_low = out_weight.astype(jnp.bfloat16)
    gate_low = gate_weight.astype(jnp.bfloat16)
    up_low = up_weight.astype(jnp.bfloat16)
    down_low = down_weight.astype(jnp.bfloat16)
    vectors_low = vectors.astype(jnp.bfloat16)
    seq_index = lax.axis_index("seq")
    outputs = []
    input_grads = []
    shard_sum = None
    for batch_index in range(MICRO):
        params_low = (
            lax.all_gather(query_low, ("dp", "seq"), axis=0, tiled=True),
            lax.all_gather(key_low, ("dp", "seq"), axis=0, tiled=True),
            lax.all_gather(value_reduced, ("dp", "seq"), axis=0, tiled=True),
            lax.all_gather(out_low, ("dp", "seq"), axis=1, tiled=True),
            lax.all_gather(gate_low, ("dp", "seq"), axis=0, tiled=True),
            lax.all_gather(up_low, ("dp", "seq"), axis=0, tiled=True),
            lax.all_gather(down_low, ("dp", "seq"), axis=1, tiled=True),
            lax.all_gather(vectors_low, ("dp", "seq"), axis=0, tiled=True),
        )
        output_rows, kept = layer_forward(
            params_low, inputs[batch_index, 0], starts[batch_index, 0], seq_index
        )
        outputs.append(output_rows)
        params_back = (
            lax.all_gather(query_low, ("dp", "seq"), axis=0, tiled=True),
            lax.all_gather(key_low, ("dp", "seq"), axis=0, tiled=True),
            lax.all_gather(value_reduced, ("dp", "seq"), axis=0, tiled=True),
            lax.all_gather(out_low, ("dp", "seq"), axis=1, tiled=True),
            lax.all_gather(gate_low, ("dp", "seq"), axis=0, tiled=True),
            lax.all_gather(up_low, ("dp", "seq"), axis=0, tiled=True),
            lax.all_gather(down_low, ("dp", "seq"), axis=1, tiled=True),
            lax.all_gather(vectors_low, ("dp", "seq"), axis=0, tiled=True),
        )
        input_grad, gradients = layer_backward(params_back, kept, cotangent[batch_index, 0])
        input_grads.append(input_grad)
        g_query, g_key, g_value, g_out, g_gate, g_up, g_down, g_vectors = gradients
        shards = (
            lax.psum_scatter(g_query, ("dp", "seq"), scatter_dimension=0, tiled=True),
            lax.psum_scatter(g_key, ("dp", "seq"), scatter_dimension=0, tiled=True),
            lax.psum_scatter(g_value, ("dp", "seq"), scatter_dimension=0, tiled=True),
            lax.psum_scatter(g_out, ("dp", "seq"), scatter_dimension=1, tiled=True),
            lax.psum_scatter(g_gate, ("dp", "seq"), scatter_dimension=0, tiled=True),
            lax.psum_scatter(g_up, ("dp", "seq"), scatter_dimension=0, tiled=True),
            lax.psum_scatter(g_down, ("dp", "seq"), scatter_dimension=1, tiled=True),
            lax.psum_scatter(g_vectors, ("dp", "seq"), scatter_dimension=0, tiled=True),
        )
        if shard_sum is None:
            shard_sum = shards
        else:
            shard_sum = tuple((former + latter for former, latter in zip(shard_sum, shards)))
    grad_query, grad_key, grad_value, grad_out, grad_gate, grad_up, grad_down, grad_vectors = (
        shard_sum
    )
    grad_blocks = local_blocks(
        grad_query, grad_key, grad_value, grad_out, grad_gate, grad_up, grad_down
    )
    weight_blocks = local_blocks(
        query_weight, key_weight, value_weight, out_weight, gate_weight, up_weight, down_weight
    )
    capacity = first_moment.shape[0]
    slot_count = lax.axis_size(("dp", "seq")) * capacity
    block_count = owner_slot.shape[0]
    slot_block = (
        jnp.full((slot_count,), -1, jnp.int32)
        .at[owner_slot]
        .set(jnp.arange(block_count, dtype=jnp.int32))
    )
    slot_used = slot_block >= 0
    slot_index = jnp.maximum(slot_block, 0)
    send_mask = slot_used.astype(jnp.float32)[:, None, None]
    send_grads = jnp.take(grad_blocks, slot_index, axis=0) * send_mask
    send_weights = jnp.take(weight_blocks, slot_index, axis=0) * send_mask
    owned_grads, owned_weights = (
        lax.all_to_all(
            send_grads.astype(jnp.bfloat16), ("dp", "seq"), split_axis=0, concat_axis=1, tiled=True
        ).astype(send_grads.dtype),
        lax.all_to_all(
            send_weights.astype(jnp.bfloat16),
            ("dp", "seq"),
            split_axis=0,
            concat_axis=1,
            tiled=True,
        ).astype(send_weights.dtype),
    )
    local_used = lax.dynamic_slice_in_dim(
        slot_used, lax.axis_index(("dp", "seq")) * capacity, capacity, 0
    )
    new_first, new_second, new_blocks = rotated_adam(
        owned_grads, owned_weights, first_moment, second_moment, basis_left, basis_right, local_used
    )
    vector_second_new, vector_new = vector_adam(vectors, grad_vectors, vector_first, vector_second)
    output = jnp.stack(outputs)[:, None]
    input_grad_all = jnp.stack(input_grads)[:, None]
    return (
        output,
        input_grad_all,
        grad_query,
        grad_key,
        grad_value,
        grad_out,
        grad_gate,
        grad_up,
        grad_down,
        grad_vectors,
        new_first,
        new_second,
        new_blocks,
        vector_second_new,
        vector_new,
    )


def solution(mesh):
    return jax.shard_map(
        on_device,
        mesh=mesh,
        in_specs=(
            P(None, "dp", "seq", None),
            P(None, "dp", "seq", None),
            P(None, "dp", None),
            P(("dp", "seq"), None),
            P(("dp", "seq"), None),
            P(("dp", "seq"), None),
            P(None, ("dp", "seq")),
            P(("dp", "seq"), None),
            P(("dp", "seq"), None),
            P(None, ("dp", "seq")),
            P(("dp", "seq")),
            P(),
            P(("dp", "seq"), None, None),
            P(("dp", "seq"), None, None),
            P(("dp", "seq"), None, None),
            P(("dp", "seq"), None, None),
            P(("dp", "seq")),
            P(("dp", "seq")),
        ),
        out_specs=(
            P(None, "dp", "seq", None),
            P(None, "dp", "seq", None),
            P(("dp", "seq"), None),
            P(("dp", "seq"), None),
            P(("dp", "seq"), None),
            P(None, ("dp", "seq")),
            P(("dp", "seq"), None),
            P(("dp", "seq"), None),
            P(None, ("dp", "seq")),
            P(("dp", "seq")),
            P(("dp", "seq"), None, None),
            P(("dp", "seq"), None, None),
            P(("dp", "seq"), None, None),
            P(("dp", "seq")),
            P(("dp", "seq")),
        ),
        check_vma=False,
    )
```

profile of v0, /device:TPU:0, one launch (start us, length us, event | category | flops | bytes accessed | tf_op | source)
XLA Modules:
  0.0 2707.4 jit_solution(749614425941153429)
XLA Ops:
  14.5 71.2 %all-gather.1 = bf16[32,28,128]{2,1,0:T(8,128)(2,1)S(1)} all-gather(bf16[1,28,128]{2,1,0:T(8,128)(2,1)S(1)} %convert_bitcast_fusion.11), channel_id=1, replica_groups=mesh['dp'=16,'seq'=2] {'dp','seq'}, dimensions={0}, use_global_device_ids=true | all-gather | bytes 236544 | tf_op jit(solution)/shard_map/all_gather | solution.py:465
  86.0 37.2 %all-reduce = bf16[2944]{0:T(1024)(128)(2,1)S(1)} all-reduce(bf16[2944]{0:T(1024)(128)(2,1)S(1)} %dynamic-update-slice), channel_id=1, replica_groups=mesh['dp'=16,'seq'=2] {'dp','seq'}, use_global_device_ids=true, to_apply=%add | all-reduce | flops 2944 | bytes 11776
  132.3 69.2 %all-gather.2 = bf16[32,28,128]{2,1,0:T(8,128)(2,1)S(1)} all-gather(bf16[1,28,128]{2,1,0:T(8,128)(2,1)S(1)} %convert_bitcast_fusion.10), channel_id=1, replica_groups=mesh['dp'=16,'seq'=2] {'dp','seq'}, dimensions={0}, use_global_device_ids=true | all-gather | bytes 236544 | tf_op jit(solution)/shard_map/all_gather | solution.py:466
  297.9 32.9 %while.56 = (s32[]{:T(128)}, bf16[2,512,448]{1,2,0:T(8,128)(2,1)}, f32[2,1,7,512]{3,2,1,0:T(8,128)S(1)}, s32[2]{0:T(128)S(1)}, s32[1024]{0:T(1024)S(1)}, /*index...) while((s32[]{:T(128)}, bf16[2,512,448]{1,2,0:T(8,128)(2,1)}, ...), condition=%wide.region_6.7_spmd.clone, body=%wide.region_3.6_spmd.clone.sunk | while | flops 985363456 | bytes 55709932 | solution.py:193
  342.3 32.9 %while.57 = (s32[]{:T(128)}, bf16[2,512,448]{1,2,0:T(8,128)(2,1)}, f32[2,1,7,512]{3,2,1,0:T(8,128)S(1)}, s32[2]{0:T(128)S(1)}, s32[1024]{0:T(1024)S(1)}, /*index...) while((s32[]{:T(128)}, bf16[2,512,448]{1,2,0:T(8,128)(2,1)}, ...), condition=%wide.region_14.15_spmd.clone, body=%wide.region_11.14_spmd.clone.sunk | while | flops 985363456 | bytes 55709932 | solution.py:193
  383.9 11.1 all-to-all-done.7
  399.7 13.1 reshape.856
  412.8 12.9 reshape.858
  425.7 11.4 fusion.219
  445.0 13.0 reshape.860
  458.0 17.2 multiply_convert_fusion.2
  486.1 12.1 multiply_reduce_fusion.1
  506.2 11.3 fusion.222
  543.4 11.2 fusion.175
  554.7 17.4 multiply_convert_fusion
  572.1 11.0 fusion.167
  583.1 12.3 convolution_add_fusion.2
  595.4 409.1 %fusion.14 = f32[4864,32]{0,1:T(8,128)} fusion(f32[4864,896]{0,1:T(8,128)} %convolution_add_fusion.2), kind=kCustom, calls=%all-reduce-scatter.6 | all-reduce-scatter fusion | flops 4980737 | bytes 18055168
  1016.3 12.0 fusion.226
  1028.4 11.8 multiply_reduce_fusion
  1051.7 18.3 convolution_add_fusion.1
  1070.0 18.2 convolution_add_fusion
  1117.9 79.9 %while.58 = (s32[]{:T(128)}, f32[1024,1,64]{0,2,1:T(8,128)}, f32[1024,1,64]{0,2,1:T(8,128)}, bf16[2,512,448]{1,2,0:T(8,128)(2,1)}, s32[2]{0:T(128)S(1)}, /*index...) while((s32[]{:T(128)}, f32[1024,1,64]{0,2,1:T(8,128)}, ...), condition=%wide.region_19.20_spmd.clone, body=%wide.region_17.19_spmd.clone.sunk | while | flops 2384196608 | bytes 143677824 | solution.py:238
  1204.6 76.9 %while.59 = (s32[]{:T(128)}, f32[1024,1,64]{0,2,1:T(8,128)}, f32[1024,1,64]{0,2,1:T(8,128)}, bf16[2,512,448]{1,2,0:T(8,128)(2,1)}, s32[2]{0:T(128)S(1)}, /*index...) while((s32[]{:T(128)}, f32[1024,1,64]{0,2,1:T(8,128)}, ...), condition=%wide.region_24.25_spmd.clone, body=%wide.region_22.24_spmd.clone.sunk | while | flops 2384196608 | bytes 142104992 | solution.py:238
  1344.7 989.1 %fusion.214 = (f32[32,896]{1,0:T(8,128)}, f32[32,128]{1,0:T(8,128)}, f32[32,128]{1,0:T(8,128)S(1)}, f32[896,32]{0,1:T(8,128)}, f32[32,4864]{1,0:T(8,128)S(1)}, /*index=5*/f32[32,4864]{1,0:T(8,128)S(1)}) fusion(f32[896,896]{1,0:T(8,128)} %convolution_add_fusion.4, f32[896,128]{1,0:T(8,128)} %convolution_add_fusion.10, f32[896,128]{1,0:T(8,128)} %convolution_add_fusion.9, ...), kind=kCustom, calls=%all-reduce-scatter.7 | all-reduce-scatter fusion | flops 12058625 | bytes 43712512
  2338.5 14.9 collective-permute-start.6
  2377.2 20.6 concatenate.58
  2496.6 19.4 collective-permute-start.20
  2521.0 20.2 concatenate.56
  2542.4 20.3 concatenate.57
  2595.8 17.5 all-to-all-done.16
  2617.2 51.8 %all-reduce.8 = f32[2944]{0:T(1024)S(1)} all-reduce(f32[2944]{0:T(1024)S(1)} %add.457), channel_id=17, replica_groups=mesh['dp'=16,'seq'=2] {'dp','seq'}, use_global_device_ids=true, to_apply=%region_45.46.clone | all-reduce | flops 2944 | bytes 23552
  (741 shorter events, 719.6 us)
Async XLA Ops:
  7.2 244.2 %all-gather.13.cloned.1.call-start = ((), (), s32[]{:S(2)}) async-start(), calls=%async_computation.18 | async-start | bytes 1892352 | tf_op jit(solution)/shard_map/all_gather | solution.py:464
  9.0 265.2 %all-gather.15.cloned.1.call-start = ((), (), s32[]{:S(2)}) async-start(), calls=%async_computation.19 | async-start | bytes 1892352 | tf_op jit(solution)/shard_map/all_gather | solution.py:467
  10.6 389.1 %all-gather.17.cloned.1.call-start = ((), (), s32[]{:S(2)}) async-start(), calls=%async_computation.20 | async-start | bytes 10272768 | tf_op jit(solution)/shard_map/all_gather | solution.py:468
  12.5 400.3 %all-gather.19.cloned.1.call-start = ((), (), s32[]{:S(2)}) async-start(), calls=%async_computation.21 | async-start | bytes 10272768 | tf_op jit(solution)/shard_map/all_gather | solution.py:469
  127.4 98.9 %all-to-all-start.5 = ((bf16[512,2,64]{0,2,1:T(8,128)(2,1)}), bf16[512,2,64]{0,2,1:T(8,128)(2,1)}, u32[]{:S(2)}, u32[]{:S(2)}) async-start(bf16[512,2,64]{0,2,1:T(8,128)(2,1)} %pad_maximum_fusion.3), calls=%async_computation.5 | async-start | bytes 262144 | tf_op jit(solution)/shard_map/all_to_all | solution.py:286
  131.4 313.6 %all-gather.21.cloned.1.call-start = ((), (), s32[]{:S(2)}) async-start(), calls=%async_computation.22 | async-start | bytes 10272768 | tf_op jit(solution)/shard_map/all_gather | solution.py:470
  288.5 42.3 %all-to-all-start.4 = ((bf16[512,2,448]{0,2,1:T(8,128)(2,1)}), bf16[512,2,448]{0,2,1:T(8,128)(2,1)S(1)}, u32[]{:S(2)}, u32[]{:S(2)}) async-start(bf16[512,2,448]{0,2,1:T(8,128)(2,1)} %bitcast.24), calls=%async_computation.4 | async-start | bytes 1835008 | tf_op jit(solution)/shard_map/all_to_all | solution.py:285
  336.5 38.7 %all-to-all-start.3 = ((bf16[2,512,448]{1,2,0:T(8,128)(2,1)}), bf16[2,512,448]{1,2,0:T(8,128)(2,1)}, u32[]{:S(2)}, u32[]{:S(2)}) async-start(bf16[2,512,448]{1,2,0:T(8,128)(2,1)} %get-tuple-element.240), calls=%async_computation.3 | async-start | bytes 1835008 | tf_op jit(solution)/shard_map/all_to_all | solution.py:291
  1004.5 1333.9 %collective-permute-start.26 = (f32[4864,32]{0,1:T(8,128)}, f32[4864,32]{0,1:T(8,128)}, u32[]{:S(2)}, u32[]{:S(2)}) collective-permute-start(f32[4864,32]{0,1:T(8,128)} %fusion.14), channel_id=1, source_target_pairs={{0,3},{1,4},{2,5},{3,6},{4,7},{5,8},{6,9},{7,10},{8,11},{9,12},{10... | collective-permute-start | bytes 1867784
  1008.3 1345.0 %collective-permute-start.25 = (f32[4864,32]{0,1:T(8,128)}, f32[4864,32]{0,1:T(8,128)}, u32[]{:S(2)}, u32[]{:S(2)}) collective-permute-start(f32[4864,32]{0,1:T(8,128)} %fusion.14), channel_id=1, source_target_pairs={{0,2},{1,3},{2,4},{3,5},{4,6},{5,7},{6,8},{7,9},{8,10},{9,11},{10,... | collective-permute-start | bytes 1867784
  1014.1 1341.1 %collective-permute-start.24 = (f32[4864,32]{0,1:T(8,128)}, f32[4864,32]{0,1:T(8,128)}, u32[]{:S(2)}, u32[]{:S(2)}) collective-permute-start(f32[4864,32]{0,1:T(8,128)} %fusion.14), channel_id=1, source_target_pairs={{0,1},{1,2},{2,3},{3,4},{4,5},{5,6},{6,7},{7,8},{8,9},{9,10},{10,1... | collective-permute-start | bytes 1867784
  1046.9 51.9 %all-to-all-start.12 = ((bf16[512,2,448]{0,2,1:T(8,128)(2,1)}), bf16[512,2,448]{0,2,1:T(8,128)(2,1)}, u32[]{:S(2)}, u32[]{:S(2)}) async-start(bf16[512,2,448]{0,2,1:T(8,128)(2,1)} %bitcast.784), calls=%async_computation.12 | async-start | bytes 1835008 | tf_op jit(solution)/shard_map/all_to_all | solution.py:378
  1092.7 1243.2 %collective-permute-start.27 = (f32[4864,28]{0,1:T(8,128)}, f32[4864,28]{0,1:T(8,128)}, u32[]{:S(2)}, u32[]{:S(2)}) collective-permute-start(f32[4864,28]{0,1:T(8,128)} %slice.148), channel_id=1, source_target_pairs={{0,4},{1,5},{2,6},{3,7},{4,8},{5,9},{6,10},{7,11},{8,12},{9,13},{1... | collective-permute-start | bytes 1634312
  1199.6 87.2 %all-to-all-start.10 = ((bf16[2,512,64]{1,2,0:T(8,128)(2,1)}), bf16[2,512,64]{1,2,0:T(8,128)(2,1)}, u32[]{:S(2)}, u32[]{:S(2)}) async-start(bf16[2,512,64]{1,2,0:T(8,128)(2,1)} %copy.194), calls=%async_computation.10 | async-start | bytes 262144 | tf_op jit(solution)/shard_map/all_to_all | solution.py:384
  2338.5 61.0 %collective-permute-start.6 = (f32[32,128]{1,0:T(8,128)}, f32[32,128]{1,0:T(8,128)}, u32[]{:S(2)}, u32[]{:S(2)}) collective-permute-start(f32[32,128]{1,0:T(8,128)} %get-tuple-element.549), channel_id=1, source_target_pairs={{0,3},{1,4},{2,5},{3,6},{4,7},{5,8},{6,9},{7,10},{8,11},{9,12},{10... | collective-permute-start | bytes 49160
  2353.3 55.5 %collective-permute-start.5 = (f32[32,128]{1,0:T(8,128)}, f32[32,128]{1,0:T(8,128)}, u32[]{:S(2)}, u32[]{:S(2)}) collective-permute-start(f32[32,128]{1,0:T(8,128)} %get-tuple-element.549), channel_id=1, source_target_pairs={{0,2},{1,3},{2,4},{3,5},{4,6},{5,7},{6,8},{7,9},{8,10},{9,11},{10,... | collective-permute-start | bytes 49160
  2355.2 56.4 %collective-permute-start.4 = (f32[32,128]{1,0:T(8,128)}, f32[32,128]{1,0:T(8,128)}, u32[]{:S(2)}, u32[]{:S(2)}) collective-permute-start(f32[32,128]{1,0:T(8,128)} %get-tuple-element.549), channel_id=1, source_target_pairs={{0,1},{1,2},{2,3},{3,4},{4,5},{5,6},{6,7},{7,8},{8,9},{9,10},{10,1... | collective-permute-start | bytes 49160
  2358.2 57.3 %collective-permute-start.10 = (f32[32,128]{1,0:T(8,128)S(1)}, f32[32,128]{1,0:T(8,128)}, u32[]{:S(2)}, u32[]{:S(2)}) collective-permute-start(f32[32,128]{1,0:T(8,128)S(1)} %get-tuple-element.550), channel_id=1, source_target_pairs={{0,3},{1,4},{2,5},{3,6},{4,7},{5,8},{6,9},{7,10},{8,11},{9,12},{10... | collective-permute-start | bytes 49160
  2361.2 56.1 %collective-permute-start.9 = (f32[32,128]{1,0:T(8,128)S(1)}, f32[32,128]{1,0:T(8,128)}, u32[]{:S(2)}, u32[]{:S(2)}) collective-permute-start(f32[32,128]{1,0:T(8,128)S(1)} %get-tuple-element.550), channel_id=1, source_target_pairs={{0,2},{1,3},{2,4},{3,5},{4,6},{5,7},{6,8},{7,9},{8,10},{9,11},{10,... | collective-permute-start | bytes 49160
  2399.4 45.3 %collective-permute-start.2 = (f32[32,896]{1,0:T(8,128)}, f32[32,896]{1,0:T(8,128)}, u32[]{:S(2)}, u32[]{:S(2)}) collective-permute-start(f32[32,896]{1,0:T(8,128)} %get-tuple-element.548), channel_id=1, source_target_pairs={{0,3},{1,4},{2,5},{3,6},{4,7},{5,8},{6,9},{7,10},{8,11},{9,12},{10... | collective-permute-start | bytes 344072
  2408.8 38.9 %collective-permute-start.1 = (f32[32,896]{1,0:T(8,128)}, f32[32,896]{1,0:T(8,128)}, u32[]{:S(2)}, u32[]{:S(2)}) collective-permute-start(f32[32,896]{1,0:T(8,128)} %get-tuple-element.548), channel_id=1, source_target_pairs={{0,2},{1,3},{2,4},{3,5},{4,6},{5,7},{6,8},{7,9},{8,10},{9,11},{10,... | collective-permute-start | bytes 344072
  2411.6 38.2 %collective-permute-start = (f32[32,896]{1,0:T(8,128)}, f32[32,896]{1,0:T(8,128)}, u32[]{:S(2)}, u32[]{:S(2)}) collective-permute-start(f32[32,896]{1,0:T(8,128)} %get-tuple-element.548), channel_id=1, source_target_pairs={{0,1},{1,2},{2,3},{3,4},{4,5},{5,6},{6,7},{7,8},{8,9},{9,10},{10,1... | collective-permute-start | bytes 344072
  2432.7 32.6 %collective-permute-start.14 = (f32[896,32]{0,1:T(8,128)S(1)}, f32[896,32]{0,1:T(8,128)}, u32[]{:S(2)}, u32[]{:S(2)}) collective-permute-start(f32[896,32]{0,1:T(8,128)S(1)} %copy-done.76), channel_id=1, source_target_pairs={{0,3},{1,4},{2,5},{3,6},{4,7},{5,8},{6,9},{7,10},{8,11},{9,12},{10... | collective-permute-start | bytes 344072
  2444.8 29.4 %collective-permute-start.12 = (f32[896,32]{0,1:T(8,128)S(1)}, f32[896,32]{0,1:T(8,128)}, u32[]{:S(2)}, u32[]{:S(2)}) collective-permute-start(f32[896,32]{0,1:T(8,128)S(1)} %copy-done.76), channel_id=1, source_target_pairs={{0,1},{1,2},{2,3},{3,4},{4,5},{5,6},{6,7},{7,8},{8,9},{9,10},{10,1... | collective-permute-start | bytes 344072
  2447.7 48.9 %collective-permute-start.18 = (f32[32,4864]{1,0:T(8,128)S(1)}, f32[32,4864]{1,0:T(8,128)}, u32[]{:S(2)}, u32[]{:S(2)}) collective-permute-start(f32[32,4864]{1,0:T(8,128)S(1)} %get-tuple-element.552), channel_id=1, source_target_pairs={{0,3},{1,4},{2,5},{3,6},{4,7},{5,8},{6,9},{7,10},{8,11},{9,12},{10... | collective-permute-start | bytes 1867784
  2462.8 54.8 %collective-permute-start.17 = (f32[32,4864]{1,0:T(8,128)S(1)}, f32[32,4864]{1,0:T(8,128)}, u32[]{:S(2)}, u32[]{:S(2)}) collective-permute-start(f32[32,4864]{1,0:T(8,128)S(1)} %get-tuple-element.552), channel_id=1, source_target_pairs={{0,2},{1,3},{2,4},{3,5},{4,6},{5,7},{6,8},{7,9},{8,10},{9,11},{10,... | collective-permute-start | bytes 1867784
  2465.3 55.7 %collective-permute-start.16 = (f32[32,4864]{1,0:T(8,128)S(1)}, f32[32,4864]{1,0:T(8,128)}, u32[]{:S(2)}, u32[]{:S(2)}) collective-permute-start(f32[32,4864]{1,0:T(8,128)S(1)} %get-tuple-element.552), channel_id=1, source_target_pairs={{0,1},{1,2},{2,3},{3,4},{4,5},{5,6},{6,7},{7,8},{8,9},{9,10},{10,1... | collective-permute-start | bytes 1867784
  2470.3 72.1 %collective-permute-start.22 = (f32[32,4864]{1,0:T(8,128)S(1)}, f32[32,4864]{1,0:T(8,128)}, u32[]{:S(2)}, u32[]{:S(2)}) collective-permute-start(f32[32,4864]{1,0:T(8,128)S(1)} %get-tuple-element.553), channel_id=1, source_target_pairs={{0,3},{1,4},{2,5},{3,6},{4,7},{5,8},{6,9},{7,10},{8,11},{9,12},{10... | collective-permute-start | bytes 1867784
  2490.9 51.5 %collective-permute-start.21 = (f32[32,4864]{1,0:T(8,128)S(1)}, f32[32,4864]{1,0:T(8,128)}, u32[]{:S(2)}, u32[]{:S(2)}) collective-permute-start(f32[32,4864]{1,0:T(8,128)S(1)} %get-tuple-element.553), channel_id=1, source_target_pairs={{0,2},{1,3},{2,4},{3,5},{4,6},{5,7},{6,8},{7,9},{8,10},{9,11},{10,... | collective-permute-start | bytes 1867784
  2496.6 45.8 %collective-permute-start.20 = (f32[32,4864]{1,0:T(8,128)S(1)}, f32[32,4864]{1,0:T(8,128)}, u32[]{:S(2)}, u32[]{:S(2)}) collective-permute-start(f32[32,4864]{1,0:T(8,128)S(1)} %get-tuple-element.553), channel_id=1, source_target_pairs={{0,1},{1,2},{2,3},{3,4},{4,5},{5,6},{6,7},{7,8},{8,9},{9,10},{10,1... | collective-permute-start | bytes 1867784
  2578.8 34.5 %all-to-all-start.16 = ((bf16[160,28,128]{2,1,0:T(8,128)(2,1)}), bf16[160,28,128]{2,1,0:T(8,128)(2,1)S(1)}, u32[]{:S(2)}, u32[]{:S(2)}) async-start(bf16[160,28,128]{2,1,0:T(8,128)(2,1)} %get-tuple-element.621), calls=%async_computation.16 | async-start | bytes 2621440 | tf_op jit(solution)/shard_map/all_to_all | solution.py:527
  2613.3 63.5 %all-to-all-start.17 = ((bf16[160,28,128]{2,1,0:T(8,128)(2,1)}), bf16[160,28,128]{2,1,0:T(8,128)(2,1)}, u32[]{:S(2)}, u32[]{:S(2)}) async-start(bf16[160,28,128]{2,1,0:T(8,128)(2,1)} %get-tuple-element.620), calls=%async_computation.17 | async-start | bytes 2621440 | tf_op jit(solution)/shard_map/all_to_all | solution.py:530
  (185 other events, 7316.1 us)
Sparse Core Ops, SparseCore 0:
  11.0 58.7 all-gather.12
  72.7 54.8 all-gather.14
  131.0 83.7 all-gather.16
  218.0 90.2 all-gather.18
  311.0 92.2 all-gather.20
where the time goes:
time: 2720 us; the launch traced here: 2710 us
  blocking collectives  1630 us (60%)
  matrix products  423 us (16%)
  local copies, waits for them, and re-layouts  250 us (9%)
  starting transfers between devices  194 us (7%)
  other arithmetic  113 us (4%)
  waiting for transfers between devices  68 us (2%)
    unnamed x4, blocking collectives  1490 us
    unnamed x320, local copies, waits for them, and re-layouts  172 us
    unnamed x28, starting transfers between devices  125 us
    dot_general x14, matrix products, contract_cols(): lax.dot_general(former, latter, (((1,), (1,)), ((), ())), preferred_eleme...  97.4 us
    dot_general x14, matrix products, contract_rows(): lax.dot_general(former, latter, (((0,), (0,)), ((), ())), preferred_eleme...  97 us
    all_gather x1, blocking collectives, on_device(): lax.all_gather(key_low, ('dp', 'seq'), axis=0, tiled=True)  71.2 us
    all_gather x1, blocking collectives, on_device(): lax.all_gather(value_reduced, ('dp', 'seq'), axis=0, tiled=True)  69.2 us
  transfers between devices with their start and end apart: 51, of which 13 were waited for; matrix products, arithmetic and copies ran while one was open for 57% of the time, Pallas kernels for 0%

commit v1 on v0

v1 whole, which is shorter than its diff:
```python
import functools
import math

import jax
import jax.numpy as jnp
import numpy as np
from jax import lax
from jax.experimental import pallas as pl
from jax.experimental.pallas import tpu as pltpu
from jax.sharding import PartitionSpec as P

D = 896
QUERY_HEADS = 14
KEY_VALUE_HEADS = 2
HEAD_SIZE = 64
BW = 128
MICRO = 2
STEP = 10
QW = 896
KW = 128
QKV = QW + 2 * KW
FF = 4864

norm_epsilon = 1e-06
rope_theta = 1000000.0
beta_first = 0.9
beta_second = 0.999
adam_epsilon = 1e-08
weight_decay = 0.01
rate_matrix = 0.1
rate_vector = 0.5
masked_value = -1e30

F32 = jnp.float32
BF16 = jnp.bfloat16
BOTH = ("dp", "seq")

TILE = 256
CHUNKS = (1280, 1280, 1280, 1024)
OFFSETS = (0, 1280, 2560, 3840)
QUARTER = 112
HALF = 448
TOKEN_TILE = 256

HEAD_SETS = (
    ((0, 1, 2, 3), 0, 0),
    ((0, 1, 2), 1, 0),
    ((3, 4, 5, 6), 1, 1),
    ((4, 5, 6), 0, 1),
)
SET_ROWS = (0, 512, 896, 1408)
ALL_ROWS = 1792


def params(mib, **more):
    return pltpu.CompilerParams(vmem_limit_bytes=mib * 1024 * 1024, **more)


def dot_nn(a, b):
    return lax.dot_general(a, b, (((1,), (0,)), ((), ())), preferred_element_type=F32)


def dot_nt(a, b):
    return lax.dot_general(a, b, (((1,), (1,)), ((), ())), preferred_element_type=F32)


def dot_tn(a, b):
    return lax.dot_general(a, b, (((0,), (0,)), ((), ())), preferred_element_type=F32)


class Places:
    def __init__(self, n_dp, n_seq):
        self.line = n_dp // 4
        self.rows = D // (n_dp * n_seq)
        self.n_dev = n_dp * n_seq

        def pairs(move):
            found = []
            for z in range(self.line):
                for x in range(2):
                    for c in range(2):
                        for y in range(2):
                            tz, tx, tc, ty = move(z, x, c, y)
                            found.append(
                                (((z * 2 + x) * 2 + c) * 2 + y, ((tz * 2 + tx) * 2 + tc) * 2 + ty)
                            )
            return found

        self.sibling = pairs(lambda z, x, c, y: (z, x, 1 - c, y))
        self.long = pairs(lambda z, x, c, y: (z, 1 - x, c, y) if c == 0 else (z, x, c, 1 - y))
        self.short = pairs(lambda z, x, c, y: (z, 1 - x, c, y) if c == 1 else (z, x, c, 1 - y))
        self.ahead = [
            pairs(lambda z, x, c, y, k=k: ((z + k) % self.line, x, c, y)) for k in range(self.line)
        ]

    def natural_rows(self):
        dp = lax.axis_index("dp")
        y = lax.axis_index("seq")
        z, x, c = dp // 4, (dp // 2) % 2, dp % 2
        place = jnp.arange(D, dtype=jnp.int32)
        dc, da, db = place // HALF, (place // (2 * QUARTER)) % 2, (place // QUARTER) % 2
        dz, inner = (place % QUARTER) // self.rows, place % self.rows
        c_own = c ^ dc
        x_own = x ^ jnp.where(c_own == 0, da, db)
        y_own = y ^ jnp.where(c_own == 0, db, da)
        z_own = (z + dz) % self.line
        return self.rows * (((z_own * 2 + x_own) * 2 + c_own) * 2 + y_own) + inner


def send(array, pairs):
    return lax.ppermute(array, BOTH, pairs)


def gather_pieces(places, shard):
    line = [shard] + [send(shard, places.ahead[-k % places.line]) for k in range(1, places.line)]
    own = jnp.concatenate(line, axis=0)
    short = send(own, places.short)
    quarters = [own, short, send(own, places.long), send(short, places.long)]
    return quarters + [send(piece, places.sibling) for piece in quarters]


def reduce_rows(places, own, other):
    first = send(other, places.sibling)
    f, q, h = F32, QUARTER, places.rows
    second = send(
        (own[2 * q :].astype(f) + first[2 * q :].astype(f)).astype(BF16), places.long
    )
    third = send(
        (own[q : 2 * q].astype(f) + first[q : 2 * q].astype(f) + second[q:].astype(f)).astype(BF16),
        places.short,
    )
    total = own[:q].astype(f) + first[:q].astype(f) + second[:q].astype(f) + third.astype(f)
    arrived = [
        send(total[k * h : (k + 1) * h].astype(BF16), places.ahead[k])
        for k in range(1, places.line)
    ]
    result = total[:h]
    for part in arrived:
        result = result + part.astype(f)
    return result


def swap_halves(tile, low_half):
    return jnp.where(low_half, pltpu.roll(tile, 96, 1), pltpu.roll(tile, 32, 1))


def project_kernel(x_ref, pi_ref, *refs):
    pieces, (gain_ref, bias_ref, cos_ref, sin_ref, xp_ref, nl_ref, q_ref, k_ref, v_ref, w_scr) = (
        refs[:8],
        refs[8:],
    )

    @pl.when(pl.program_id(0) == 0)
    def _():
        for k in range(8):
            w_scr[QUARTER * k : QUARTER * (k + 1), :] = pieces[k][:, :QKV]

    xp = dot_nn(x_ref[...], pi_ref[...])
    inv = lax.rsqrt(jnp.sum(xp * xp, axis=1, keepdims=True) * (1.0 / D) + norm_epsilon)
    nl = (xp * inv * gain_ref[...]).astype(BF16)
    xp_ref[...] = xp.astype(BF16)
    nl_ref[...] = nl
    lin = dot_nn(nl, w_scr[...]) + bias_ref[...]
    cos, sin = cos_ref[...], sin_ref[...]
    low = lax.broadcasted_iota(jnp.int32, cos.shape, 1) % HEAD_SIZE < HEAD_SIZE // 2
    for t in range(8):
        piece = lin[:, 128 * t : 128 * (t + 1)]
        turned = (piece * cos + swap_halves(piece, low) * sin).astype(BF16)
        if t < 7:
            q_ref[:, 128 * t : 128 * (t + 1)] = (turned.astype(F32) * 0.125).astype(BF16)
        else:
            k_ref[...] = turned
    v_ref[...] = lin[:, QW + KW :].astype(BF16)


def project(x, pi, pieces, gain, bias, cos, sin):
    rows = x.shape[0]
    width = pieces[0].shape[1]

    def tile(cols):
        return pl.BlockSpec((TOKEN_TILE, cols), lambda t: (t, 0))

    def whole(r, c):
        return pl.BlockSpec((r, c), lambda t: (0, 0))

    shapes = [(D, BF16), (D, BF16), (QW, BF16), (KW, BF16), (KW, BF16)]
    return pl.pallas_call(
        project_kernel,
        grid=(rows // TOKEN_TILE,),
        in_specs=[tile(D), whole(D, D)]
        + [whole(QUARTER, width)] * 8
        + [whole(1, D), whole(1, QKV), tile(128), tile(128)],
        out_specs=[tile(c) for c, _ in shapes],
        out_shape=[jax.ShapeDtypeStruct((rows, c), t) for c, t in shapes],
        scratch_shapes=[pltpu.VMEM((D, QKV), BF16)],
        compiler_params=params(40),
        cost_estimate=pl.CostEstimate(
            flops=2 * rows * D * (D + QKV), bytes_accessed=14 << 20, transcendentals=0
        ),
        name="project",
    )(x, pi, *pieces, gain, bias, cos, sin)


def padded_heads(recv, own, out):
    lane = lax.broadcasted_iota(jnp.int32, (512, 128), 1)
    for part, ref in enumerate((recv, own)):
        natural = ref[0].astype(F32)
        crossed = pltpu.roll(natural, 64, 1)
        rows = pl.ds(512 * part, 512)
        for s, (_, half, head) in enumerate(HEAD_SETS):
            source = natural if half == head else crossed
            keep = (lane >= 64) if half else (lane < 64)
            out[s, rows, :] = jnp.where(keep, source, 0.0).astype(BF16)


def block_bias(kb, i, begin):
    shape = (128, 128)
    key = kb * 128 + lax.broadcasted_iota(jnp.int32, shape, 1)
    query = 512 + i * 128 + lax.broadcasted_iota(jnp.int32, shape, 0)
    return jnp.where((key >= begin) & (key <= query), 0.0, masked_value)


def stacked(tile_of, pairs):
    return jnp.concatenate([tile_of(p) for p in pairs], axis=0)


def attend_kernel(
    lo_ref, q_ref, kr_ref, ko_ref, vr_ref, vo_ref, ds_ref, o_ref, lse_ref, kp, vp, s_scr, m_scr, l_scr, acc
):
    b, i = pl.program_id(0), pl.program_id(1)

    @pl.when(i == 0)
    def _():
        padded_heads(kr_ref, ko_ref, kp)
        padded_heads(vr_ref, vo_ref, vp)

    lo, hi = lo_ref[b, i], i + 5
    begin = ds_ref[0]
    m_scr[...] = jnp.full(m_scr.shape, masked_value, F32)
    l_scr[...] = jnp.zeros(l_scr.shape, F32)
    acc[...] = jnp.zeros(acc.shape, F32)

    def scores(kb, carry):
        bias = block_bias(kb, i, begin)
        keys = pl.ds(pl.multiple_of(kb * 128, 128), 128)
        for s, (pairs, _, _) in enumerate(HEAD_SETS):
            x = stacked(lambda p: q_ref[0, :, 128 * p : 128 * (p + 1)], pairs)
            raw = dot_nt(x, kp[s, keys, :])
            for n in range(len(pairs)):
                rows = slice(SET_ROWS[s] + 128 * n, SET_ROWS[s] + 128 * (n + 1))
                value = raw[128 * n : 128 * (n + 1)] + bias
                s_scr[kb, rows, :] = value
                m_scr[rows, :] = jnp.maximum(m_scr[rows, :], value)
        return carry

    lax.fori_loop(lo, hi, scores, 0)
    top = jnp.max(m_scr[...], axis=1, keepdims=True)
    m_scr[...] = jnp.broadcast_to(top, m_scr.shape)

    def weigh(kb, carry):
        keys = pl.ds(pl.multiple_of(kb * 128, 128), 128)
        for s, (pairs, _, _) in enumerate(HEAD_SETS):
            rows = slice(SET_ROWS[s], SET_ROWS[s] + 128 * len(pairs))
            p = jnp.exp(s_scr[kb, rows, :] - m_scr[rows, :])
            l_scr[rows, :] += p
            acc[rows, :] += dot_nn(p.astype(BF16), vp[s, keys, :])
        return carry

    lax.fori_loop(lo, hi, weigh, 0)
    total = jnp.sum(l_scr[...], axis=1, keepdims=True)
    lse = m_scr[:, :1] + jnp.log(total)
    share = 1.0 / total
    lane = lax.broadcasted_iota(jnp.int32, (128, 128), 1)
    lanes = jnp.zeros((128, 128), F32)
    outs = [None] * 7
    for s, (pairs, half, _) in enumerate(HEAD_SETS):
        for n, p in enumerate(pairs):
            rows = slice(SET_ROWS[s] + 128 * n, SET_ROWS[s] + 128 * (n + 1))
            part = acc[rows, :] * share[rows]
            outs[p] = part if outs[p] is None else outs[p] + part
            lanes = jnp.where(lane == 2 * p + half, lse[rows], lanes)
    for p in range(7):
        o_ref[0, :, 128 * p : 128 * (p + 1)] = outs[p].astype(BF16)
    lse_ref[0] = lanes


def attend_specs():
    def block(cols):
        return pl.BlockSpec((1, 128, cols), lambda b, i, lo: (b, i, 0))

    def stream(cols):
        return pl.BlockSpec((1, 512, cols), lambda b, i, lo: (b, 0, 0))

    return block, stream


def attend(lo, q, k_recv, k_own, v_recv, v_own, begin):
    block, stream = attend_specs()
    return pl.pallas_call(
        attend_kernel,
        grid_spec=pltpu.PrefetchScalarGridSpec(
            num_scalar_prefetch=1,
            grid=(MICRO, 4),
            in_specs=[block(QW)] + [stream(KW)] * 4 + [block(1)],
            out_specs=[block(QW), block(128)],
            scratch_shapes=[
                pltpu.VMEM((4, 1024, 128), BF16),
                pltpu.VMEM((4, 1024, 128), BF16),
                pltpu.VMEM((8, ALL_ROWS, 128), F32),
                pltpu.VMEM((ALL_ROWS, 128), F32),
                pltpu.VMEM((ALL_ROWS, 128), F32),
                pltpu.VMEM((ALL_ROWS, 128), F32),
            ],
        ),
        out_shape=[
            jax.ShapeDtypeStruct((MICRO, 512, QW), BF16),
            jax.ShapeDtypeStruct((MICRO, 512, 128), F32),
        ],
        compiler_params=params(40),
        cost_estimate=pl.CostEstimate(
            flops=20 * 10**9, bytes_accessed=6 << 20, transcendentals=4 * 10**6
        ),
        name="attend",
    )(lo, q, k_recv, k_own, v_recv, v_own, begin)


def attend_back_kernel(
    lo_ref, q_ref, kr_ref, ko_ref, vr_ref, vo_ref, ds_ref, o_ref, do_ref, lse_ref,
    dq_ref, own_ref, recv_ref, kp, vp, dk, dv, dq_acc,
):
    b, i = pl.program_id(0), pl.program_id(1)

    @pl.when(i == 0)
    def _():
        padded_heads(kr_ref, ko_ref, kp)
        padded_heads(vr_ref, vo_ref, vp)
        dk[...] = jnp.zeros(dk.shape, F32)
        dv[...] = jnp.zeros(dv.shape, F32)

    lo, hi = lo_ref[b, i], i + 5
    begin = ds_ref[0]
    lane = lax.broadcasted_iota(jnp.int32, (128, 128), 1)
    dq_acc[...] = jnp.zeros(dq_acc.shape, F32)
    lse_all = lse_ref[0]
    lse, dots = [], []
    for s, (pairs, half, _) in enumerate(HEAD_SETS):
        for p in pairs:
            cols = slice(128 * p, 128 * (p + 1))
            product = o_ref[0, :, cols].astype(F32) * do_ref[0, :, cols].astype(F32)
            keep = (lane >= 64) if half else (lane < 64)
            dots.append(jnp.sum(jnp.where(keep, product, 0.0), axis=1, keepdims=True))
            head = 2 * p + half
            lse.append(lse_all[:, head : head + 1])

    def one_block(kb, carry):
        bias = block_bias(kb, i, begin)
        keys = pl.ds(pl.multiple_of(kb * 128, 128), 128)
        at = 0
        for s, (pairs, _, _) in enumerate(HEAD_SETS):
            x = stacked(lambda p: q_ref[0, :, 128 * p : 128 * (p + 1)], pairs)
            y = stacked(lambda p: do_ref[0, :, 128 * p : 128 * (p + 1)], pairs)
            raw = dot_nt(x, kp[s, keys, :])
            d_prob = dot_nt(y, vp[s, keys, :])
            probs, d_scores = [], []
            for n in range(len(pairs)):
                rows = slice(128 * n, 128 * (n + 1))
                p = jnp.exp(raw[rows] + bias - lse[at + n])
                probs.append(p.astype(BF16))
                d_scores.append((p * (d_prob[rows] - dots[at + n])).astype(BF16))
            at += len(pairs)
            prob = jnp.concatenate(probs, axis=0)
            d_score = jnp.concatenate(d_scores, axis=0)
            d_query = dot_nn(d_score, kp[s, keys, :])
            for n, p in enumerate(pairs):
                dq_acc[p] += d_query[128 * n : 128 * (n + 1)]
            dk[s, keys, :] += dot_tn(d_score, x)
            dv[s, keys, :] += dot_tn(prob, y)
        return carry

    lax.fori_loop(lo, hi, one_block, 0)
    for p in range(7):
        dq_ref[0, :, 128 * p : 128 * (p + 1)] = (dq_acc[p] * 0.125).astype(BF16)

    @pl.when(i == 3)
    def _():
        wide = lax.broadcasted_iota(jnp.int32, (512, 128), 1) < 64
        for part, ref in enumerate((recv_ref, own_ref)):
            rows = pl.ds(512 * part, 512)
            for n, grads in enumerate((dk, dv)):
                low = grads[0, rows, :] + pltpu.roll(grads[1, rows, :], 64, 1)
                high = grads[2, rows, :] + pltpu.roll(grads[3, rows, :], 64, 1)
                value = jnp.where(wide, low, high)
                ref[0, :, 128 * n : 128 * (n + 1)] = value.astype(ref.dtype)


def attend_back(lo, q, k_recv, k_own, v_recv, v_own, begin, out, d_out, lse):
    block, stream = attend_specs()
    return pl.pallas_call(
        attend_back_kernel,
        grid_spec=pltpu.PrefetchScalarGridSpec(
            num_scalar_prefetch=1,
            grid=(MICRO, 4),
            in_specs=[block(QW)]
            + [stream(KW)] * 4
            + [block(1), block(QW), block(QW), block(128)],
            out_specs=[block(QW), stream(256), stream(256)],
            scratch_shapes=[
                pltpu.VMEM((4, 1024, 128), BF16),
                pltpu.VMEM((4, 1024, 128), BF16),
                pltpu.VMEM((4, 1024, 128), F32),
                pltpu.VMEM((4, 1024, 128), F32),
                pltpu.VMEM((7, 128, 128), F32),
            ],
        ),
        out_shape=[
            jax.ShapeDtypeStruct((MICRO, 512, QW), BF16),
            jax.ShapeDtypeStruct((MICRO, 512, 256), F32),
            jax.ShapeDtypeStruct((MICRO, 512, 256), BF16),
        ],
        compiler_params=params(40),
        cost_estimate=pl.CostEstimate(
            flops=50 * 10**9, bytes_accessed=10 << 20, transcendentals=4 * 10**6
        ),
        name="attend_back",
    )(lo, q, k_recv, k_own, v_recv, v_own, begin, out, d_out, lse)


def middle_kernel(att_ref, xp_ref, *refs):
    pieces, (gain_ref, res_ref, n_ref, nt_ref, w_scr) = (refs[:8], refs[8:])

    @pl.when(pl.program_id(0) == 0)
    def _():
        for k in range(8):
            w_scr[QUARTER * k : QUARTER * (k + 1), :] = pieces[k][:, QKV : QKV + QW]

    residual = xp_ref[...].astype(F32) + dot_nt(att_ref[...], w_scr[...])
    inv = lax.rsqrt(jnp.sum(residual * residual, axis=1, keepdims=True) * (1.0 / D) + norm_epsilon)
    normed = residual * inv * gain_ref[...]
    res_ref[...] = residual
    n_ref[...] = normed.astype(BF16)
    nt_ref[...] = normed.T.astype(BF16)


def middle(attended, xp, pieces, gain):
    rows = xp.shape[0]
    width = pieces[0].shape[1]

    def tile(cols):
        return pl.BlockSpec((TOKEN_TILE, cols), lambda t: (t, 0))

    def whole(r, c):
        return pl.BlockSpec((r, c), lambda t: (0, 0))

    return pl.pallas_call(
        middle_kernel,
        grid=(rows // TOKEN_TILE,),
        in_specs=[tile(QW), tile(D)] + [whole(QUARTER, width)] * 8 + [whole(1, D)],
        out_specs=[tile(D), tile(D), pl.BlockSpec((D, TOKEN_TILE), lambda t: (0, t))],
        out_shape=[
            jax.ShapeDtypeStruct((rows, D), F32),
            jax.ShapeDtypeStruct((rows, D), BF16),
            jax.ShapeDtypeStruct((D, rows), BF16),
        ],
        scratch_shapes=[pltpu.VMEM((D, QW), BF16)],
        compiler_params=params(40),
        cost_estimate=pl.CostEstimate(
            flops=2 * rows * D * QW, bytes_accessed=14 << 20, transcendentals=0
        ),
        name="middle",
    )(attended, xp, *pieces, gain)


def middle_back_kernel(res_ref, mlp_ref, dn_ref, cot_ref, att_ref, pi_ref, *refs):
    pieces, (gain_ref, out_ref, dres_ref, datt_ref, own_ref, sib_ref, dgain_ref, w_scr, g_scr) = (
        refs[:8],
        refs[8:],
    )
    t = pl.program_id(0)

    @pl.when(t == 0)
    def _():
        for k in range(8):
            w_scr[QUARTER * k : QUARTER * (k + 1), :] = pieces[k][:, QKV : QKV + QW]
        g_scr[...] = jnp.zeros(g_scr.shape, F32)
        dgain_ref[...] = jnp.zeros(dgain_ref.shape, F32)

    residual = res_ref[...]
    inv = lax.rsqrt(jnp.sum(residual * residual, axis=1, keepdims=True) * (1.0 / D) + norm_epsilon)
    out_low = (residual + mlp_ref[...]).astype(BF16)
    out_ref[...] = dot_nt(out_low, pi_ref[...]).astype(BF16)
    d_normed = dn_ref[...]
    hat = residual * inv
    scaled = d_normed * gain_ref[...]
    dgain_ref[...] += jnp.sum(d_normed * hat, axis=0, keepdims=True)
    mean = jnp.sum(scaled * hat, axis=1, keepdims=True) * (1.0 / D)
    d_res = cot_ref[...].astype(F32) + inv * (scaled - hat * mean)
    dres_ref[...] = d_res
    low = d_res.astype(BF16)
    datt_ref[...] = dot_nn(low, w_scr[...]).astype(BF16)
    g_scr[...] += dot_tn(low, att_ref[...])

    @pl.when(t == pl.num_programs(0) - 1)
    def _():
        own_ref[...] = g_scr[:HALF].astype(BF16)
        sib_ref[...] = g_scr[HALF:].astype(BF16)


def middle_back(residual, mlp, d_normed, cot, attended, pi, pieces, gain):
    rows = residual.shape[0]
    width = pieces[0].shape[1]

    def tile(cols):
        return pl.BlockSpec((TOKEN_TILE, cols), lambda t: (t, 0))

    def whole(r, c):
        return pl.BlockSpec((r, c), lambda t: (0, 0))

    return pl.pallas_call(
        middle_back_kernel,
        grid=(rows // TOKEN_TILE,),
        in_specs=[tile(D)] * 4
        + [tile(QW), whole(D, D)]
        + [whole(QUARTER, width)] * 8
        + [whole(1, D)],
        out_specs=[tile(D), tile(D), tile(QW), whole(HALF, QW), whole(HALF, QW), whole(1, D)],
        out_shape=[
            jax.ShapeDtypeStruct((rows, D), BF16),
            jax.ShapeDtypeStruct((rows, D), F32),
            jax.ShapeDtypeStruct((rows, QW), BF16),
            jax.ShapeDtypeStruct((HALF, QW), BF16),
            jax.ShapeDtypeStruct((HALF, QW), BF16),
            jax.ShapeDtypeStruct((1, D), F32),
        ],
        scratch_shapes=[pltpu.VMEM((D, QW), BF16), pltpu.VMEM((D, QW), F32)],
        compiler_params=params(48),
        cost_estimate=pl.CostEstimate(
            flops=6 * rows * D * QW, bytes_accessed=26 << 20, transcendentals=0
        ),
        name="middle_back",
    )(residual, mlp, d_normed, cot, attended, pi, *pieces, gain)


def feed_kernel(wide, started, *refs):
    n_in = 4 + (2 if started else 0)
    n_hbm, nt_hbm, cot_hbm, cott_hbm = refs[:4]
    sums_in = refs[4:n_in]
    pieces = refs[n_in : n_in + 8]
    mlp_hbm, dn_hbm, own_hbm, sib_hbm = refs[n_in + 8 : n_in + 12]
    (n_v, nt_v, cot_v, cott_v, w_v, mlp_v, dn_v, act_v, grad_v, in_sem, w_sem, out_sem, g_sem) = refs[
        n_in + 12 :
    ]
    rows_all = n_v.shape[0]
    steps = wide // TILE

    loads = [
        pltpu.make_async_copy(src, dst, in_sem.at[k])
        for k, (src, dst) in enumerate(
            [(n_hbm, n_v), (cot_hbm, cot_v), (nt_hbm, nt_v), (cott_hbm, cott_v)]
            + ([(sums_in[0], mlp_v), (sums_in[1], dn_v)] if started else [])
        )
    ]
    weights = [
        [
            pltpu.make_async_copy(
                pieces[k].at[:, m * wide : (m + 1) * wide],
                w_v.at[m, QUARTER * k : QUARTER * (k + 1), :],
                w_sem.at[m, k],
            )
            for k in range(8)
        ]
        for m in range(3)
    ]
    loads[0].start()
    for m in range(3):
        for copy in weights[m]:
            copy.start()
        if m == 1:
            loads[1].start()
    for copy in loads[2:]:
        copy.start()
    loads[0].wait()
    loads[1].wait()
    for m in range(3):
        for copy in weights[m]:
            copy.wait()

    span = 512
    stores = []
    for part in range(rows_all // span):
        rows = pl.ds(part * span, span)

        def activate(j, carry):
            cols = pl.ds(pl.multiple_of(j * TILE, TILE), TILE)
            normed = n_v[rows, :]
            gate = dot_nn(normed, w_v[0, :, cols])
            up = dot_nn(normed, w_v[1, :, cols])
            d_hidden = dot_nn(cot_v[rows, :], w_v[2, :, cols])
            s = 1.0 / (1.0 + jnp.exp(-gate))
            silu = gate * s
            act_v[2, rows, cols] = (silu * up).astype(BF16)
            act_v[0, rows, cols] = (d_hidden * up * s * (1.0 + gate * (1.0 - s))).astype(BF16)
            act_v[1, rows, cols] = (d_hidden * silu).astype(BF16)
            return carry

        lax.fori_loop(0, steps, activate, 0)
        if part == 0:
            for copy in loads[4:]:
                copy.wait()
        mlp = dot_nt(act_v[2, rows, :], w_v[2])
        dn = dot_nt(act_v[0, rows, :], w_v[0]) + dot_nt(act_v[1, rows, :], w_v[1])
        if started:
            mlp = mlp + mlp_v[rows, :]
            dn = dn + dn_v[rows, :]
        mlp_v[rows, :] = mlp
        dn_v[rows, :] = dn
        for k, (src, dst) in enumerate(((mlp_v, mlp_hbm), (dn_v, dn_hbm))):
            copy = pltpu.make_async_copy(src.at[rows, :], dst.at[rows, :], out_sem.at[part, k])
            copy.start()
            stores.append(copy)

    loads[2].wait()
    loads[3].wait()

    def parts_of(m, j):
        cols = pl.ds(pl.multiple_of(j * TILE, TILE), TILE)
        target = pl.ds(pl.multiple_of(m * wide + j * TILE, TILE), TILE)
        return [
            pltpu.make_async_copy(
                grad_v.at[m, pl.ds(HALF * h, HALF), cols], dst.at[:, target], g_sem.at[m, j, h]
            )
            for h, dst in enumerate((own_hbm, sib_hbm))
        ]

    def gradients(j, carry):
        cols = pl.ds(pl.multiple_of(j * TILE, TILE), TILE)
        for m, left in enumerate((nt_v, nt_v, cott_v)):
            grad_v[m, :, cols] = dot_nn(left[...], act_v[m, :, cols]).astype(BF16)
            for copy in parts_of(m, j):
                copy.start()
        return carry

    lax.fori_loop(0, steps, gradients, 0)

    def settle(j, carry):
        for m in range(3):
            for copy in parts_of(m, j):
                copy.wait()
        return carry

    lax.fori_loop(0, steps, settle, 0)
    for copy in stores:
        copy.wait()


def feed(wide, normed, normed_t, cot, cot_t, sums, pieces):
    rows = normed.shape[0]
    started = sums is not None
    any_spec = pl.BlockSpec(memory_space=pl.ANY)
    extra = list(sums) if started else []
    n_in = 12 + len(extra)
    return pl.pallas_call(
        functools.partial(feed_kernel, wide, started),
        in_specs=[any_spec] * n_in,
        out_specs=[any_spec] * 4,
        out_shape=[
            jax.ShapeDtypeStruct((rows, D), F32),
            jax.ShapeDtypeStruct((rows, D), F32),
            jax.ShapeDtypeStruct((HALF, 3 * wide), BF16),
            jax.ShapeDtypeStruct((HALF, 3 * wide), BF16),
        ],
        scratch_shapes=[
            pltpu.VMEM((rows, D), BF16),
            pltpu.VMEM((D, rows), BF16),
            pltpu.VMEM((rows, D), BF16),
            pltpu.VMEM((D, rows), BF16),
            pltpu.VMEM((3, D, wide), BF16),
            pltpu.VMEM((rows, D), F32),
            pltpu.VMEM((rows, D), F32),
            pltpu.VMEM((3, rows, wide), BF16),
            pltpu.VMEM((3, D, wide), BF16),
            pltpu.SemaphoreType.DMA((6,)),
            pltpu.SemaphoreType.DMA((3, 8)),
            pltpu.SemaphoreType.DMA((2, 2)),
            pltpu.SemaphoreType.DMA((3, wide // TILE, 2)),
        ],
        compiler_params=params(56),
        cost_estimate=pl.CostEstimate(
            flops=18 * rows * D * wide,
            bytes_accessed=(7 + 7 + 7 + 7 + 14) << 20,
            transcendentals=rows * wide,
        ),
        name="feed",
    )(normed, normed_t, cot, cot_t, *extra, *pieces)


def project_back_kernel(dq_ref, dk_ref, dv_ref, cos_ref, sin_ref, nl_ref, xp_ref, dres_ref, pi_ref, *refs):
    pieces, (gain_ref, ig_ref, own_ref, sib_ref, dgain_ref, dbias_ref, w_scr, g_scr) = (
        refs[:8],
        refs[8:],
    )
    t = pl.program_id(0)

    @pl.when(t == 0)
    def _():
        for k in range(8):
            w_scr[QUARTER * k : QUARTER * (k + 1), :] = pieces[k][:, :QKV]
        g_scr[...] = jnp.zeros(g_scr.shape, F32)
        dgain_ref[...] = jnp.zeros(dgain_ref.shape, F32)
        dbias_ref[...] = jnp.zeros(dbias_ref.shape, F32)

    cos, sin = cos_ref[...], sin_ref[...]
    low = lax.broadcasted_iota(jnp.int32, cos.shape, 1) % HEAD_SIZE < HEAD_SIZE // 2
    parts = []
    for n in range(8):
        piece = (dq_ref[:, 128 * n : 128 * (n + 1)] if n < 7 else dk_ref[...]).astype(F32)
        parts.append((piece * cos - swap_halves(piece, low) * sin).astype(BF16))
    parts.append(dv_ref[...])
    d_lin = jnp.concatenate(parts, axis=1)
    dbias_ref[...] += jnp.sum(d_lin.astype(F32), axis=0, keepdims=True)
    d_normed = dot_nt(d_lin, w_scr[...])
    xp = xp_ref[...].astype(F32)
    inv = lax.rsqrt(jnp.sum(xp * xp, axis=1, keepdims=True) * (1.0 / D) + norm_epsilon)
    hat = xp * inv
    scaled = d_normed * gain_ref[...]
    dgain_ref[...] += jnp.sum(d_normed * hat, axis=0, keepdims=True)
    mean = jnp.sum(scaled * hat, axis=1, keepdims=True) * (1.0 / D)
    grad = dres_ref[...] + inv * (scaled - hat * mean)
    high = grad.astype(BF16)
    rest = (grad - high.astype(F32)).astype(BF16)
    ig_ref[...] = dot_nt(high, pi_ref[...]) + dot_nt(rest, pi_ref[...])
    g_scr[...] += dot_tn(nl_ref[...], d_lin)

    @pl.when(t == pl.num_programs(0) - 1)
    def _():
        own_ref[...] = g_scr[:HALF].astype(BF16)
        sib_ref[...] = g_scr[HALF:].astype(BF16)


def project_back(dq, dk, dv, cos, sin, nl, xp, d_res, pi, pieces, gain):
    rows = xp.shape[0]
    width = pieces[0].shape[1]

    def tile(cols):
        return pl.BlockSpec((TOKEN_TILE, cols), lambda t: (t, 0))

    def whole(r, c):
        return pl.BlockSpec((r, c), lambda t: (0, 0))

    return pl.pallas_call(
        project_back_kernel,
        grid=(rows // TOKEN_TILE,),
        in_specs=[tile(QW), tile(KW), tile(KW), tile(128), tile(128), tile(D), tile(D), tile(D)]
        + [whole(D, D)]
        + [whole(QUARTER, width)] * 8
        + [whole(1, D)],
        out_specs=[tile(D), whole(HALF, QKV), whole(HALF, QKV), whole(1, D), whole(1, QKV)],
        out_shape=[
            jax.ShapeDtypeStruct((rows, D), F32),
            jax.ShapeDtypeStruct((HALF, QKV), BF16),
            jax.ShapeDtypeStruct((HALF, QKV), BF16),
            jax.ShapeDtypeStruct((1, D), F32),
            jax.ShapeDtypeStruct((1, QKV), F32),
        ],
        scratch_shapes=[pltpu.VMEM((D, QKV), BF16), pltpu.VMEM((D, QKV), F32)],
        compiler_params=params(48),
        cost_estimate=pl.CostEstimate(
            flops=4 * rows * D * (QKV + D), bytes_accessed=24 << 20, transcendentals=0
        ),
        name="project_back",
    )(dq, dk, dv, cos, sin, nl, xp, d_res, pi, *pieces, gain)


def column_blocks(matrix):
    return matrix.reshape(matrix.shape[0], -1, BW).transpose(1, 0, 2)


def rotate_into(left_side, tile_view, right_side):
    half_turn = jnp.einsum("sba,stbe->stae", left_side, tile_view, precision=lax.Precision.HIGHEST)
    return jnp.einsum("stae,sef->staf", half_turn, right_side, precision=lax.Precision.HIGHEST)


def rotate_back(left_side, tile_view, right_side):
    half_turn = jnp.einsum("sab,stbe->stae", left_side, tile_view, precision=lax.Precision.HIGHEST)
    return jnp.einsum("stae,sfe->staf", half_turn, right_side, precision=lax.Precision.HIGHEST)


def step_of(first_new, second_new):
    return (
        first_new
        / (1.0 - beta_first**STEP)
        / (jnp.sqrt(second_new / (1.0 - beta_second**STEP)) + adam_epsilon)
    )


def rotated_adam(block_grads, block_weights, first_moment, second_moment, basis_left, basis_right, slot_used):
    slot_total = block_grads.shape[0]
    tile_view = block_grads.reshape(slot_total, -1, BW, BW)
    rotated = rotate_into(basis_left, tile_view, basis_right).reshape(block_grads.shape)
    first_new = beta_first * first_moment + (1.0 - beta_first) * rotated
    second_new = beta_second * second_moment + (1.0 - beta_second) * rotated * rotated
    turned = rotate_back(
        basis_left, step_of(first_new, second_new).reshape(slot_total, -1, BW, BW), basis_right
    ).reshape(block_grads.shape)
    updated = block_weights - rate_matrix * (turned + weight_decay * block_weights)
    used = slot_used[:, None, None]
    return (
        jnp.where(used, first_new, 0.0),
        jnp.where(used, second_new, 0.0),
        jnp.where(used, updated, 0.0),
    )


def vector_adam(vectors, grad_vectors, vector_first, vector_second):
    first_new = beta_first * vector_first + (1.0 - beta_first) * grad_vectors
    second_new = beta_second * vector_second + (1.0 - beta_second) * grad_vectors * grad_vectors
    return (second_new, vectors - rate_vector * step_of(first_new, second_new))


def split_two(value):
    high = value.astype(BF16)
    return high, (value - high.astype(F32)).astype(BF16)


def on_device(
    places,
    inputs,
    cotangent,
    starts,
    query_weight,
    key_weight,
    value_weight,
    out_weight,
    gate_weight,
    up_weight,
    down_weight,
    vectors,
    owner_slot,
    first_moment,
    second_moment,
    basis_left,
    basis_right,
    vector_first,
    vector_second,
):
    n_dev, shard_rows = places.n_dev, places.rows
    here = inputs.shape[2]
    seq_index = lax.axis_index("seq")
    vec_here = vectors.shape[0]

    out_t, down_t = out_weight.T, down_weight.T
    attention_low = jnp.concatenate(
        [m.astype(BF16) for m in (query_weight, key_weight, value_weight, out_t)], axis=1
    )
    feed_low = [
        jnp.concatenate(
            [m[:, o : o + w].astype(BF16) for m in (gate_weight, up_weight, down_t)], axis=1
        )
        for o, w in zip(OFFSETS, CHUNKS)
    ]
    vectors_low = lax.all_gather(
        jnp.pad(vectors.astype(BF16), (0, 128 - vec_here)).reshape(1, 128), BOTH, axis=0, tiled=True
    )
    vectors_full = vectors_low[:, :vec_here].reshape(-1)

    natural = places.natural_rows()
    pi = (jnp.arange(D, dtype=jnp.int32)[:, None] == natural[None, :]).astype(BF16)
    gains = jnp.pad(vectors_full[: 2 * D].reshape(2, D), ((0, 6), (0, 0)))
    gains = dot_nn(gains, pi)
    gain_attn, gain_mlp = gains[0:1], gains[1:2]
    bias = vectors_full[2 * D :].astype(F32).reshape(1, QKV)

    attention_pieces = gather_pieces(places, attention_low)
    feed_pieces = [gather_pieces(places, shard) for shard in feed_low]

    spots = seq_index * here + jnp.arange(here, dtype=jnp.int32)
    own_starts = starts[:, 0]
    before = own_starts[:, None, :] <= spots[None, :, None]
    doc_begin = jnp.max(jnp.where(before, own_starts[:, None, :], 0), axis=2)
    relative = (spots[None, :] - doc_begin).astype(F32).reshape(-1)
    frequency = jnp.power(
        rope_theta, -jnp.arange(0, HEAD_SIZE, 2, dtype=F32) / HEAD_SIZE
    )
    angles = relative[:, None] * frequency[None, :]
    cos, sin = jnp.cos(angles), jnp.sin(angles)
    cos = jnp.concatenate([cos] * 4, axis=1)
    sin = jnp.concatenate([-sin, sin, -sin, sin], axis=1)
    begin = doc_begin + here - seq_index * here
    lo = begin[:, ::128] // 128
    begin = begin[:, :, None]

    x = inputs[:, 0].reshape(-1, D)
    cot = cotangent[:, 0].reshape(-1, D)
    cot_p = dot_nn(cot, pi).astype(BF16)
    cot_t = lax.dot_general(
        pi, cot, (((0,), (1,)), ((), ())), preferred_element_type=F32
    ).astype(BF16)

    xp, nl, q, k, v = project(x, pi, attention_pieces, gain_attn, bias, cos, sin)

    forth = [(2 * n, 2 * n + 1) for n in range(n_dev // 2)]
    back = [(2 * n + 1, 2 * n) for n in range(n_dev // 2)]
    kv = send(jnp.concatenate([k, v], axis=1), forth)

    def streams(array):
        return array.reshape(MICRO, here, array.shape[-1])

    heads = (
        lo,
        streams(q),
        streams(kv[:, :KW]),
        streams(k),
        streams(kv[:, KW:]),
        streams(v),
        begin,
    )
    attended, lse = attend(*heads)
    attended_flat = attended.reshape(-1, QW)
    residual, normed, normed_t = middle(attended_flat, xp, attention_pieces, gain_mlp)

    sums = None
    feed_shards = []
    for wide, pieces in zip(CHUNKS, feed_pieces):
        mlp, d_normed, own, other = feed(wide, normed, normed_t, cot_p, cot_t, sums, pieces)
        sums = (mlp, d_normed)
        feed_shards.append(reduce_rows(places, own, other))

    output, d_res, d_att, own_out, other_out, d_gain_mlp = middle_back(
        residual, sums[0], sums[1], cot_p, attended_flat, pi, attention_pieces, gain_mlp
    )
    grad_out_t = reduce_rows(places, own_out, other_out)
    dq, dkv_own, dkv_recv = attend_back(*heads, attended, streams(d_att), lse)
    dkv = (dkv_own + send(dkv_recv, back).astype(F32)).astype(BF16).reshape(-1, 2 * KW)
    input_grad, own_in, other_in, d_gain_attn, d_bias = project_back(
        dq.reshape(-1, QW), dkv[:, :KW], dkv[:, KW:], cos, sin, nl, xp, d_res, pi,
        attention_pieces, gain_attn,
    )

    d_gains = jnp.concatenate([d_gain_attn, d_gain_mlp, jnp.zeros((6, D), F32)], axis=0)
    high, rest = split_two(d_gains)
    d_gains = dot_nt(high, pi) + dot_nt(rest, pi)
    d_vectors = jnp.concatenate([d_gains[0], d_gains[1], d_bias[0]])
    lanes = -(-vec_here // shard_rows)
    d_vectors = jnp.pad(
        d_vectors.reshape(n_dev, vec_here), ((0, 0), (0, lanes * shard_rows - vec_here))
    ).reshape(D, lanes)
    riders = dot_tn(pi, jnp.pad(d_vectors, ((0, 0), (0, 128 - lanes))).astype(BF16)).astype(BF16)
    own_in = jnp.concatenate([own_in, riders[:HALF]], axis=1)
    other_in = jnp.concatenate([other_in, riders[HALF:]], axis=1)
    grad_in = reduce_rows(places, own_in, other_in)
    grad_vectors = grad_in[:, QKV : QKV + lanes].reshape(-1)[:vec_here]

    grad_query, grad_key, grad_value = (
        grad_in[:, :QW],
        grad_in[:, QW : QW + KW],
        grad_in[:, QW + KW : QKV],
    )
    grad_gate, grad_up, grad_down_t = (
        jnp.concatenate(
            [shard[:, m * w : (m + 1) * w] for shard, w in zip(feed_shards, CHUNKS)], axis=1
        )
        for m in range(3)
    )

    grads_all = jnp.concatenate([grad_in[:, :QKV], grad_out_t, grad_gate, grad_up, grad_down_t], axis=1)
    weights_all = jnp.concatenate(
        [query_weight, key_weight, value_weight, out_t, gate_weight, up_weight, down_t], axis=1
    )
    grad_blocks = column_blocks(grads_all.astype(BF16))
    weight_blocks = column_blocks(weights_all.astype(BF16))
    capacity = first_moment.shape[0]
    slot_count = n_dev * capacity
    slot_block = (
        jnp.full((slot_count,), -1, jnp.int32)
        .at[owner_slot]
        .set(jnp.arange(owner_slot.shape[0], dtype=jnp.int32))
    )
    slot_used = slot_block >= 0
    slot_index = jnp.maximum(slot_block, 0)
    owned_grads, owned_weights = (
        lax.all_to_all(
            jnp.take(blocks, slot_index, axis=0), BOTH, split_axis=0, concat_axis=1, tiled=True
        ).astype(F32)
        for blocks in (grad_blocks, weight_blocks)
    )
    local_used = lax.dynamic_slice_in_dim(
        slot_used, lax.axis_index(BOTH) * capacity, capacity, 0
    )
    new_first, new_second, new_blocks = rotated_adam(
        owned_grads, owned_weights, first_moment, second_moment, basis_left, basis_right, local_used
    )
    vector_second_new, vector_new = vector_adam(vectors, grad_vectors, vector_first, vector_second)
    return (
        output.reshape(inputs.shape),
        input_grad.reshape(inputs.shape),
        grad_query,
        grad_key,
        grad_value,
        grad_out_t.T,
        grad_gate,
        grad_up,
        grad_down_t.T,
        grad_vectors,
        new_first,
        new_second,
        new_blocks,
        vector_second_new,
        vector_new,
    )


def solution(mesh):
    rows = P(("dp", "seq"), None)
    columns = P(None, ("dp", "seq"))
    tokens = P(None, "dp", "seq", None)
    slots = P(("dp", "seq"), None, None)
    line = P(("dp", "seq"))
    places = Places(mesh.shape["dp"], mesh.shape["seq"])
    return jax.shard_map(
        functools.partial(on_device, places),
        mesh=mesh,
        in_specs=(
            tokens, tokens, P(None, "dp", None), rows, rows, rows, columns, rows, rows, columns,
            line, P(), slots, slots, slots, slots, line, line,
        ),
        out_specs=(
            tokens, tokens, rows, rows, rows, columns, rows, rows, columns, line,
            slots, slots, slots, line, line,
        ),
        check_vma=False,
    )
```

time: 2720 us -> 840 us (0.31)
  blocking collectives: 1630 us -> 65.9 us
  matrix products: 423 us -> 21.5 us
  Pallas kernels: 0 us -> 220 us
  local copies, waits for them, and re-layouts: 250 us -> 37.7 us
  waiting for transfers between devices: 68 us -> 268 us
  other arithmetic: 113 us -> 64.9 us
  starting transfers between devices: 194 us -> 150 us
    unnamed x4 -> x0, blocking collectives: 1490 us -> none
    dot_general x70 -> x5, matrix products: 409 us -> 7.37 us  [the longest x2 5.05 us: dot_nn(): lax.dot_general(a, b, (((1,), (0,)), ((), ())), preferred_element_type=F32)]
    pallas_call x0 -> x10, Pallas kernels: none -> 220 us  [the longest x4 132 us: feed(): pl.pallas_call(functools.partial(feed_kernel, wide, started), in_specs=[a...]
    ppermute x0 -> x88, waiting for transfers between devices: none -> 213 us  [send(): return lax.ppermute(array, BOTH, pairs)]
    unnamed x320 -> x297, local copies, waits for them, and re-layouts: 172 us -> 9.56 us
    ppermute x0 -> x88, starting transfers between devices: none -> 142 us  [send(): return lax.ppermute(array, BOTH, pairs)]
    unnamed x28 -> x0, starting transfers between devices: 125 us -> none
    all_gather x2 -> x1, blocking collectives: 140 us -> 65.9 us  [on_device(): lax.all_gather(jnp.pad(vectors.astype(BF16), (0, 128 - vec_here)).reshape...]
  transfers between devices with their start and end apart: 51 -> 90, of which waited for: 13 -> 30; matrix products, arithmetic and copies ran while one was open for 57% -> 9% of each run, Pallas kernels for 0% -> 16%
where the time goes in v1:
time: 840 us; the launch traced here: 831 us
  waiting for transfers between devices  268 us (32%)
  Pallas kernels  220 us (26%)
  starting transfers between devices  150 us (18%)
  blocking collectives  65.9 us (8%)
  other arithmetic  64.9 us (8%)
  local copies, waits for them, and re-layouts  37.7 us (4%)
  matrix products  21.5 us (3%)
    ppermute x88, waiting for transfers between devices, send(): return lax.ppermute(array, BOTH, pairs)  213 us
    ppermute x88, starting transfers between devices, send(): return lax.ppermute(array, BOTH, pairs)  142 us
    pallas_call x4, Pallas kernels, feed(): pl.pallas_call(functools.partial(feed_kernel, wide, started), in_specs=[a...  132 us
    all_gather x1, blocking collectives, on_device(): lax.all_gather(jnp.pad(vectors.astype(BF16), (0, 128 - vec_here)).reshape...  65.9 us
    all_to_all x2, waiting for transfers between devices, on_device(): lax.all_to_all(jnp.take(blocks, slot_index, axis=0), BOTH, split_axis=0,...  54.4 us
    pallas_call x1, Pallas kernels, attend_back(): pl.pallas_call(attend_back_kernel, grid_spec=pltpu.PrefetchScalarGridSpec...  27 us
    pallas_call x1, Pallas kernels, attend(): pl.pallas_call(attend_kernel, grid_spec=pltpu.PrefetchScalarGridSpec(num_...  18.6 us
  transfers between devices with their start and end apart: 90, of which 30 were waited for; matrix products, arithmetic and copies ran while one was open for 9% of the time, Pallas kernels for 16%

profile of v1, /device:TPU:0, one launch (start us, length us, event | category | flops | bytes accessed | tf_op | source)
XLA Modules:
  0.0 831.0 jit_solution(4596257646399878160)
XLA Ops:
  30.4 65.9 %all-gather.1 = bf16[32,1,128]{2,1,0:T(2,128)(2,1)S(1)} all-gather(bf16[1,1,128]{2,1,0:T(2,128)(2,1)S(1)} %pad_bitcast_fusion), channel_id=2, replica_groups=mesh['dp'=16,'seq'=2] {'dp','seq'}, dimensions={0}, use_global_device_ids=true | all-gather | bytes 8448 | tf_op jit(solution)/shard_map/all_gather | solution.py:860
  102.7 11.7 %collective-permute-done.3.refs_1_ = bf16[112,2048]{1,0:T(8,128)(2,1)S(1)} collective-permute-done((bf16[112,2048]{1,0:T(8,128)(2,1)S(1)}, bf16[112,2048]{1,0:T(8,128)(2,1)S(1)}, u32[]{:S(2)}, u32[]{:S(2)}) %collective-permute-start.3) | collective-permute-done | bytes 458784 | tf_op jit(solution)/shard_map/ppermute | solution.py:111
  126.7 10.7 %collective-permute-done.12 = bf16[28,3840]{1,0:T(8,128)(2,1)S(1)} collective-permute-done((bf16[28,3840]{1,0:T(8,128)(2,1)S(1)}, bf16[28,3840]{1,0:T(8,128)(2,1)S(1)}, u32[]{:S(2)}, u32[]{:S(2)}) %collective-permute-start.12) | collective-permute-done | bytes 215072 | tf_op jit(solution)/shard_map/ppermute | solution.py:111
  149.6 7.1 project.1
  163.3 12.3 %collective-permute-done.32 = bf16[28,3840]{1,0:T(8,128)(2,1)S(1)} collective-permute-done((bf16[28,3840]{1,0:T(8,128)(2,1)S(1)}, bf16[28,3840]{1,0:T(8,128)(2,1)S(1)}, u32[]{:S(2)}, u32[]{:S(2)}) %collective-permute-start.32) | collective-permute-done | bytes 215072 | tf_op jit(solution)/shard_map/ppermute | solution.py:111
  205.3 13.5 %collective-permute-done.24.refs_7_ = bf16[112,3840]{1,0:T(8,128)(2,1)} collective-permute-done((bf16[112,3840]{1,0:T(8,128)(2,1)S(1)}, bf16[112,3840]{1,0:T(8,128)(2,1)}, u32[]{:S(2)}, u32[]{:S(2)}) %collective-permute-start.24) | collective-permute-done | bytes 860192 | tf_op jit(solution)/shard_map/ppermute | solution.py:111
  227.0 12.9 %collective-permute-start.20 = (bf16[112,3840]{1,0:T(8,128)(2,1)S(1)}, bf16[112,3840]{1,0:T(8,128)(2,1)S(1)}, u32[]{:S(2)}, u32[]{:S(2)}) collective-permute-start(bf16[112,3840]{1,0:T(8,128)(2,1)S(1)} %collective-permute-done.16.refs_7_), channel_id=1, source_target_pairs={{0,2},{1,3},{2,0},{3,1},{4,6},{5,7},{6,4},{7,5},{8,10},{9,11},{10,... | collective-permute-start | bytes 2580488 | tf_op jit(solution)/shard_map/ppermute | solution.py:111
  240.1 18.6 %attend.1 = (bf16[2,512,896]{2,1,0:T(8,128)(2,1)S(1)}, f32[2,512,128]{2,1,0:T(8,128)S(1)}) custom-call(s32[2,4]{1,0:T(2,128)S(1)} %and_select_fusion.lo_ref, bf16[2,512,896]{2,1,0:T(8,128)(2,1)S(1)} %bitcast.110, bf16[2,512,128]{2,1,0:T(8,128)(2,1)S(1)} %bitcast.106, bf16[2,512,128]{2,1,0:T(8,128)(2,1)S(1)} %bitcast.100, bf16[2,512,128]{2,1,0:T(8,128)(2,1)S(1)} %bitcast.104, ...), custom_call_target="tpu_custom_call" | custom-call | flops 20000000000 | bytes 6291456 | tf_op jit(solution)/shard_map/attend/pallas_call | solution.py:299
  267.9 5.5 collective-permute-start.28
  275.6 33.3 %feed.4 = (f32[1024,896]{1,0:T(8,128)}, f32[1024,896]{1,0:T(8,128)}, bf16[448,3840]{1,0:T(8,128)(2,1)}, bf16[448,3840]{1,0:T(8,128)(2,1)}) custom-call(bf16[1024,896]{1,0:T(8,128)(2,1)} %copy-done.39, bf16[896,1024]{1,0:T(8,128)(2,1)} %copy-done.40, bf16[1024,896]{1,0:T(8,128)(2,1)} %bitcast.114, bf16[896,1024]{1,0:T(8,128)(2,1)} %copy.96.refs_3_, ...), custom_call_target="tpu_custom_call" | custom-call | flops 21139292160 | bytes 44040192 | tf_op jit(solution)/shard_map/feed/pallas_call | solution.py:661
  311.2 34.6 %feed.5 = (f32[1024,896]{1,0:T(8,128)}, f32[1024,896]{1,0:T(8,128)}, bf16[448,3840]{1,0:T(8,128)(2,1)}, bf16[448,3840]{1,0:T(8,128)(2,1)}) custom-call(bf16[1024,896]{1,0:T(8,128)(2,1)} %copy-done.39, bf16[896,1024]{1,0:T(8,128)(2,1)} %copy-done.40, bf16[1024,896]{1,0:T(8,128)(2,1)} %bitcast.115, bf16[896,1024]{1,0:T(8,128)(2,1)} %copy.96.refs_3_, ...), custom_call_target="tpu_custom_call" | custom-call | flops 21139292160 | bytes 44040192 | tf_op jit(solution)/shard_map/feed/pallas_call | solution.py:661
  347.0 34.7 %feed.6 = (f32[1024,896]{1,0:T(8,128)}, f32[1024,896]{1,0:T(8,128)}, bf16[448,3840]{1,0:T(8,128)(2,1)}, bf16[448,3840]{1,0:T(8,128)(2,1)}) custom-call(bf16[1024,896]{1,0:T(8,128)(2,1)} %copy-done.39, bf16[896,1024]{1,0:T(8,128)(2,1)} %copy-done.40, bf16[1024,896]{1,0:T(8,128)(2,1)} %bitcast.116, bf16[896,1024]{1,0:T(8,128)(2,1)} %copy.96.refs_3_, ...), custom_call_target="tpu_custom_call" | custom-call | flops 21139292160 | bytes 44040192 | tf_op jit(solution)/shard_map/feed/pallas_call | solution.py:661
  382.9 29.3 %feed.7 = (f32[1024,896]{1,0:T(8,128)}, f32[1024,896]{1,0:T(8,128)}, bf16[448,3072]{1,0:T(8,128)(2,1)}, bf16[448,3072]{1,0:T(8,128)(2,1)}) custom-call(bf16[1024,896]{1,0:T(8,128)(2,1)} %copy-done.39, bf16[896,1024]{1,0:T(8,128)(2,1)} %copy-done.40, bf16[1024,896]{1,0:T(8,128)(2,1)} %bitcast.117, bf16[896,1024]{1,0:T(8,128)(2,1)} %copy.96.refs_3_, ...), custom_call_target="tpu_custom_call" | custom-call | flops 16911433728 | bytes 44040192 | tf_op jit(solution)/shard_map/feed/pallas_call | solution.py:661
  412.2 13.6 %middle_back.1 = (bf16[1024,896]{1,0:T(8,128)(2,1)}, f32[1024,896]{1,0:T(8,128)}, bf16[1024,896]{1,0:T(8,128)(2,1)}, bf16[448,896]{1,0:T(8,128)(2,1)S(1)}, bf16[...) custom-call(f32[1024,896]{1,0:T(8,128)} %get-tuple-element.61.res_ref, f32[1024,896]{1,0:T(8,128)} %get-tuple-element.70.mlp_ref, ...), custom_call_target="tpu_custom_call" | custom-call | flops 4932501504 | bytes 27262976 | tf_op jit(solution)/shard_map/middle_back/pallas_call | solution.py:518
  427.4 27.0 %attend_back.1 = (bf16[2,512,896]{2,1,0:T(8,128)(2,1)S(1)}, f32[2,512,256]{2,1,0:T(8,128)S(1)}, bf16[2,512,256]{2,1,0:T(8,128)(2,1)S(1)}) custom-call(s32[2,4]{1,0:T(2,128)S(1)} %and_select_fusion.lo_ref, bf16[2,512,896]{2,1,0:T(8,128)(2,1)S(1)} %bitcast.111, bf16[2,512,128]{2,1,0:T(8,128)(2,1)S(1)} %bitcast.107, bf16[2,512,128]{2,1,0:T(8,128)(2,1)S(1)} %bitcast.101, ...), custom_call_target="tpu_custom_call" | custom-call | flops 49999998976 | bytes 10485760 | tf_op jit(solution)/shard_map/attend_back/pallas_call | solution.py:398
  457.1 15.8 %collective-permute-done.51 = bf16[2,512,256]{2,1,0:T(8,128)(2,1)S(1)} collective-permute-done((bf16[2,512,256]{2,1,0:T(8,128)(2,1)S(1)}, bf16[2,512,256]{2,1,0:T(8,128)(2,1)S(1)}, u32[]{:S(2)}, u32[]{:S(2)}) %collective-permute-start.51) | collective-permute-done | bytes 524320 | tf_op jit(solution)/shard_map/ppermute | solution.py:111
  473.2 16.7 %project_back.1 = (f32[1024,896]{1,0:T(8,128)}, bf16[448,1152]{1,0:T(8,128)(2,1)}, bf16[448,1152]{1,0:T(8,128)(2,1)}, f32[1,896]{1,0:T(1,128)S(1)}, f32[1,1152]{1,0:T(1,128)S(1)}) custom-call(bf16[1024,896]{1,0:T(8,128)(2,1)} %bitcast.112, bf16[1024,128]{1,0:T(8,128)(2,1)S(1)} %get-tuple-element.217.dk_ref, bf16[1024,128]{1,0:T(8,128)(2,1)S(1)} %get-tuple-element.216.dv_ref, ...), custom_call_target="tpu_custom_call" | custom-call | flops 7516192768 | bytes 25165824 | tf_op jit(solution)/shard_map/project_back/pallas_call | solution.py:749
  515.9 5.9 collective-permute-done.53
  533.8 8.0 collective-permute-start.57
  541.8 7.7 collective-permute-start.56
  551.5 5.5 collective-permute-done.56
  567.3 12.3 %collective-permute-done.83 = bf16[224,3072]{1,0:T(8,128)(2,1)S(1)} collective-permute-done((bf16[224,3072]{1,0:T(8,128)(2,1)S(1)}, bf16[224,3072]{1,0:T(8,128)(2,1)S(1)}, u32[]{:S(2)}, u32[]{:S(2)}) %collective-permute-start.83) | collective-permute-done | bytes 1376288 | tf_op jit(solution)/shard_map/ppermute | solution.py:111
  583.9 15.5 %collective-permute-done.84 = bf16[112,3072]{1,0:T(8,128)(2,1)S(1)} collective-permute-done((bf16[112,3072]{1,0:T(8,128)(2,1)S(1)}, bf16[112,3072]{1,0:T(8,128)(2,1)S(1)}, u32[]{:S(2)}, u32[]{:S(2)}) %collective-permute-start.84) | collective-permute-done | bytes 688160 | tf_op jit(solution)/shard_map/ppermute | solution.py:111
  611.7 6.9 collective-permute-done.86
  620.7 6.1 collective-permute-done.71
  628.2 35.4 %collective-permute-done.65 = bf16[224,3840]{1,0:T(8,128)(2,1)S(1)} collective-permute-done((bf16[224,3840]{1,0:T(8,128)(2,1)S(1)}, bf16[224,3840]{1,0:T(8,128)(2,1)S(1)}, u32[]{:S(2)}, u32[]{:S(2)}) %collective-permute-start.65) | collective-permute-done | bytes 1720352 | tf_op jit(solution)/shard_map/ppermute | solution.py:111
  669.5 7.2 collective-permute-done.66
  688.1 15.1 %collective-permute-done.68 = bf16[28,3840]{1,0:T(8,128)(2,1)S(1)} collective-permute-done((bf16[28,3840]{1,0:T(8,128)(2,1)S(1)}, bf16[28,3840]{1,0:T(8,128)(2,1)S(1)}, u32[]{:S(2)}, u32[]{:S(2)}) %collective-permute-start.68) | collective-permute-done | bytes 215072 | tf_op jit(solution)/shard_map/ppermute | solution.py:111
  703.3 9.3 %collective-permute-start.73 = (bf16[28,3840]{1,0:T(8,128)(2,1)S(1)}, bf16[28,3840]{1,0:T(8,128)(2,1)S(1)}, u32[]{:S(2)}, u32[]{:S(2)}) collective-permute-start(bf16[28,3840]{1,0:T(8,128)(2,1)S(1)} %get-tuple-element.207), channel_id=1, source_target_pairs={{0,8},{1,9},{2,10},{3,11},{4,12},{5,13},{6,14},{7,15},{8,16},{9,17... | collective-permute-start | bytes 645128 | tf_op jit(solution)/shard_map/ppermute | solution.py:111
  712.7 12.1 %collective-permute-start.79 = (bf16[28,3840]{1,0:T(8,128)(2,1)S(1)}, bf16[28,3840]{1,0:T(8,128)(2,1)S(1)}, u32[]{:S(2)}, u32[]{:S(2)}) collective-permute-start(bf16[28,3840]{1,0:T(8,128)(2,1)S(1)} %get-tuple-element.210), channel_id=1, source_target_pairs={{0,8},{1,9},{2,10},{3,11},{4,12},{5,13},{6,14},{7,15},{8,16},{9,17... | collective-permute-start | bytes 645128 | tf_op jit(solution)/shard_map/ppermute | solution.py:111
  744.0 27.5 %all-to-all-done = bf16[160,28,128]{2,1,0:T(8,128)(2,1)S(1)} async-done(((bf16[160,28,128]{2,1,0:T(8,128)(2,1)}), bf16[160,28,128]{2,1,0:T(8,128)(2,1)S(1)}, u32[]{:S(2)}, u32[]{:S(2)}) %all-to-all-start) | async-done | bytes 1146912 | tf_op jit(solution)/shard_map/all_to_all | solution.py:980
  780.1 26.9 %all-to-all-done.1 = bf16[160,28,128]{2,1,0:T(8,128)(2,1)} async-done(((bf16[160,28,128]{2,1,0:T(8,128)(2,1)}), bf16[160,28,128]{2,1,0:T(8,128)(2,1)}, u32[]{:S(2)}, u32[]{:S(2)}) %all-to-all-start.1) | async-done | bytes 1146912 | tf_op jit(solution)/shard_map/all_to_all | solution.py:980
  (586 shorter events, 262.8 us)
Async XLA Ops:
  7.2 92.4 %collective-permute-start.2 = (bf16[28,2048]{1,0:T(8,128)(2,1)}, bf16[28,2048]{1,0:T(8,128)(2,1)}, u32[]{:S(2)}, u32[]{:S(2)}) collective-permute-start(bf16[28,2048]{1,0:T(8,128)(2,1)} %pad_maximum_fusion.16), channel_id=1, source_target_pairs={{0,8},{1,9},{2,10},{3,11},{4,12},{5,13},{6,14},{7,15},{8,16},{9,17... | collective-permute-start | bytes 344072 | tf_op jit(solution)/shard_map/ppermute | solution.py:111
  10.2 89.5 %collective-permute-start.1 = (bf16[28,2048]{1,0:T(8,128)(2,1)}, bf16[28,2048]{1,0:T(8,128)(2,1)}, u32[]{:S(2)}, u32[]{:S(2)}) collective-permute-start(bf16[28,2048]{1,0:T(8,128)(2,1)} %pad_maximum_fusion.16), channel_id=1, source_target_pairs={{0,16},{1,17},{2,18},{3,19},{4,20},{5,21},{6,22},{7,23},{8,24},{9,... | collective-permute-start | bytes 344072 | tf_op jit(solution)/shard_map/ppermute | solution.py:111
  12.8 86.9 %collective-permute-start = (bf16[28,2048]{1,0:T(8,128)(2,1)}, bf16[28,2048]{1,0:T(8,128)(2,1)}, u32[]{:S(2)}, u32[]{:S(2)}) collective-permute-start(bf16[28,2048]{1,0:T(8,128)(2,1)} %pad_maximum_fusion.16), channel_id=1, source_target_pairs={{0,24},{1,25},{2,26},{3,27},{4,28},{5,29},{6,30},{7,31},{8,0},{9,1... | collective-permute-start | bytes 344072 | tf_op jit(solution)/shard_map/ppermute | solution.py:111
  18.9 96.6 %collective-permute-start.43 = (bf16[28,3072]{1,0:T(8,128)(2,1)}, bf16[28,3072]{1,0:T(8,128)(2,1)}, u32[]{:S(2)}, u32[]{:S(2)}) collective-permute-start(bf16[28,3072]{1,0:T(8,128)(2,1)} %pad_maximum_fusion.15), channel_id=1, source_target_pairs={{0,8},{1,9},{2,10},{3,11},{4,12},{5,13},{6,14},{7,15},{8,16},{9,17... | collective-permute-start | bytes 516104 | tf_op jit(solution)/shard_map/ppermute | solution.py:111
  19.6 97.9 %collective-permute-start.42 = (bf16[28,3072]{1,0:T(8,128)(2,1)}, bf16[28,3072]{1,0:T(8,128)(2,1)}, u32[]{:S(2)}, u32[]{:S(2)}) collective-permute-start(bf16[28,3072]{1,0:T(8,128)(2,1)} %pad_maximum_fusion.15), channel_id=1, source_target_pairs={{0,16},{1,17},{2,18},{3,19},{4,20},{5,21},{6,22},{7,23},{8,24},{9,... | collective-permute-start | bytes 516104 | tf_op jit(solution)/shard_map/ppermute | solution.py:111
  202.6 63.8 %collective-permute-start.34 = (bf16[112,3840]{1,0:T(8,128)(2,1)}, bf16[112,3840]{1,0:T(8,128)(2,1)}, u32[]{:S(2)}, u32[]{:S(2)}) collective-permute-start(bf16[112,3840]{1,0:T(8,128)(2,1)} %pad_maximum_fusion.3.refs_6_), channel_id=1, source_target_pairs={{0,1},{1,0},{2,6},{3,7},{4,5},{5,4},{6,2},{7,3},{8,9},{9,8},{10,14... | collective-permute-start | bytes 2580488 | tf_op jit(solution)/shard_map/ppermute | solution.py:111
  218.8 49.1 %collective-permute-start.18 = (bf16[112,3840]{1,0:T(8,128)(2,1)}, bf16[112,3840]{1,0:T(8,128)(2,1)S(1)}, u32[]{:S(2)}, u32[]{:S(2)}) collective-permute-start(bf16[112,3840]{1,0:T(8,128)(2,1)} %collective-permute-done.14.refs_5_), channel_id=1, source_target_pairs={{0,2},{1,3},{2,0},{3,1},{4,6},{5,7},{6,4},{7,5},{8,10},{9,11},{10,... | collective-permute-start | bytes 2580488 | tf_op jit(solution)/shard_map/ppermute | solution.py:111
  218.8 54.6 %collective-permute-start.19 = (bf16[112,3840]{1,0:T(8,128)(2,1)}, bf16[112,3840]{1,0:T(8,128)(2,1)S(1)}, u32[]{:S(2)}, u32[]{:S(2)}) collective-permute-start(bf16[112,3840]{1,0:T(8,128)(2,1)} %collective-permute-done.15.refs_6_), channel_id=1, source_target_pairs={{0,2},{1,3},{2,0},{3,1},{4,6},{5,7},{6,4},{7,5},{8,10},{9,11},{10,... | collective-permute-start | bytes 2580488 | tf_op jit(solution)/shard_map/ppermute | solution.py:111
  223.9 49.6 %collective-permute-start.26 = (bf16[112,3840]{1,0:T(8,128)(2,1)}, bf16[112,3840]{1,0:T(8,128)(2,1)}, u32[]{:S(2)}, u32[]{:S(2)}) collective-permute-start(bf16[112,3840]{1,0:T(8,128)(2,1)} %collective-permute-done.24.refs_7_), channel_id=1, source_target_pairs={{0,4},{1,5},{2,3},{3,2},{4,0},{5,1},{6,7},{7,6},{8,12},{9,13},{10,... | collective-permute-start | bytes 2580488 | tf_op jit(solution)/shard_map/ppermute | solution.py:111
  227.0 46.5 %collective-permute-start.20 = (bf16[112,3840]{1,0:T(8,128)(2,1)S(1)}, bf16[112,3840]{1,0:T(8,128)(2,1)S(1)}, u32[]{:S(2)}, u32[]{:S(2)}) collective-permute-start(bf16[112,3840]{1,0:T(8,128)(2,1)S(1)} %collective-permute-done.16.refs_7_), channel_id=1, source_target_pairs={{0,2},{1,3},{2,0},{3,1},{4,6},{5,7},{6,4},{7,5},{8,10},{9,11},{10,... | collective-permute-start | bytes 2580488 | tf_op jit(solution)/shard_map/ppermute | solution.py:111
  266.4 42.6 %collective-permute-start.35 = (bf16[112,3840]{1,0:T(8,128)(2,1)}, bf16[112,3840]{1,0:T(8,128)(2,1)S(1)}, u32[]{:S(2)}, u32[]{:S(2)}) collective-permute-start(bf16[112,3840]{1,0:T(8,128)(2,1)} %pad_maximum_fusion.3.refs_6_), channel_id=1, source_target_pairs={{0,4},{1,5},{2,3},{3,2},{4,0},{5,1},{6,7},{7,6},{8,12},{9,13},{10,... | collective-permute-start | bytes 2580488 | tf_op jit(solution)/shard_map/ppermute | solution.py:111
  267.9 42.0 %collective-permute-start.28 = (bf16[112,3840]{1,0:T(8,128)(2,1)}, bf16[112,3840]{1,0:T(8,128)(2,1)S(1)}, u32[]{:S(2)}, u32[]{:S(2)}) collective-permute-start(bf16[112,3840]{1,0:T(8,128)(2,1)} %collective-permute-done.24.refs_7_), channel_id=1, source_target_pairs={{0,2},{1,3},{2,0},{3,1},{4,6},{5,7},{6,4},{7,5},{8,10},{9,11},{10,... | collective-permute-start | bytes 2580488 | tf_op jit(solution)/shard_map/ppermute | solution.py:111
  273.4 36.6 %collective-permute-start.29 = (bf16[112,3840]{1,0:T(8,128)(2,1)}, bf16[112,3840]{1,0:T(8,128)(2,1)}, u32[]{:S(2)}, u32[]{:S(2)}) collective-permute-start(bf16[112,3840]{1,0:T(8,128)(2,1)} %collective-permute-done.25.refs_8_), channel_id=1, source_target_pairs={{0,2},{1,3},{2,0},{3,1},{4,6},{5,7},{6,4},{7,5},{8,10},{9,11},{10,... | collective-permute-start | bytes 2580488 | tf_op jit(solution)/shard_map/ppermute | solution.py:111
  273.5 37.2 %collective-permute-start.36 = (bf16[112,3840]{1,0:T(8,128)(2,1)}, bf16[112,3840]{1,0:T(8,128)(2,1)S(1)}, u32[]{:S(2)}, u32[]{:S(2)}) collective-permute-start(bf16[112,3840]{1,0:T(8,128)(2,1)} %collective-permute-done.34.refs_7_), channel_id=1, source_target_pairs={{0,4},{1,5},{2,3},{3,2},{4,0},{5,1},{6,7},{7,6},{8,12},{9,13},{10,... | collective-permute-start | bytes 2580488 | tf_op jit(solution)/shard_map/ppermute | solution.py:111
  273.5 37.3 %collective-permute-start.30 = (bf16[112,3840]{1,0:T(8,128)(2,1)}, bf16[112,3840]{1,0:T(8,128)(2,1)}, u32[]{:S(2)}, u32[]{:S(2)}) collective-permute-start(bf16[112,3840]{1,0:T(8,128)(2,1)} %collective-permute-done.26.refs_9_), channel_id=1, source_target_pairs={{0,2},{1,3},{2,0},{3,1},{4,6},{5,7},{6,4},{7,5},{8,10},{9,11},{10,... | collective-permute-start | bytes 2580488 | tf_op jit(solution)/shard_map/ppermute | solution.py:111
  309.0 36.9 %collective-permute-start.37 = (bf16[112,3840]{1,0:T(8,128)(2,1)}, bf16[112,3840]{1,0:T(8,128)(2,1)S(1)}, u32[]{:S(2)}, u32[]{:S(2)}) collective-permute-start(bf16[112,3840]{1,0:T(8,128)(2,1)} %pad_maximum_fusion.3.refs_6_), channel_id=1, source_target_pairs={{0,2},{1,3},{2,0},{3,1},{4,6},{5,7},{6,4},{7,5},{8,10},{9,11},{10,... | collective-permute-start | bytes 2580488 | tf_op jit(solution)/shard_map/ppermute | solution.py:111
  309.9 36.2 %collective-permute-start.46 = (bf16[112,3072]{1,0:T(8,128)(2,1)}, bf16[112,3072]{1,0:T(8,128)(2,1)}, u32[]{:S(2)}, u32[]{:S(2)}) collective-permute-start(bf16[112,3072]{1,0:T(8,128)(2,1)} %collective-permute-done.44.refs_7_), channel_id=1, source_target_pairs={{0,4},{1,5},{2,3},{3,2},{4,0},{5,1},{6,7},{7,6},{8,12},{9,13},{10,... | collective-permute-start | bytes 2064392 | tf_op jit(solution)/shard_map/ppermute | solution.py:111
  310.0 36.5 %collective-permute-start.38 = (bf16[112,3840]{1,0:T(8,128)(2,1)}, bf16[112,3840]{1,0:T(8,128)(2,1)}, u32[]{:S(2)}, u32[]{:S(2)}) collective-permute-start(bf16[112,3840]{1,0:T(8,128)(2,1)} %collective-permute-done.34.refs_7_), channel_id=1, source_target_pairs={{0,2},{1,3},{2,0},{3,1},{4,6},{5,7},{6,4},{7,5},{8,10},{9,11},{10,... | collective-permute-start | bytes 2580488 | tf_op jit(solution)/shard_map/ppermute | solution.py:111
  310.7 35.9 %collective-permute-start.39 = (bf16[112,3840]{1,0:T(8,128)(2,1)S(1)}, bf16[112,3840]{1,0:T(8,128)(2,1)}, u32[]{:S(2)}, u32[]{:S(2)}) collective-permute-start(bf16[112,3840]{1,0:T(8,128)(2,1)S(1)} %collective-permute-done.35.refs_8_), channel_id=1, source_target_pairs={{0,2},{1,3},{2,0},{3,1},{4,6},{5,7},{6,4},{7,5},{8,10},{9,11},{10,... | collective-permute-start | bytes 2580488 | tf_op jit(solution)/shard_map/ppermute | solution.py:111
  310.8 36.2 %collective-permute-start.40 = (bf16[112,3840]{1,0:T(8,128)(2,1)S(1)}, bf16[112,3840]{1,0:T(8,128)(2,1)}, u32[]{:S(2)}, u32[]{:S(2)}) collective-permute-start(bf16[112,3840]{1,0:T(8,128)(2,1)S(1)} %collective-permute-done.36.refs_9_), channel_id=1, source_target_pairs={{0,2},{1,3},{2,0},{3,1},{4,6},{5,7},{6,4},{7,5},{8,10},{9,11},{10,... | collective-permute-start | bytes 2580488 | tf_op jit(solution)/shard_map/ppermute | solution.py:111
  345.9 35.8 %collective-permute-start.47 = (bf16[112,3072]{1,0:T(8,128)(2,1)}, bf16[112,3072]{1,0:T(8,128)(2,1)S(1)}, u32[]{:S(2)}, u32[]{:S(2)}) collective-permute-start(bf16[112,3072]{1,0:T(8,128)(2,1)} %pad_maximum_fusion.4.refs_6_), channel_id=1, source_target_pairs={{0,2},{1,3},{2,0},{3,1},{4,6},{5,7},{6,4},{7,5},{8,10},{9,11},{10,... | collective-permute-start | bytes 2064392 | tf_op jit(solution)/shard_map/ppermute | solution.py:111
  509.5 48.4 %collective-permute-start.82 = (bf16[448,3072]{1,0:T(8,128)(2,1)}, bf16[448,3072]{1,0:T(8,128)(2,1)}, u32[]{:S(2)}, u32[]{:S(2)}) collective-permute-start(bf16[448,3072]{1,0:T(8,128)(2,1)} %get-tuple-element.95), channel_id=1, source_target_pairs={{0,2},{1,3},{2,0},{3,1},{4,6},{5,7},{6,4},{7,5},{8,10},{9,11},{10,... | collective-permute-start | bytes 8257544 | tf_op jit(solution)/shard_map/ppermute | solution.py:111
  509.6 54.6 %collective-permute-start.76 = (bf16[448,3840]{1,0:T(8,128)(2,1)}, bf16[448,3840]{1,0:T(8,128)(2,1)}, u32[]{:S(2)}, u32[]{:S(2)}) collective-permute-start(bf16[448,3840]{1,0:T(8,128)(2,1)} %get-tuple-element.93), channel_id=1, source_target_pairs={{0,2},{1,3},{2,0},{3,1},{4,6},{5,7},{6,4},{7,5},{8,10},{9,11},{10,... | collective-permute-start | bytes 10321928 | tf_op jit(solution)/shard_map/ppermute | solution.py:111
  562.9 42.0 %collective-permute-start.64 = (bf16[448,3840]{1,0:T(8,128)(2,1)}, bf16[448,3840]{1,0:T(8,128)(2,1)S(1)}, u32[]{:S(2)}, u32[]{:S(2)}) collective-permute-start(bf16[448,3840]{1,0:T(8,128)(2,1)} %get-tuple-element.89), channel_id=1, source_target_pairs={{0,2},{1,3},{2,0},{3,1},{4,6},{5,7},{6,4},{7,5},{8,10},{9,11},{10,... | collective-permute-start | bytes 10321928 | tf_op jit(solution)/shard_map/ppermute | solution.py:111
  566.4 52.4 %collective-permute-start.77 = (bf16[224,3840]{1,0:T(8,128)(2,1)S(1)}, bf16[224,3840]{1,0:T(8,128)(2,1)S(1)}, u32[]{:S(2)}, u32[]{:S(2)}) collective-permute-start(bf16[224,3840]{1,0:T(8,128)(2,1)S(1)} %add_convert_fusion), channel_id=1, source_target_pairs={{0,4},{1,5},{2,3},{3,2},{4,0},{5,1},{6,7},{7,6},{8,12},{9,13},{10,... | collective-permute-start | bytes 5160968 | tf_op jit(solution)/shard_map/ppermute | solution.py:111
  581.8 45.0 %collective-permute-start.71 = (bf16[224,3840]{1,0:T(8,128)(2,1)S(1)}, bf16[224,3840]{1,0:T(8,128)(2,1)S(1)}, u32[]{:S(2)}, u32[]{:S(2)}) collective-permute-start(bf16[224,3840]{1,0:T(8,128)(2,1)S(1)} %add_convert_fusion.1), channel_id=1, source_target_pairs={{0,4},{1,5},{2,3},{3,2},{4,0},{5,1},{6,7},{7,6},{8,12},{9,13},{10,... | collective-permute-start | bytes 5160968 | tf_op jit(solution)/shard_map/ppermute | solution.py:111
  610.2 53.4 %collective-permute-start.65 = (bf16[224,3840]{1,0:T(8,128)(2,1)S(1)}, bf16[224,3840]{1,0:T(8,128)(2,1)S(1)}, u32[]{:S(2)}, u32[]{:S(2)}) collective-permute-start(bf16[224,3840]{1,0:T(8,128)(2,1)S(1)} %add_convert_fusion.2), channel_id=1, source_target_pairs={{0,4},{1,5},{2,3},{3,2},{4,0},{5,1},{6,7},{7,6},{8,12},{9,13},{10,... | collective-permute-start | bytes 5160968 | tf_op jit(solution)/shard_map/ppermute | solution.py:111
  620.4 43.6 %collective-permute-start.78 = (bf16[112,3840]{1,0:T(8,128)(2,1)S(1)}, bf16[112,3840]{1,0:T(8,128)(2,1)S(1)}, u32[]{:S(2)}, u32[]{:S(2)}) collective-permute-start(bf16[112,3840]{1,0:T(8,128)(2,1)S(1)} %add_convert_fusion.4), channel_id=1, source_target_pairs={{0,1},{1,0},{2,6},{3,7},{4,5},{5,4},{6,2},{7,3},{8,9},{9,8},{10,14... | collective-permute-start | bytes 2580488 | tf_op jit(solution)/shard_map/ppermute | solution.py:111
  627.1 53.2 %collective-permute-start.72 = (bf16[112,3840]{1,0:T(8,128)(2,1)S(1)}, bf16[112,3840]{1,0:T(8,128)(2,1)S(1)}, u32[]{:S(2)}, u32[]{:S(2)}) collective-permute-start(bf16[112,3840]{1,0:T(8,128)(2,1)S(1)} %add_convert_fusion.5), channel_id=1, source_target_pairs={{0,1},{1,0},{2,6},{3,7},{4,5},{5,4},{6,2},{7,3},{8,9},{9,8},{10,14... | collective-permute-start | bytes 2580488 | tf_op jit(solution)/shard_map/ppermute | solution.py:111
  665.7 61.6 %collective-permute-start.81 = (bf16[28,3840]{1,0:T(8,128)(2,1)S(1)}, bf16[28,3840]{1,0:T(8,128)(2,1)S(1)}, u32[]{:S(2)}, u32[]{:S(2)}) collective-permute-start(bf16[28,3840]{1,0:T(8,128)(2,1)S(1)} %get-tuple-element.211), channel_id=1, source_target_pairs={{0,24},{1,25},{2,26},{3,27},{4,28},{5,29},{6,30},{7,31},{8,0},{9,1... | collective-permute-start | bytes 645128 | tf_op jit(solution)/shard_map/ppermute | solution.py:111
  667.2 60.1 %collective-permute-start.80 = (bf16[28,3840]{1,0:T(8,128)(2,1)S(1)}, bf16[28,3840]{1,0:T(8,128)(2,1)S(1)}, u32[]{:S(2)}, u32[]{:S(2)}) collective-permute-start(bf16[28,3840]{1,0:T(8,128)(2,1)S(1)} %get-tuple-element.212), channel_id=1, source_target_pairs={{0,16},{1,17},{2,18},{3,19},{4,20},{5,21},{6,22},{7,23},{8,24},{9,... | collective-permute-start | bytes 645128 | tf_op jit(solution)/shard_map/ppermute | solution.py:111
  735.4 36.1 %all-to-all-start = ((bf16[160,28,128]{2,1,0:T(8,128)(2,1)}), bf16[160,28,128]{2,1,0:T(8,128)(2,1)S(1)}, u32[]{:S(2)}, u32[]{:S(2)}) async-start(bf16[160,28,128]{2,1,0:T(8,128)(2,1)} %get-tuple-element.261), calls=%async_computation | async-start | bytes 2621440 | tf_op jit(solution)/shard_map/all_to_all | solution.py:980
  (199 other events, 3698.3 us)

commit v2 on v1

v2 whole, which is shorter than its diff:
```python
import functools
import math

import jax
import jax.numpy as jnp
import numpy as np
from jax import lax
from jax.experimental import pallas as pl
from jax.experimental.pallas import tpu as pltpu
from jax.sharding import PartitionSpec as P

D = 896
QUERY_HEADS = 14
KEY_VALUE_HEADS = 2
HEAD_SIZE = 64
BW = 128
MICRO = 2
STEP = 10
QW = 896
KW = 128
QKV = QW + 2 * KW
FF = 4864

norm_epsilon = 1e-06
rope_theta = 1000000.0
beta_first = 0.9
beta_second = 0.999
adam_epsilon = 1e-08
weight_decay = 0.01
rate_matrix = 0.1
rate_vector = 0.5
masked_value = -1e30

F32 = jnp.float32
BF16 = jnp.bfloat16
BOTH = ("dp", "seq")

TILE = 256
CHUNKS = (1280, 1280, 1280, 1024)
OFFSETS = (0, 1280, 2560, 3840)
QUARTER = 112
HALF = 448
TOKEN_TILE = 256

HEAD_SETS = (
    ((0, 1, 2, 3), 0, 0),
    ((0, 1, 2), 1, 0),
    ((3, 4, 5, 6), 1, 1),
    ((4, 5, 6), 0, 1),
)
SET_ROWS = (0, 512, 896, 1408)
ALL_ROWS = 1792


def params(mib, **more):
    return pltpu.CompilerParams(vmem_limit_bytes=mib * 1024 * 1024, **more)


def dot_nn(a, b):
    return lax.dot_general(a, b, (((1,), (0,)), ((), ())), preferred_element_type=F32)


def dot_nt(a, b):
    return lax.dot_general(a, b, (((1,), (1,)), ((), ())), preferred_element_type=F32)


def dot_tn(a, b):
    return lax.dot_general(a, b, (((0,), (0,)), ((), ())), preferred_element_type=F32)


def following(kernel, n_in, after):
    def wrapped(*refs):
        return kernel(*refs[:n_in], *refs[n_in + len(after) :])

    return wrapped


TINY = pl.CostEstimate(flops=1, bytes_accessed=1, transcendentals=0)
ANYWHERE = pl.BlockSpec(memory_space=pl.ANY)


class Places:
    def __init__(self, n_dp, n_seq):
        self.line = n_dp // 4
        self.rows = D // (n_dp * n_seq)
        self.n_dev = n_dp * n_seq

        def pairs(move):
            found = []
            for z in range(self.line):
                for x in range(2):
                    for c in range(2):
                        for y in range(2):
                            tz, tx, tc, ty = move(z, x, c, y)
                            found.append(
                                (((z * 2 + x) * 2 + c) * 2 + y, ((tz * 2 + tx) * 2 + tc) * 2 + ty)
                            )
            return found

        self.sibling = pairs(lambda z, x, c, y: (z, x, 1 - c, y))
        self.long = pairs(lambda z, x, c, y: (z, 1 - x, c, y) if c == 0 else (z, x, c, 1 - y))
        self.short = pairs(lambda z, x, c, y: (z, 1 - x, c, y) if c == 1 else (z, x, c, 1 - y))
        self.ahead = [
            pairs(lambda z, x, c, y, k=k: ((z + k) % self.line, x, c, y)) for k in range(self.line)
        ]

    def natural_rows(self):
        dp = lax.axis_index("dp")
        y = lax.axis_index("seq")
        z, x, c = dp // 4, (dp // 2) % 2, dp % 2
        place = jnp.arange(D, dtype=jnp.int32)
        dc, da, db = place // HALF, (place // (2 * QUARTER)) % 2, (place // QUARTER) % 2
        dz, inner = (place % QUARTER) // self.rows, place % self.rows
        c_own = c ^ dc
        x_own = x ^ jnp.where(c_own == 0, da, db)
        y_own = y ^ jnp.where(c_own == 0, db, da)
        z_own = (z + dz) % self.line
        return self.rows * (((z_own * 2 + x_own) * 2 + c_own) * 2 + y_own) + inner


def send(array, pairs):
    return lax.ppermute(array, BOTH, pairs)


def line_parts(places, shard):
    return [shard] + [send(shard, places.ahead[-k % places.line]) for k in range(1, places.line)]


def stack_kernel(count, *refs):
    ins, (out, scr) = refs[:count], refs[count:]
    rows = ins[0].shape[1]
    for k, ref in enumerate(ins):
        scr[rows * k : rows * (k + 1), :] = ref[0].astype(F32)
    out[0] = scr[...].astype(BF16)


def stacked_rows(parts, after=()):
    pages, rows, width = parts[0].shape
    return pl.pallas_call(
        following(functools.partial(stack_kernel, len(parts)), len(parts), after),
        grid=(pages,),
        in_specs=[pl.BlockSpec((1, rows, width), lambda m: (m, 0, 0))] * len(parts)
        + [ANYWHERE] * len(after),
        out_specs=pl.BlockSpec((1, QUARTER, width), lambda m: (m, 0, 0)),
        out_shape=jax.ShapeDtypeStruct((pages, QUARTER, width), BF16),
        scratch_shapes=[pltpu.VMEM((QUARTER, width), F32)],
        compiler_params=params(32),
        cost_estimate=TINY,
        name="stacked_rows",
    )(*parts, *after)


def neighbours():
    dp, seq = lax.axis_index("dp"), lax.axis_index("seq")
    core = lax.rem(dp, 2)
    first = dp + 2 - 4 * lax.rem(dp // 2, 2)
    sibling = (dp + 1 - 2 * core, seq)
    long = (jnp.where(core == 0, first, dp), jnp.where(core == 0, seq, 1 - seq))
    short = (jnp.where(core == 0, dp, first), jnp.where(core == 0, 1 - seq, seq))
    return sibling, long, short


def greet(devices):
    barrier = pltpu.get_barrier_semaphore()
    for device in devices:
        pl.semaphore_signal(barrier, inc=1, device_id=device, device_id_type=pl.DeviceIdType.MESH)
    pl.semaphore_wait(barrier, len(devices))


def push(src, dst, sems, n, device):
    return pltpu.make_async_remote_copy(
        src_ref=src,
        dst_ref=dst,
        send_sem=sems.at[0, n],
        recv_sem=sems.at[1, n],
        device_id=device,
        device_id_type=pl.DeviceIdType.MESH,
    )


def quarter(ref, k):
    return ref.at[:, pl.ds(QUARTER * k, QUARTER), :]


def spread_kernel(own, out, sems, here_sem):
    sibling, long, short = neighbours()
    greet((sibling, long, short))
    here = pltpu.make_async_copy(own, quarter(out, 0), here_sem)
    moves = [
        push(own, quarter(out, 1), sems, 0, short),
        push(own, quarter(out, 2), sems, 1, long),
        push(own, quarter(out, 4), sems, 2, sibling),
    ]
    here.start()
    for move in moves:
        move.start()
    for k, first in ((1, 3), (2, None), (3, None)):
        moves[{1: 0, 2: 1, 3: 3}[k]].wait_recv()
        if first is not None:
            moves.append(push(quarter(out, 1), quarter(out, 3), sems, 3, long))
            moves[-1].start()
        moves.append(push(quarter(out, k), quarter(out, 4 + k), sems, 3 + k, sibling))
        moves[-1].start()
    here.wait()
    for n, move in enumerate(moves):
        move.wait_send()
        if n not in (0, 1, 3):
            move.wait_recv()


def spread(own, after=()):
    return pl.pallas_call(
        following(spread_kernel, 1, after),
        in_specs=[ANYWHERE] * (1 + len(after)),
        out_specs=ANYWHERE,
        out_shape=jax.ShapeDtypeStruct((1, D, own.shape[2]), BF16),
        scratch_shapes=[pltpu.SemaphoreType.DMA((2, 7)), pltpu.SemaphoreType.DMA],
        compiler_params=params(60, collective_id=8, has_side_effects=True),
        cost_estimate=TINY,
        name="spread",
    )(own, *after)


def fold_kernel(count, *refs):
    total = refs[0][...].astype(F32)
    for ref in refs[1:count]:
        total = total + ref[...].astype(F32)
    refs[count][...] = total.astype(BF16)


def fold(terms, rows, after=()):
    pages, _, width = terms[0][0].shape

    def spec(block):
        return pl.BlockSpec((1, rows, width), lambda m: (m, block, 0))

    return pl.pallas_call(
        following(functools.partial(fold_kernel, len(terms)), len(terms), after),
        grid=(pages,),
        in_specs=[spec(block) for _, block in terms] + [ANYWHERE] * len(after),
        out_specs=spec(0),
        out_shape=jax.ShapeDtypeStruct((pages, rows, width), BF16),
        compiler_params=params(32),
        cost_estimate=TINY,
        name="fold",
    )(*[array for array, _ in terms], *after)


def share_kernel(count, rows, *refs):
    scr = refs[-1]
    outs = refs[count:-1]
    total = refs[0][0].astype(F32)
    for ref in refs[1:count]:
        total = total + ref[0].astype(F32)
    scr[...] = total
    for k, ref in enumerate(outs):
        ref[0] = scr[rows * k : rows * (k + 1), :].astype(ref.dtype)


def share(terms, rows, line, after=()):
    pages, _, width = terms[0].shape
    part = pl.BlockSpec((1, rows, width), lambda m: (m, 0, 0))
    return pl.pallas_call(
        following(functools.partial(share_kernel, len(terms), rows), len(terms), after),
        grid=(pages,),
        in_specs=[pl.BlockSpec((1, QUARTER, width), lambda m: (m, 0, 0))] * len(terms)
        + [ANYWHERE] * len(after),
        out_specs=[part] * line,
        out_shape=[
            jax.ShapeDtypeStruct((pages, rows, width), F32 if k == 0 else BF16) for k in range(line)
        ],
        scratch_shapes=[pltpu.VMEM((QUARTER, width), F32)],
        compiler_params=params(32),
        cost_estimate=TINY,
        name="share",
    )(*terms, *after)


class Reduce:
    def __init__(self, places, terms, passed=None):
        self.places, self.terms, self.passed = places, terms, passed

    def second_step(self, after=()):
        operand = self.passed
        if operand is None:
            operand = fold([(t, 1) for t in self.terms], 2 * QUARTER, after)
        self.terms = self.terms + [send(operand, self.places.long)]
        return operand

    def third_step(self, after=()):
        operand = fold([(t, 1) for t in self.terms], QUARTER, after)
        self.terms = self.terms + [send(operand, self.places.short)]
        return operand

    def last_step(self, after=()):
        mine, *parts = share(self.terms, self.places.rows, self.places.line, after)
        self.parts = [mine] + [
            send(part, self.places.ahead[k + 1]) for k, part in enumerate(parts)
        ]
        return mine


def round_kernel(spans, *refs):
    ins, out = refs[:-1], refs[-1]
    at = [0] * out.shape[0]
    for page, which, offset, width in spans:
        out[page, :, at[page] : at[page] + width] = ins[which][:, offset : offset + width].astype(BF16)
        at[page] += width


def rounded(parts, spans, after=()):
    rows, pages = parts[0].shape[0], 1 + max(page for page, _, _, _ in spans)
    width = sum(width for page, _, _, width in spans if page == 0)
    return pl.pallas_call(
        following(functools.partial(round_kernel, spans), len(parts), after),
        in_specs=[pl.BlockSpec(memory_space=pltpu.VMEM)] * len(parts) + [ANYWHERE] * len(after),
        out_specs=pl.BlockSpec(memory_space=pltpu.VMEM),
        out_shape=jax.ShapeDtypeStruct((pages, rows, width), BF16),
        compiler_params=params(32),
        cost_estimate=TINY,
        name="rounded",
    )(*parts, *after)


def swap_halves(tile, low_half):
    return jnp.where(low_half, pltpu.roll(tile, 96, 1), pltpu.roll(tile, 32, 1))


def project_kernel(x_ref, pi_ref, *refs):
    w_ref, gain_ref, bias_ref, cos_ref, sin_ref, xp_ref, nl_ref, q_ref, k_ref, v_ref = refs
    xp = dot_nn(x_ref[...], pi_ref[...])
    inv = lax.rsqrt(jnp.sum(xp * xp, axis=1, keepdims=True) * (1.0 / D) + norm_epsilon)
    nl = (xp * inv * gain_ref[...]).astype(BF16)
    xp_ref[...] = xp.astype(BF16)
    nl_ref[...] = nl
    lin = dot_nn(nl, w_ref[:, :QKV]) + bias_ref[...]
    cos, sin = cos_ref[...], sin_ref[...]
    low = lax.broadcasted_iota(jnp.int32, cos.shape, 1) % HEAD_SIZE < HEAD_SIZE // 2
    for t in range(8):
        piece = lin[:, 128 * t : 128 * (t + 1)]
        turned = (piece * cos + swap_halves(piece, low) * sin).astype(BF16)
        if t < 7:
            q_ref[:, 128 * t : 128 * (t + 1)] = (turned.astype(F32) * 0.125).astype(BF16)
        else:
            k_ref[...] = turned
    v_ref[...] = lin[:, QW + KW :].astype(BF16)


def project(x, pi, weights, gain, bias, cos, sin, after=()):
    rows = x.shape[0]
    width = weights.shape[1]

    def tile(cols):
        return pl.BlockSpec((TOKEN_TILE, cols), lambda t: (t, 0))

    def whole(r, c):
        return pl.BlockSpec((r, c), lambda t: (0, 0))

    shapes = [(D, BF16), (D, BF16), (QW, BF16), (KW, BF16), (KW, BF16)]
    return pl.pallas_call(
        following(project_kernel, 7, after),
        grid=(rows // TOKEN_TILE,),
        in_specs=[tile(D), whole(D, D)]
        + [whole(D, width)]
        + [whole(1, D), whole(1, QKV), tile(128), tile(128)]
        + [ANYWHERE] * len(after),
        out_specs=[tile(c) for c, _ in shapes],
        out_shape=[jax.ShapeDtypeStruct((rows, c), t) for c, t in shapes],
        compiler_params=params(56),
        cost_estimate=TINY,
        name="project",
    )(x, pi, weights, gain, bias, cos, sin, *after)


def padded_heads(recv, own, out):
    lane = lax.broadcasted_iota(jnp.int32, (512, 128), 1)
    for part, ref in enumerate((recv, own)):
        if ref is None:
            continue
        natural = ref[0].astype(F32)
        crossed = pltpu.roll(natural, 64, 1)
        rows = pl.ds(512 * part, 512)
        for s, (_, half, head) in enumerate(HEAD_SETS):
            source = natural if half == head else crossed
            keep = (lane >= 64) if half else (lane < 64)
            out[s, rows, :] = jnp.where(keep, source, 0.0).astype(BF16)


def block_bias(kb, i, begin):
    shape = (128, 128)
    key = kb * 128 + lax.broadcasted_iota(jnp.int32, shape, 1)
    query = 512 + i * 128 + lax.broadcasted_iota(jnp.int32, shape, 0)
    return jnp.where((key >= begin) & (key <= query), 0.0, masked_value)


def stacked(tile_of, pairs):
    return jnp.concatenate([tile_of(p) for p in pairs], axis=0)


def attend_kernel(
    lo_ref, q_ref, kr_ref, ko_ref, vr_ref, vo_ref, ds_ref, o_ref, lse_ref, kp, vp, s_scr, m_scr, l_scr, acc
):
    b, i = pl.program_id(0), pl.program_id(1)

    @pl.when(i == 0)
    def _():
        padded_heads(kr_ref, ko_ref, kp)
        padded_heads(vr_ref, vo_ref, vp)

    lo, hi = lo_ref[b, i], i + 5
    begin = ds_ref[0]
    m_scr[...] = jnp.full(m_scr.shape, masked_value, F32)
    l_scr[...] = jnp.zeros(l_scr.shape, F32)
    acc[...] = jnp.zeros(acc.shape, F32)

    def scores(kb, carry):
        bias = block_bias(kb, i, begin)
        keys = pl.ds(pl.multiple_of(kb * 128, 128), 128)
        for s, (pairs, _, _) in enumerate(HEAD_SETS):
            x = stacked(lambda p: q_ref[0, :, 128 * p : 128 * (p + 1)], pairs)
            raw = dot_nt(x, kp[s, keys, :])
            for n in range(len(pairs)):
                rows = slice(SET_ROWS[s] + 128 * n, SET_ROWS[s] + 128 * (n + 1))
                value = raw[128 * n : 128 * (n + 1)] + bias
                s_scr[kb, rows, :] = value
                m_scr[rows, :] = jnp.maximum(m_scr[rows, :], value)
        return carry

    lax.fori_loop(lo, hi, scores, 0)
    top = jnp.max(m_scr[...], axis=1, keepdims=True)
    m_scr[...] = jnp.broadcast_to(top, m_scr.shape)

    def weigh(kb, carry):
        keys = pl.ds(pl.multiple_of(kb * 128, 128), 128)
        for s, (pairs, _, _) in enumerate(HEAD_SETS):
            rows = slice(SET_ROWS[s], SET_ROWS[s] + 128 * len(pairs))
            p = jnp.exp(s_scr[kb, rows, :] - m_scr[rows, :])
            l_scr[rows, :] += p
            acc[rows, :] += dot_nn(p.astype(BF16), vp[s, keys, :])
        return carry

    lax.fori_loop(lo, hi, weigh, 0)
    total = jnp.sum(l_scr[...], axis=1, keepdims=True)
    lse = m_scr[:, :1] + jnp.log(total)
    share = 1.0 / total
    lane = lax.broadcasted_iota(jnp.int32, (128, 128), 1)
    lanes = jnp.zeros((128, 128), F32)
    outs = [None] * 7
    for s, (pairs, half, _) in enumerate(HEAD_SETS):
        for n, p in enumerate(pairs):
            rows = slice(SET_ROWS[s] + 128 * n, SET_ROWS[s] + 128 * (n + 1))
            part = acc[rows, :] * share[rows]
            outs[p] = part if outs[p] is None else outs[p] + part
            lanes = jnp.where(lane == 2 * p + half, lse[rows], lanes)
    for p in range(7):
        o_ref[0, :, 128 * p : 128 * (p + 1)] = outs[p].astype(BF16)
    lse_ref[0] = lanes


def attend_specs():
    def block(cols):
        return pl.BlockSpec((1, 128, cols), lambda b, i, lo: (b, i, 0))

    def stream(cols):
        return pl.BlockSpec((1, 512, cols), lambda b, i, lo: (b, 0, 0))

    return block, stream


def attend(lo, q, k_recv, k_own, v_recv, v_own, begin, after=()):
    block, stream = attend_specs()
    return pl.pallas_call(
        following(attend_kernel, 7, after),
        grid_spec=pltpu.PrefetchScalarGridSpec(
            num_scalar_prefetch=1,
            grid=(MICRO, 4),
            in_specs=[block(QW)] + [stream(KW)] * 4 + [block(1)] + [ANYWHERE] * len(after),
            out_specs=[block(QW), block(128)],
            scratch_shapes=[
                pltpu.VMEM((4, 1024, 128), BF16),
                pltpu.VMEM((4, 1024, 128), BF16),
                pltpu.VMEM((8, ALL_ROWS, 128), F32),
                pltpu.VMEM((ALL_ROWS, 128), F32),
                pltpu.VMEM((ALL_ROWS, 128), F32),
                pltpu.VMEM((ALL_ROWS, 128), F32),
            ],
        ),
        out_shape=[
            jax.ShapeDtypeStruct((MICRO, 512, QW), BF16),
            jax.ShapeDtypeStruct((MICRO, 512, 128), F32),
        ],
        compiler_params=params(56),
        cost_estimate=TINY,
        name="attend",
    )(lo, q, k_recv, k_own, v_recv, v_own, begin, *after)


def attend_back_kernel(
    lo_ref, q_ref, kr_ref, ko_ref, vr_ref, vo_ref, ds_ref, o_ref, do_ref, lse_ref,
    dq_ref, own_ref, recv_ref, kp, vp, dk, dv, dq_acc,
):
    b, i = pl.program_id(0), pl.program_id(1)

    @pl.when(i == 0)
    def _():
        padded_heads(kr_ref, ko_ref, kp)
        padded_heads(vr_ref, vo_ref, vp)
        dk[...] = jnp.zeros(dk.shape, F32)
        dv[...] = jnp.zeros(dv.shape, F32)

    lo, hi = lo_ref[b, i], i + 5
    begin = ds_ref[0]
    lane = lax.broadcasted_iota(jnp.int32, (128, 128), 1)
    dq_acc[...] = jnp.zeros(dq_acc.shape, F32)
    lse_all = lse_ref[0]
    lse, dots = [], []
    for s, (pairs, half, _) in enumerate(HEAD_SETS):
        for p in pairs:
            cols = slice(128 * p, 128 * (p + 1))
            product = o_ref[0, :, cols].astype(F32) * do_ref[0, :, cols].astype(F32)
            keep = (lane >= 64) if half else (lane < 64)
            dots.append(jnp.sum(jnp.where(keep, product, 0.0), axis=1, keepdims=True))
            head = 2 * p + half
            lse.append(lse_all[:, head : head + 1])

    def one_block(kb, carry):
        bias = block_bias(kb, i, begin)
        keys = pl.ds(pl.multiple_of(kb * 128, 128), 128)
        at = 0
        for s, (pairs, _, _) in enumerate(HEAD_SETS):
            x = stacked(lambda p: q_ref[0, :, 128 * p : 128 * (p + 1)], pairs)
            y = stacked(lambda p: do_ref[0, :, 128 * p : 128 * (p + 1)], pairs)
            raw = dot_nt(x, kp[s, keys, :])
            d_prob = dot_nt(y, vp[s, keys, :])
            probs, d_scores = [], []
            for n in range(len(pairs)):
                rows = slice(128 * n, 128 * (n + 1))
                p = jnp.exp(raw[rows] + bias - lse[at + n])
                probs.append(p.astype(BF16))
                d_scores.append((p * (d_prob[rows] - dots[at + n])).astype(BF16))
            at += len(pairs)
            prob = jnp.concatenate(probs, axis=0)
            d_score = jnp.concatenate(d_scores, axis=0)
            d_query = dot_nn(d_score, kp[s, keys, :])
            for n, p in enumerate(pairs):
                dq_acc[p] += d_query[128 * n : 128 * (n + 1)]
            dk[s, keys, :] += dot_tn(d_score, x)
            dv[s, keys, :] += dot_tn(prob, y)
        return carry

    lax.fori_loop(lo, hi, one_block, 0)
    for p in range(7):
        dq_ref[0, :, 128 * p : 128 * (p + 1)] = (dq_acc[p] * 0.125).astype(BF16)

    @pl.when(i == 3)
    def _():
        wide = lax.broadcasted_iota(jnp.int32, (512, 128), 1) < 64
        for part, ref in enumerate((recv_ref, own_ref)):
            rows = pl.ds(512 * part, 512)
            for n, grads in enumerate((dk, dv)):
                low = grads[0, rows, :] + pltpu.roll(grads[1, rows, :], 64, 1)
                high = grads[2, rows, :] + pltpu.roll(grads[3, rows, :], 64, 1)
                value = jnp.where(wide, low, high)
                ref[0, :, 128 * n : 128 * (n + 1)] = value.astype(ref.dtype)


def attend_back(lo, q, k_recv, k_own, v_recv, v_own, begin, out, d_out, lse, after=()):
    block, stream = attend_specs()
    return pl.pallas_call(
        following(attend_back_kernel, 10, after),
        grid_spec=pltpu.PrefetchScalarGridSpec(
            num_scalar_prefetch=1,
            grid=(MICRO, 4),
            in_specs=[block(QW)]
            + [stream(KW)] * 4
            + [block(1), block(QW), block(QW), block(128)]
            + [ANYWHERE] * len(after),
            out_specs=[block(QW), stream(256), stream(256)],
            scratch_shapes=[
                pltpu.VMEM((4, 1024, 128), BF16),
                pltpu.VMEM((4, 1024, 128), BF16),
                pltpu.VMEM((4, 1024, 128), F32),
                pltpu.VMEM((4, 1024, 128), F32),
                pltpu.VMEM((7, 128, 128), F32),
            ],
        ),
        out_shape=[
            jax.ShapeDtypeStruct((MICRO, 512, QW), BF16),
            jax.ShapeDtypeStruct((MICRO, 512, 256), F32),
            jax.ShapeDtypeStruct((MICRO, 512, 256), BF16),
        ],
        compiler_params=params(56),
        cost_estimate=TINY,
        name="attend_back",
    )(lo, q, k_recv, k_own, v_recv, v_own, begin, out, d_out, lse, *after)


def middle_kernel(att_ref, xp_ref, *refs):
    w_ref, gain_ref, res_ref, n_ref, nt_ref = refs
    residual = xp_ref[...].astype(F32) + dot_nt(att_ref[...], w_ref[:, QKV : QKV + QW])
    inv = lax.rsqrt(jnp.sum(residual * residual, axis=1, keepdims=True) * (1.0 / D) + norm_epsilon)
    normed = residual * inv * gain_ref[...]
    res_ref[...] = residual
    n_ref[...] = normed.astype(BF16)
    nt_ref[...] = normed.T.astype(BF16)


def middle(attended, xp, weights, gain, after=()):
    rows = xp.shape[0]
    width = weights.shape[1]

    def tile(cols):
        return pl.BlockSpec((TOKEN_TILE, cols), lambda t: (t, 0))

    def whole(r, c):
        return pl.BlockSpec((r, c), lambda t: (0, 0))

    return pl.pallas_call(
        following(middle_kernel, 4, after),
        grid=(rows // TOKEN_TILE,),
        in_specs=[tile(QW), tile(D)]
        + [whole(D, width)]
        + [whole(1, D)]
        + [ANYWHERE] * len(after),
        out_specs=[tile(D), tile(D), pl.BlockSpec((D, TOKEN_TILE), lambda t: (0, t))],
        out_shape=[
            jax.ShapeDtypeStruct((rows, D), F32),
            jax.ShapeDtypeStruct((rows, D), BF16),
            jax.ShapeDtypeStruct((D, rows), BF16),
        ],
        compiler_params=params(56),
        cost_estimate=TINY,
        name="middle",
    )(attended, xp, weights, gain, *after)


def middle_back_kernel(res_ref, mlp_ref, dn_ref, cot_ref, att_ref, pi_ref, *refs):
    w_ref, gain_ref, out_ref, dres_ref, datt_ref, own_ref, sib_ref, dgain_ref, g_scr = refs
    t = pl.program_id(0)

    @pl.when(t == 0)
    def _():
        g_scr[...] = jnp.zeros(g_scr.shape, F32)
        dgain_ref[...] = jnp.zeros(dgain_ref.shape, F32)

    residual = res_ref[...]
    inv = lax.rsqrt(jnp.sum(residual * residual, axis=1, keepdims=True) * (1.0 / D) + norm_epsilon)
    out_low = (residual + mlp_ref[...]).astype(BF16)
    out_ref[...] = dot_nt(out_low, pi_ref[...]).astype(BF16)
    d_normed = dn_ref[...]
    hat = residual * inv
    scaled = d_normed * gain_ref[...]
    dgain_ref[...] += jnp.sum(d_normed * hat, axis=0, keepdims=True)
    mean = jnp.sum(scaled * hat, axis=1, keepdims=True) * (1.0 / D)
    d_res = cot_ref[...].astype(F32) + inv * (scaled - hat * mean)
    dres_ref[...] = d_res
    low = d_res.astype(BF16)
    datt_ref[...] = dot_nn(low, w_ref[:, QKV : QKV + QW]).astype(BF16)
    g_scr[...] += dot_tn(low, att_ref[...])

    @pl.when(t == pl.num_programs(0) - 1)
    def _():
        own_ref[...] = g_scr[:HALF].astype(BF16)
        sib_ref[...] = g_scr[HALF:].astype(BF16)


def middle_back(residual, mlp, d_normed, cot, attended, pi, weights, gain, after=()):
    rows = residual.shape[0]
    width = weights.shape[1]

    def tile(cols):
        return pl.BlockSpec((TOKEN_TILE, cols), lambda t: (t, 0))

    def whole(r, c):
        return pl.BlockSpec((r, c), lambda t: (0, 0))

    return pl.pallas_call(
        following(middle_back_kernel, 8, after),
        grid=(rows // TOKEN_TILE,),
        in_specs=[tile(D)] * 4
        + [tile(QW), whole(D, D)]
        + [whole(D, width)]
        + [whole(1, D)]
        + [ANYWHERE] * len(after),
        out_specs=[tile(D), tile(D), tile(QW), whole(HALF, QW), whole(HALF, QW), whole(1, D)],
        out_shape=[
            jax.ShapeDtypeStruct((rows, D), BF16),
            jax.ShapeDtypeStruct((rows, D), F32),
            jax.ShapeDtypeStruct((rows, QW), BF16),
            jax.ShapeDtypeStruct((HALF, QW), BF16),
            jax.ShapeDtypeStruct((HALF, QW), BF16),
            jax.ShapeDtypeStruct((1, D), F32),
        ],
        scratch_shapes=[pltpu.VMEM((D, QW), F32)],
        compiler_params=params(56),
        cost_estimate=TINY,
        name="middle_back",
    )(residual, mlp, d_normed, cot, attended, pi, weights, gain, *after)


def feed_kernel(wide, started, n_pieces, coming, *refs):
    n_in = 4 + (2 if started else 0)
    n_hbm, nt_hbm, cot_hbm, cott_hbm = refs[:4]
    sums_in = refs[4:n_in]
    pieces = refs[n_in : n_in + n_pieces]
    n_in += n_pieces
    if coming:
        line_hbm = refs[n_in]
        n_in += 1
    mlp_hbm, dn_hbm, keep_hbm, pass_hbm, far_hbm = refs[n_in : n_in + 5]
    n_in += 5
    if coming:
        next_hbm = refs[n_in]
        n_in += 1
    (
        n_v, nt_v, cot_v, cott_v, w_v, mlp_v, dn_v, act_v, grad_v, came_v,
        in_sem, w_sem, w_send, w_recv, out_sem, g_sem, g_send, g_recv, next_sem, next_here,
    ) = refs[n_in:]
    rows_all = n_v.shape[0]
    steps = wide // TILE
    span = 512
    parts = rows_all // span
    sibling, long, short = neighbours()
    mesh_id = pl.DeviceIdType.MESH
    share_rows = HALF // n_pieces

    def tile_of(j):
        return pl.ds(pl.multiple_of(j * TILE, TILE), TILE)

    def weight_copy(k, j):
        return pltpu.make_async_copy(
            pieces[k].at[:, :, tile_of(j)],
            w_v.at[:, pl.ds(share_rows * k, share_rows), tile_of(j)],
            w_sem.at[k, j],
        )

    def weight_push(k, j):
        return pltpu.make_async_remote_copy(
            src_ref=pieces[k].at[:, :, tile_of(j)],
            dst_ref=w_v.at[:, pl.ds(HALF + share_rows * k, share_rows), tile_of(j)],
            send_sem=w_send.at[k, j],
            recv_sem=w_recv.at[k, j],
            device_id=sibling,
            device_id_type=mesh_id,
        )

    def gradient_push(j):
        return pltpu.make_async_remote_copy(
            src_ref=grad_v.at[:, pl.ds(HALF, HALF), tile_of(j)],
            dst_ref=came_v.at[:, :, tile_of(j)],
            send_sem=g_send.at[j],
            recv_sem=g_recv.at[j],
            device_id=sibling,
            device_id_type=mesh_id,
        )

    def sum_copies(j):
        return [
            pltpu.make_async_copy(
                grad_v.at[:, pl.ds(2 * QUARTER * h, 2 * QUARTER), tile_of(j)],
                hbm.at[:, :, tile_of(j)],
                g_sem.at[j, h],
            )
            for h, hbm in enumerate((keep_hbm, pass_hbm))
        ]

    def add_sibling(j):
        cols = tile_of(j)
        gradient_push(j).wait_recv()
        for m in range(3):
            total = grad_v[m, :HALF, cols].astype(F32) + came_v[m, :, cols].astype(F32)
            grad_v[m, :HALF, cols] = total.astype(BF16)
        for copy in sum_copies(j):
            copy.start()

    def span_of(part):
        return pl.ds(part * span, span)

    loads = [
        pltpu.make_async_copy(src, dst, in_sem.at[n])
        for n, (src, dst) in enumerate(
            [(n_hbm, n_v), (cot_hbm, cot_v), (nt_hbm, nt_v), (cott_hbm, cott_v)]
            + ([(sums_in[0], mlp_v), (sums_in[1], dn_v)] if started else [])
        )
    ]
    loads[0].start()
    greet((sibling, long, short) if coming else (sibling,))

    def fetch(j, carry):
        for k in range(n_pieces):
            weight_copy(k, j).start()
            weight_push(k, j).start()
        return carry

    fetch(0, 0)
    for copy in loads[1:4]:
        copy.start()
    lax.fori_loop(1, steps, fetch, 0)
    for copy in loads[4:]:
        copy.start()
    if coming:
        at, width = coming
        line = line_hbm.at[:, :, pl.ds(at, width)]
        line_copy = pltpu.make_async_copy(line, quarter(next_hbm, 0), next_here)
        moves = [
            push(line, quarter(next_hbm, 1), next_sem, 0, short),
            push(line, quarter(next_hbm, 2), next_sem, 1, long),
            push(quarter(next_hbm, 1), quarter(next_hbm, 3), next_sem, 2, long),
        ]
        line_copy.start()
        moves[0].start()
        moves[1].start()

    for copy in loads[:4]:
        copy.wait()

    def columns(j, carry):
        for k in range(n_pieces):
            weight_copy(k, j).wait()
            weight_push(k, j).wait_recv()
        cols = tile_of(j)
        for part in range(parts):
            rows = span_of(part)
            normed = n_v[rows, :]
            gate = dot_nn(normed, w_v[0, :, cols])
            up = dot_nn(normed, w_v[1, :, cols])
            d_hidden = dot_nn(cot_v[rows, :], w_v[2, :, cols])
            s = 1.0 / (1.0 + jnp.exp(-gate))
            silu = gate * s
            act_v[2, rows, cols] = (silu * up).astype(BF16)
            act_v[0, rows, cols] = (d_hidden * up * s * (1.0 + gate * (1.0 - s))).astype(BF16)
            act_v[1, rows, cols] = (d_hidden * silu).astype(BF16)
        for m, left in ((2, cott_v), (0, nt_v), (1, nt_v)):
            grad_v[m, :, cols] = dot_nn(left[...], act_v[m, :, cols]).astype(BF16)
        gradient_push(j).start()

        @pl.when(j > 0)
        def _():
            add_sibling(j - 1)

        return carry

    lax.fori_loop(0, steps, columns, 0)
    stores = [pltpu.make_async_copy(w_v.at[:, pl.ds(HALF, HALF), :], far_hbm, out_sem.at[parts, 0])]
    stores[0].start()
    if coming:
        moves[0].wait_recv()
        moves[2].start()
    for copy in loads[4:]:
        copy.wait()
    for part in range(parts):
        rows = span_of(part)
        for k in range(2):
            if k == 0:
                total, ref, hbm = dot_nt(act_v[2, rows, :], w_v[2]), mlp_v, mlp_hbm
            else:
                total = dot_nt(act_v[0, rows, :], w_v[0]) + dot_nt(act_v[1, rows, :], w_v[1])
                ref, hbm = dn_v, dn_hbm
            ref[rows, :] = total + ref[rows, :] if started else total
            if part == 0 and k == 0:
                add_sibling(steps - 1)
            stores.append(
                pltpu.make_async_copy(ref.at[rows, :], hbm.at[rows, :], out_sem.at[part, k])
            )
            stores[-1].start()

    def settle(j, carry):
        for k in range(n_pieces):
            weight_push(k, j).wait_send()
        gradient_push(j).wait_send()
        for copy in sum_copies(j):
            copy.wait()
        return carry

    lax.fori_loop(0, steps, settle, 0)
    for copy in stores:
        copy.wait()
    if coming:
        line_copy.wait()
        moves[0].wait_send()
        moves[1].wait()
        moves[2].wait()


def feed(number, wide, normed, normed_t, cot, cot_t, sums, pieces, line=None, coming=None, after=()):
    rows = normed.shape[0]
    started = sums is not None
    extra = (list(sums) if started else []) + list(pieces) + ([line] if coming else [])
    n_in = 4 + len(extra)
    steps = wide // TILE
    half = jax.ShapeDtypeStruct((3, HALF, wide), BF16)
    two_quarters = jax.ShapeDtypeStruct((3, 2 * QUARTER, wide), BF16)
    return pl.pallas_call(
        following(functools.partial(feed_kernel, wide, started, len(pieces), coming), n_in, after),
        in_specs=[ANYWHERE] * (n_in + len(after)),
        out_specs=[ANYWHERE] * (6 if coming else 5),
        out_shape=[
            jax.ShapeDtypeStruct((rows, D), F32),
            jax.ShapeDtypeStruct((rows, D), F32),
            two_quarters,
            two_quarters,
            half,
        ]
        + ([jax.ShapeDtypeStruct((3, HALF, coming[1]), BF16)] if coming else []),
        scratch_shapes=[
            pltpu.VMEM((rows, D), BF16),
            pltpu.VMEM((D, rows), BF16),
            pltpu.VMEM((rows, D), BF16),
            pltpu.VMEM((D, rows), BF16),
            pltpu.VMEM((3, D, wide), BF16),
            pltpu.VMEM((rows, D), F32),
            pltpu.VMEM((rows, D), F32),
            pltpu.VMEM((3, rows, wide), BF16),
            pltpu.VMEM((3, D, wide), BF16),
            pltpu.VMEM((3, HALF, wide), BF16),
            pltpu.SemaphoreType.DMA((6,)),
            pltpu.SemaphoreType.DMA((len(pieces), steps)),
            pltpu.SemaphoreType.DMA((len(pieces), steps)),
            pltpu.SemaphoreType.DMA((len(pieces), steps)),
            pltpu.SemaphoreType.DMA((3, 2)),
            pltpu.SemaphoreType.DMA((steps, 2)),
            pltpu.SemaphoreType.DMA((steps,)),
            pltpu.SemaphoreType.DMA((steps,)),
            pltpu.SemaphoreType.DMA((2, 3)),
            pltpu.SemaphoreType.DMA,
        ],
        compiler_params=params(56, collective_id=number, has_side_effects=True),
        cost_estimate=TINY,
        name="feed",
    )(normed, normed_t, cot, cot_t, *extra, *after)


def project_back_kernel(dq_ref, own_kv_ref, recv_kv_ref, cos_ref, sin_ref, nl_ref, xp_ref, dres_ref, pi_ref, *refs):
    w_ref, gain_ref, ig_ref, own_ref, sib_ref, dgain_ref, dbias_ref, g_scr = refs
    t = pl.program_id(0)

    @pl.when(t == 0)
    def _():
        g_scr[...] = jnp.zeros(g_scr.shape, F32)
        dgain_ref[...] = jnp.zeros(dgain_ref.shape, F32)
        dbias_ref[...] = jnp.zeros(dbias_ref.shape, F32)

    cos, sin = cos_ref[...], sin_ref[...]
    low = lax.broadcasted_iota(jnp.int32, cos.shape, 1) % HEAD_SIZE < HEAD_SIZE // 2
    parts = []
    dkv = (own_kv_ref[...] + recv_kv_ref[...].astype(F32)).astype(BF16)
    for n in range(8):
        piece = (dq_ref[:, 128 * n : 128 * (n + 1)] if n < 7 else dkv[:, :KW]).astype(F32)
        parts.append((piece * cos - swap_halves(piece, low) * sin).astype(BF16))
    parts.append(dkv[:, KW:])
    d_lin = jnp.concatenate(parts, axis=1)
    dbias_ref[...] += jnp.sum(d_lin.astype(F32), axis=0, keepdims=True)
    d_normed = dot_nt(d_lin, w_ref[:, :QKV])
    xp = xp_ref[...].astype(F32)
    inv = lax.rsqrt(jnp.sum(xp * xp, axis=1, keepdims=True) * (1.0 / D) + norm_epsilon)
    hat = xp * inv
    scaled = d_normed * gain_ref[...]
    dgain_ref[...] += jnp.sum(d_normed * hat, axis=0, keepdims=True)
    mean = jnp.sum(scaled * hat, axis=1, keepdims=True) * (1.0 / D)
    grad = dres_ref[...] + inv * (scaled - hat * mean)
    high = grad.astype(BF16)
    rest = (grad - high.astype(F32)).astype(BF16)
    ig_ref[...] = dot_nt(high, pi_ref[...]) + dot_nt(rest, pi_ref[...])
    g_scr[...] += dot_tn(nl_ref[...], d_lin)

    @pl.when(t == pl.num_programs(0) - 1)
    def _():
        own_ref[...] = g_scr[:HALF].astype(BF16)
        sib_ref[...] = g_scr[HALF:].astype(BF16)


def project_back(dq, own_kv, recv_kv, cos, sin, nl, xp, d_res, pi, weights, gain, after=()):
    rows = xp.shape[0]
    width = weights.shape[1]

    def tile(cols):
        return pl.BlockSpec((TOKEN_TILE, cols), lambda t: (t, 0))

    def whole(r, c):
        return pl.BlockSpec((r, c), lambda t: (0, 0))

    return pl.pallas_call(
        following(project_back_kernel, 11, after),
        grid=(rows // TOKEN_TILE,),
        in_specs=[tile(QW), tile(256), tile(256), tile(128), tile(128), tile(D), tile(D), tile(D)]
        + [whole(D, D)]
        + [whole(D, width)]
        + [whole(1, D)]
        + [ANYWHERE] * len(after),
        out_specs=[tile(D), whole(HALF, QKV), whole(HALF, QKV), whole(1, D), whole(1, QKV)],
        out_shape=[
            jax.ShapeDtypeStruct((rows, D), F32),
            jax.ShapeDtypeStruct((HALF, QKV), BF16),
            jax.ShapeDtypeStruct((HALF, QKV), BF16),
            jax.ShapeDtypeStruct((1, D), F32),
            jax.ShapeDtypeStruct((1, QKV), F32),
        ],
        scratch_shapes=[pltpu.VMEM((D, QKV), F32)],
        compiler_params=params(56),
        cost_estimate=TINY,
        name="project_back",
    )(dq, own_kv, recv_kv, cos, sin, nl, xp, d_res, pi, weights, gain, *after)


def step_of(first_new, second_new):
    return (
        first_new
        / (1.0 - beta_first**STEP)
        / (jnp.sqrt(second_new / (1.0 - beta_second**STEP)) + adam_epsilon)
    )


def split_two(value):
    high = value.astype(BF16)
    return high, (value - high.astype(F32)).astype(BF16)


def product(dot, a, b):
    return dot(a[0], b[0]) + (dot(a[0], b[1]) + dot(a[1], b[0]))


def side_by_side(value):
    return jnp.concatenate([value[BW * t : BW * (t + 1)] for t in range(D // BW)], axis=1)


def one_above_other(value):
    return jnp.concatenate([value[:, BW * t : BW * (t + 1)] for t in range(D // BW)], axis=0)


def adam_kernel(spans, n_arrays, block_ref, grad_ref, pi_ref, first_ref, second_ref, left_ref, right_ref, *refs):
    arrays, at = [], 0
    for count in n_arrays:
        arrays.append(refs[at : at + count])
        at += count
    first_out, second_out, block_out, w_scr, sem = refs[at:]
    block = block_ref[pl.program_id(0)]
    used = block >= 0
    places = []
    for n, pieces in enumerate(arrays):
        for page, (low, high) in enumerate(spans[n]):
            inside = used & (block >= low) & (block < high)
            column = pl.multiple_of((block - low) * BW, BW)
            places.append((inside, pieces, page, column))

    def copies(pieces, page, column):
        found, row = [], 0
        for k, piece in enumerate(pieces):
            count = piece.shape[1]
            found.append(
                pltpu.make_async_copy(
                    piece.at[page, :, pl.ds(column, BW)], w_scr.at[pl.ds(row, count), :], sem.at[k]
                )
            )
            row += count
        return found

    for inside, pieces, page, column in places:

        @pl.when(inside)
        def _(pieces=pieces, page=page, column=column):
            found = copies(pieces, page, column)
            for copy in found:
                copy.start()
            for copy in found:
                copy.wait()

    @pl.when(used)
    def _():
        grad = grad_ref[0]
        left, right = split_two(left_ref[0]), split_two(right_ref[0])
        turned = split_two(side_by_side(dot_nn(grad, right[0]) + dot_nn(grad, right[1])))
        rotated = one_above_other(product(dot_tn, left, turned))
        first_new = beta_first * first_ref[0] + (1.0 - beta_first) * rotated
        second_new = beta_second * second_ref[0] + (1.0 - beta_second) * rotated * rotated
        first_out[0] = first_new
        second_out[0] = second_new
        step = split_two(step_of(first_new, second_new))
        back = split_two(side_by_side(product(dot_nt, step, right)))
        back = one_above_other(product(dot_nn, left, back))
        weights = dot_nn(pi_ref[...], w_scr[...])
        block_out[0] = weights - rate_matrix * (back + weight_decay * weights)

    @pl.when(jnp.logical_not(used))
    def _():
        for ref in (first_out, second_out, block_out):
            ref[...] = jnp.zeros(ref.shape, F32)


def pack_kernel(spots, targets, counts, block_ref, *refs):
    n_in = sum(counts)
    ins, outs, (slots_ref, all_scr) = refs[:n_in], refs[n_in:-2], refs[-2:]
    at = 0
    for count, found in zip(counts, spots):
        for page, (width, target) in enumerate(found):
            total = ins[at][page, :, :width]
            for ref in ins[at + 1 : at + count]:
                total = total + ref[page, :, :width].astype(F32)
            all_scr[:, target : target + width] = total
        at += count
    for ref, start in zip(outs, targets):
        ref[...] = all_scr[:, start : start + ref.shape[1]]

    def one(slot, carry):
        block = jnp.maximum(block_ref[slot], 0)
        column = pl.multiple_of(block * BW, BW)
        slots_ref[slot] = all_scr[:, pl.ds(column, BW)].astype(BF16)
        return carry

    lax.fori_loop(0, slots_ref.shape[0], one, 0)


def packed(slot_block, groups, spots, targets):
    rows = groups[0][0].shape[1]
    vmem = pl.BlockSpec(memory_space=pltpu.VMEM)
    parts = [part for group in groups for part in group]
    total = (130 + 1) * BW
    return pl.pallas_call(
        functools.partial(
            pack_kernel, spots, [start for start, _ in targets], [len(g) for g in groups]
        ),
        in_specs=[pl.BlockSpec(memory_space=pltpu.SMEM)] + [vmem] * len(parts),
        out_specs=[vmem] * (len(targets) + 1),
        out_shape=[jax.ShapeDtypeStruct((rows, width), F32) for _, width in targets]
        + [jax.ShapeDtypeStruct((slot_block.shape[0], rows, BW), BF16)],
        scratch_shapes=[pltpu.VMEM((rows, total), F32)],
        compiler_params=params(48),
        cost_estimate=TINY,
        name="packed",
    )(slot_block, *parts)


def rotated_adam(slot_block, grads, pi, first_moment, second_moment, left, right, arrays, spans):
    capacity = first_moment.shape[0]
    slab = pl.BlockSpec((1, D, BW), lambda s, b: (s, 0, 0))
    basis = pl.BlockSpec((1, BW, BW), lambda s, b: (s, 0, 0))
    return pl.pallas_call(
        functools.partial(adam_kernel, spans, [len(a) for a in arrays]),
        grid_spec=pltpu.PrefetchScalarGridSpec(
            num_scalar_prefetch=1,
            grid=(capacity,),
            in_specs=[slab, pl.BlockSpec((D, D), lambda s, b: (0, 0)), slab, slab, basis, basis]
            + [ANYWHERE] * sum(len(a) for a in arrays),
            out_specs=[slab] * 3,
            scratch_shapes=[pltpu.VMEM((D, BW), BF16), pltpu.SemaphoreType.DMA((8,))],
        ),
        out_shape=[jax.ShapeDtypeStruct((capacity, D, BW), F32)] * 3,
        compiler_params=params(60),
        cost_estimate=TINY,
        name="rotated_adam",
    )(slot_block, grads, pi, first_moment, second_moment, left, right, *[p for a in arrays for p in a])


def vector_adam(vectors, grad_vectors, vector_first, vector_second):
    first_new = beta_first * vector_first + (1.0 - beta_first) * grad_vectors
    second_new = beta_second * vector_second + (1.0 - beta_second) * grad_vectors * grad_vectors
    return (second_new, vectors - rate_vector * step_of(first_new, second_new))


def on_device(
    places,
    inputs,
    cotangent,
    starts,
    query_weight,
    key_weight,
    value_weight,
    out_weight,
    gate_weight,
    up_weight,
    down_weight,
    vectors,
    owner_slot,
    first_moment,
    second_moment,
    basis_left,
    basis_right,
    vector_first,
    vector_second,
):
    n_dev, shard_rows = places.n_dev, places.rows
    here = inputs.shape[2]
    seq_index = lax.axis_index("seq")
    vec_here = vectors.shape[0]

    out_t, down_t = out_weight.T, down_weight.T
    natural = places.natural_rows()
    pi = (jnp.arange(D, dtype=jnp.int32)[:, None] == natural[None, :]).astype(BF16)
    riding = (
        jnp.arange(n_dev, dtype=jnp.int32)[:, None] * shard_rows == natural[None, :]
    ).astype(BF16)
    vector_rows = jnp.pad(vectors.reshape(1, vec_here), ((0, shard_rows - 1), (0, 128 - vec_here)))
    attention_line = stacked_rows(
        line_parts(
            places,
            rounded(
                [query_weight, key_weight, value_weight, out_t, vector_rows],
                [(0, 0, 0, QW), (0, 1, 0, KW), (0, 2, 0, KW), (0, 3, 0, QW), (0, 4, 0, 128)],
            ),
        )
    )
    feed_parts = [gate_weight, up_weight, down_t]

    def shard_of(chunks, after):
        spans = [(m, m, OFFSETS[n], CHUNKS[n]) for n in chunks for m in range(3)]
        return rounded(feed_parts, spans, after=after)

    shard_a = shard_of((0,), (attention_line,))
    attention = spread(attention_line, after=(shard_a,))
    line_a = stacked_rows(line_parts(places, shard_a), after=(attention,))
    shard_b = shard_of((1,), (attention,))
    short_a, long_a = send(line_a, places.short), send(line_a, places.long)
    attention_pages, attention = attention, attention[0]
    riders = attention[:, QKV + QW :]
    vectors_full = dot_nn(riding, riders)[:, :vec_here].reshape(-1)
    gains = jnp.pad(vectors_full[: 2 * D].reshape(2, D), ((0, 6), (0, 0))).astype(BF16)
    gains = dot_nn(gains, pi)
    gain_attn, gain_mlp = gains[0:1], gains[1:2]
    bias = vectors_full[2 * D :].reshape(1, QKV)

    spots = seq_index * here + jnp.arange(here, dtype=jnp.int32)
    own_starts = starts[:, 0]
    before = own_starts[:, None, :] <= spots[None, :, None]
    doc_begin = jnp.max(jnp.where(before, own_starts[:, None, :], 0), axis=2)
    relative = (spots[None, :] - doc_begin).astype(F32).reshape(-1)
    frequency = jnp.power(
        rope_theta, -jnp.arange(0, HEAD_SIZE, 2, dtype=F32) / HEAD_SIZE
    )
    angles = relative[:, None] * frequency[None, :]
    cos, sin = jnp.cos(angles), jnp.sin(angles)
    cos = jnp.concatenate([cos] * 4, axis=1)
    sin = jnp.concatenate([-sin, sin, -sin, sin], axis=1)
    begin = doc_begin + here - seq_index * here
    lo = begin[:, ::128] // 128
    begin = begin[:, :, None]

    x = inputs[:, 0].reshape(-1, D)
    cot = cotangent[:, 0].reshape(-1, D)
    cot_p = dot_nn(cot, pi).astype(BF16)
    cot_t = lax.dot_general(
        pi, cot, (((0,), (1,)), ((), ())), preferred_element_type=F32
    ).astype(BF16)

    xp, nl, q, k, v = project(
        x, pi, attention, gain_attn, bias, cos, sin, after=(line_a, shard_b)
    )
    line_b = stacked_rows(line_parts(places, shard_b), after=(q,))
    far_a = send(short_a, places.long)
    short_b, long_b = send(line_b, places.short), send(line_b, places.long)
    shard_c = shard_of((2, 3), (line_b,))

    forth = [(2 * n, 2 * n + 1) for n in range(n_dev // 2)]
    back = [(2 * n + 1, 2 * n) for n in range(n_dev // 2)]
    kv = send(jnp.concatenate([k, v], axis=1), forth)

    def streams(array):
        return array.reshape(MICRO, here, array.shape[-1])

    heads = (
        lo,
        streams(q),
        streams(kv[:, :KW]),
        streams(k),
        streams(kv[:, KW:]),
        streams(v),
        begin,
    )
    attended, lse = attend(*heads, after=(line_b, short_a, shard_c))
    attended_flat = attended.reshape(-1, QW)
    residual, normed, normed_t = middle(
        attended_flat, xp, attention, gain_mlp, after=(short_b,)
    )
    far_b = send(short_b, places.long)
    line_c = stacked_rows(line_parts(places, shard_c), after=(normed,))

    sums = None
    reductions, feed_pieces = [], []

    def advance(*steps, after=()):
        return tuple(getattr(reductions[n], step)(after) for n, step in steps)

    waits = [
        lambda: (),
        lambda: (),
        lambda: advance((0, "third_step"), after=sums),
        lambda: advance((0, "last_step"), (1, "third_step"), after=sums),
    ]
    pieces = [[line_a, short_a, long_a, far_a], [line_b, short_b, long_b, far_b]]
    at = 0
    for n, (wide, wait) in enumerate(zip(CHUNKS, waits)):
        coming = (at, CHUNKS[n + 2]) if n + 2 < len(CHUNKS) else None
        mlp, d_normed, kept, passed, far, *arrived = feed(
            n, wide, normed, normed_t, cot_p, cot_t, sums, pieces[n], line_c, coming, after=wait()
        )
        sums = (mlp, d_normed)
        feed_pieces.append(list(pieces[n]) + [far])
        if coming:
            pieces.append(arrived)
            at += coming[1]
        reductions.append(Reduce(places, [kept], passed))
        advance((n, "second_step"))

    output, d_res, d_att, own_out, other_out, d_gain_mlp = middle_back(
        residual, sums[0], sums[1], cot_p, attended_flat, pi, attention, gain_mlp,
        after=advance((1, "last_step"), (2, "third_step"), after=sums[:1]),
    )
    reductions.append(Reduce(places, [own_out[None], send(other_out[None], places.sibling)]))
    dq, dkv, dkv_recv = attend_back(
        *heads, attended, streams(d_att), lse,
        after=advance((2, "last_step"), (3, "third_step"), (4, "second_step"), after=(d_res,)),
    )
    dkv_recv = send(dkv_recv, back)
    input_grad, own_in, other_in, d_gain_attn, d_bias = project_back(
        dq.reshape(-1, QW), dkv.reshape(-1, 2 * KW), dkv_recv.reshape(-1, 2 * KW),
        cos, sin, nl, xp, d_res, pi,
        attention, gain_attn,
        after=advance((3, "last_step"), (4, "third_step"), after=(dq,)),
    )

    d_gains = jnp.concatenate([d_gain_attn, d_gain_mlp, jnp.zeros((6, D), F32)], axis=0)
    high, rest = split_two(d_gains)
    d_gains = dot_nt(high, pi) + dot_nt(rest, pi)
    d_vectors = jnp.concatenate([d_gains[0], d_gains[1], d_bias[0]])
    d_vectors = jnp.pad(d_vectors.reshape(n_dev, vec_here), ((0, 0), (0, 128 - vec_here)))
    riders = dot_tn(riding, d_vectors.astype(BF16)).astype(BF16)
    own_in = jnp.concatenate([own_in, riders[:HALF]], axis=1)[None]
    other_in = jnp.concatenate([other_in, riders[HALF:]], axis=1)[None]
    reductions.append(Reduce(places, [own_in, send(other_in, places.sibling)]))
    advance((4, "last_step"), after=(own_in,))
    advance((5, "second_step"), (5, "third_step"), (5, "last_step"))

    capacity = first_moment.shape[0]
    slot_count = n_dev * capacity
    slot_block = (
        jnp.full((slot_count,), -1, jnp.int32)
        .at[owner_slot]
        .set(jnp.arange(owner_slot.shape[0], dtype=jnp.int32))
    )
    spots = [
        [(w, 2048 + m * FF + o) for m in range(3)] for o, w in zip(OFFSETS, CHUNKS)
    ] + [[(QW, QKV)], [(QKV, 0)]]
    groups = [r.parts for r in reductions]
    rider_parts = [part[:, :, QKV:] for part in groups[-1]]
    groups.append(rider_parts)
    spots.append([(BW, 130 * BW)])
    targets = [
        (0, QW), (QW, KW), (QW + KW, KW), (QKV, QW),
        (2048, FF), (2048 + FF, FF), (2048 + 2 * FF, FF), (130 * BW, BW),
    ]
    (
        grad_query, grad_key, grad_value, grad_out_t, grad_gate, grad_up, grad_down_t, rider_sums, slots,
    ) = packed(slot_block, groups, spots, targets)
    grad_vectors = rider_sums[0, :vec_here]
    owned_grads = lax.all_to_all(
        slots,
        BOTH,
        split_axis=0,
        concat_axis=1,
        tiled=True,
    )
    local_block = lax.dynamic_slice_in_dim(
        slot_block, lax.axis_index(BOTH) * capacity, capacity, 0
    )
    spans = [[(0, 16)]]
    for o, w in zip(OFFSETS, CHUNKS):
        first, count = o // BW, w // BW
        spans.append(
            [(16 + 38 * m + first, 16 + 38 * m + first + count) for m in range(3)]
        )
    new_first, new_second, new_blocks = rotated_adam(
        local_block, owned_grads, pi, first_moment, second_moment, basis_left, basis_right,
        [[attention_pages]] + feed_pieces, spans,
    )
    vector_second_new, vector_new = vector_adam(vectors, grad_vectors, vector_first, vector_second)
    return (
        output.reshape(inputs.shape),
        input_grad.reshape(inputs.shape),
        grad_query,
        grad_key,
        grad_value,
        grad_out_t.T,
        grad_gate,
        grad_up,
        grad_down_t.T,
        grad_vectors,
        new_first,
        new_second,
        new_blocks,
        vector_second_new,
        vector_new,
    )


def solution(mesh):
    rows = P(("dp", "seq"), None)
    columns = P(None, ("dp", "seq"))
    tokens = P(None, "dp", "seq", None)
    slots = P(("dp", "seq"), None, None)
    line = P(("dp", "seq"))
    places = Places(mesh.shape["dp"], mesh.shape["seq"])
    return jax.shard_map(
        functools.partial(on_device, places),
        mesh=mesh,
        in_specs=(
            tokens, tokens, P(None, "dp", None), rows, rows, rows, columns, rows, rows, columns,
            line, P(), slots, slots, slots, slots, line, line,
        ),
        out_specs=(
            tokens, tokens, rows, rows, rows, columns, rows, rows, columns, line,
            slots, slots, slots, line, line,
        ),
        check_vma=False,
    )
```

time: 840 us -> 697 us (0.83)
  waiting for transfers between devices: 268 us -> 157 us
  Pallas kernels: 220 us -> 310 us
  blocking collectives: 65.9 us -> 0 us
  other arithmetic: 64.9 us -> 9.73 us
  local copies, waits for them, and re-layouts: 37.7 us -> 74.1 us
  starting transfers between devices: 150 us -> 126 us
  matrix products: 21.5 us -> 7.43 us
    pallas_call x10 -> x35, Pallas kernels: 220 us -> 310 us  [the longest x4 132 us: feed(): pl.pallas_call(following(functools.partial(feed_kernel, wide, started, le...]
    ppermute x88 -> x52, waiting for transfers between devices: 213 us -> 126 us  [send(): return lax.ppermute(array, BOTH, pairs)]
    all_gather x1 -> x0, blocking collectives: 65.9 us -> none  [on_device(): lax.all_gather(jnp.pad(vectors.astype(BF16), (0, 128 - vec_here)).reshape...]
    unnamed x297 -> x211, local copies, waits for them, and re-layouts: 9.56 us -> 58.6 us
    ppermute x88 -> x52, starting transfers between devices: 142 us -> 117 us  [send(): return lax.ppermute(array, BOTH, pairs)]
    all_to_all x2 -> x1, waiting for transfers between devices: 54.4 us -> 30.7 us  [on_device(): lax.all_to_all(slots, BOTH, split_axis=0, concat_axis=1, tiled=True)]
    convert_element_type x15 -> x0, other arithmetic: 16.4 us -> none  [the longest x6 7.19 us: reduce_rows(): (own[2 * q:].astype(f) + first[2 * q:].astype(f)).astype(BF16)]
    concatenate x14 -> x0, other arithmetic: 14.9 us -> none  [the longest x5 5.62 us: gather_pieces(): own = jnp.concatenate(line, axis=0)]
  transfers between devices with their start and end apart: 90 -> 53, of which waited for: 30 -> 20; matrix products, arithmetic and copies ran while one was open for 9% -> 4% of each run, Pallas kernels for 16% -> 29%
where the time goes in v2:
time: 697 us; the launch traced here: 686 us
  Pallas kernels  310 us (44%)
  waiting for transfers between devices  157 us (23%)
  starting transfers between devices  126 us (18%)
  local copies, waits for them, and re-layouts  74.1 us (11%)
  other arithmetic  9.73 us (1%)
  matrix products  7.43 us (1%)
    pallas_call x4, Pallas kernels, feed(): pl.pallas_call(following(functools.partial(feed_kernel, wide, started, le...  132 us
    ppermute x52, waiting for transfers between devices, send(): return lax.ppermute(array, BOTH, pairs)  126 us
    ppermute x52, starting transfers between devices, send(): return lax.ppermute(array, BOTH, pairs)  117 us
    unnamed x211, local copies, waits for them, and re-layouts  58.6 us
    pallas_call x1, Pallas kernels, attend_back(): pl.pallas_call(following(attend_back_kernel, 10, after), grid_spec=pltpu....  31.1 us
    all_to_all x1, waiting for transfers between devices, on_device(): lax.all_to_all(slots, BOTH, split_axis=0, concat_axis=1, tiled=True)  30.7 us
    pallas_call x1, Pallas kernels, spread(): pl.pallas_call(following(spread_kernel, 1, after), in_specs=[ANYWHERE] *...  24.2 us
    pallas_call x1, Pallas kernels, rotated_adam(): pl.pallas_call(functools.partial(adam_kernel, spans, [len(a) for a in arr...  22.9 us
  transfers between devices with their start and end apart: 53, of which 20 were waited for; matrix products, arithmetic and copies ran while one was open for 4% of the time, Pallas kernels for 29%

profile of v2, /device:TPU:0, one launch (start us, length us, event | category | flops | bytes accessed | tf_op | source)
XLA Modules:
  0.0 686.2 jit_solution(545383059516583956)
XLA Ops:
  4.7 5.1 collective-permute-start
  23.5 24.2 %spread.1.refs_4_.refs_3_.refs_0_ = bf16[1,896,2176]{2,1,0:T(8,128)(2,1)} custom-call(bf16[1,112,2176]{2,1,0:T(8,128)(2,1)} %copy-done.37, bf16[3,28,1280]{2,1,0:T(8,128)(2,1)} %copy-done.44), custom_call_target="tpu_custom_call" | custom-call | flops 1 | bytes 1 | tf_op jit(solution)/shard_map/spread/pallas_call | solution.py:212
  60.1 13.3 %collective-permute-done.4.refs_2_ = bf16[3,28,1280]{2,1,0:T(8,128)(2,1)} collective-permute-done((bf16[3,28,1280]{2,1,0:T(8,128)(2,1)S(1)}, bf16[3,28,1280]{2,1,0:T(8,128)(2,1)}, u32[]{:S(2)}, u32[]{:S(2)}) %collective-permute-start.4) | collective-permute-done | bytes 215072 | tf_op jit(solution)/shard_map/ppermute | solution.py:122
  80.3 10.8 %project.1 = (bf16[1024,896]{1,0:T(8,128)(2,1)}, bf16[1024,896]{1,0:T(8,128)(2,1)}, bf16[1024,896]{1,0:T(8,128)(2,1)}, bf16[1024,128]{1,0:T(8,128)(2,1)}, bf16[1024,128]{1,0:T(8,128)(2,1)}) custom-call(bf16[1024,896]{1,0:T(8,128)(2,1)} %bitcast.77, bf16[896,896]{1,0:T(8,128)(2,1)} %fusion.4.refs_1_.refs_5_.refs_8_.pi_ref, bf16[896,2176]{1,0:T(8,128)(2,1)} %bitcast.45, ...), custom_call_target="tpu_custom_call" | custom-call | flops 1 | bytes 1 | tf_op jit(solution)/shard_map/project/pallas_call | solution.py:360
  114.8 12.4 %collective-permute-done.6 = bf16[1024,256]{1,0:T(8,128)(2,1)} collective-permute-done((bf16[1024,256]{1,0:T(8,128)(2,1)}, bf16[1024,256]{1,0:T(8,128)(2,1)}, u32[]{:S(2)}, u32[]{:S(2)}) %collective-permute-start.6) | collective-permute-done | bytes 524320 | tf_op jit(solution)/shard_map/ppermute | solution.py:122
  127.2 11.1 %collective-permute-start.15 = (bf16[3,28,2304]{2,1,0:T(8,128)(2,1)S(1)}, bf16[3,28,2304]{2,1,0:T(8,128)(2,1)S(1)}, u32[]{:S(2)}, u32[]{:S(2)}) collective-permute-start(bf16[3,28,2304]{2,1,0:T(8,128)(2,1)S(1)} %rounded.7.refs_9_.refs_0_), channel_id=1, source_target_pairs={{0,16},{1,17},{2,18},{3,19},{4,20},{5,21},{6,22},{7,23},{8,24},{9,... | collective-permute-start | bytes 1161224 | tf_op jit(solution)/shard_map/ppermute | solution.py:122
  140.9 21.4 %attend.1 = (bf16[2,512,896]{2,1,0:T(8,128)(2,1)}, f32[2,512,128]{2,1,0:T(8,128)}) custom-call(s32[2,4]{1,0:T(2,128)} %and_select_fusion.refs_0_, bf16[2,512,896]{2,1,0:T(8,128)(2,1)} %bitcast.51, bf16[2,512,128]{2,1,0:T(8,128)(2,1)} %bitcast.75, bf16[2,512,128]{2,1,0:T(8,128)(2,1)} %bitcast.69, bf16[2,512,128]{2,1,0:T(8,128)(2,1)} %bitcast.73, ...), custom_call_target="tpu_custom_call" | custom-call | flops 1 | bytes 1 | tf_op jit(solution)/shard_map/attend/pallas_call | solution.py:472
  162.3 8.4 %middle.1 = (f32[1024,896]{1,0:T(8,128)}, bf16[1024,896]{1,0:T(8,128)(2,1)}, bf16[896,1024]{1,0:T(8,128)(2,1)}) custom-call(bf16[1024,896]{1,0:T(8,128)(2,1)} %bitcast.65, bf16[1024,896]{1,0:T(8,128)(2,1)} %get-tuple-element.101.refs_1_.refs_6_, bf16[896,2176]{1,0:T(8,128)(2,1)} %bitcast.46, f32[1,896]{1,0:T(1,128)} %get-tuple-element.248.refs_3_.refs_7_, ...), custom_call_target="tpu_custom_call" | custom-call | flops 1 | bytes 1 | tf_op jit(solution)/shard_map/middle/pallas_call | solution.py:618
  173.8 40.3 %feed.4 = (f32[1024,896]{1,0:T(8,128)}, f32[1024,896]{1,0:T(8,128)}, bf16[3,224,1280]{2,1,0:T(8,128)(2,1)}, bf16[3,224,1280]{2,1,0:T(8,128)(2,1)}, bf16[3,448,12...) custom-call(bf16[1024,896]{1,0:T(8,128)(2,1)} %get-tuple-element.103.refs_4_.refs_0_, ...), custom_call_target="tpu_custom_call" | custom-call | flops 1 | bytes 1 | tf_op jit(solution)/shard_map/feed/pallas_call | solution.py:893
  216.3 29.3 %collective-permute-done.17.refs_8_ = bf16[3,112,1280]{2,1,0:T(8,128)(2,1)S(1)} collective-permute-done((bf16[3,112,1280]{2,1,0:T(8,128)(2,1)S(1)}, bf16[3,112,1280]{2,1,0:T(8,128)(2,1)S(1)}, u32[]{:S(2)}, u32[]{:S(2)}) %collective-permute-start.17) | collective-permute-done | bytes 860192 | tf_op jit(solution)/shard_map/ppermute | solution.py:122
  245.6 9.2 %collective-permute-done.18.refs_9_ = bf16[3,112,1280]{2,1,0:T(8,128)(2,1)S(1)} collective-permute-done((bf16[3,112,1280]{2,1,0:T(8,128)(2,1)}, bf16[3,112,1280]{2,1,0:T(8,128)(2,1)S(1)}, u32[]{:S(2)}, u32[]{:S(2)}) %collective-permute-start.18) | collective-permute-done | bytes 860192 | tf_op jit(solution)/shard_map/ppermute | solution.py:122
  255.7 33.1 %feed.5 = (f32[1024,896]{1,0:T(8,128)}, f32[1024,896]{1,0:T(8,128)}, bf16[3,224,1280]{2,1,0:T(8,128)(2,1)}, bf16[3,224,1280]{2,1,0:T(8,128)(2,1)}, bf16[3,448,12...) custom-call(bf16[1024,896]{1,0:T(8,128)(2,1)} %get-tuple-element.103.refs_4_.refs_0_, ...), custom_call_target="tpu_custom_call" | custom-call | flops 1 | bytes 1 | tf_op jit(solution)/shard_map/feed/pallas_call | solution.py:893
  296.0 31.7 %feed.6 = (f32[1024,896]{1,0:T(8,128)}, f32[1024,896]{1,0:T(8,128)}, bf16[3,224,1280]{2,1,0:T(8,128)(2,1)}, bf16[3,224,1280]{2,1,0:T(8,128)(2,1)}, bf16[3,448,1280]{2,1,0:T(8,128)(2,1)}) custom-call(bf16[1024,896]{1,0:T(8,128)(2,1)} %get-tuple-element.103.refs_4_.refs_0_, bf16[896,1024]{1,0:T(8,128)(2,1)} %get-tuple-element.104.refs_1_, ...), custom_call_target="tpu_custom_call" | custom-call | flops 1 | bytes 1 | tf_op jit(solution)/shard_map/feed/pallas_call | solution.py:893
  338.0 13.2 %collective-permute-done.20.refs_2_ = bf16[3,112,1280]{2,1,0:T(8,128)(2,1)S(1)} collective-permute-done((bf16[3,112,1280]{2,1,0:T(8,128)(2,1)}, bf16[3,112,1280]{2,1,0:T(8,128)(2,1)S(1)}, u32[]{:S(2)}, u32[]{:S(2)}) %collective-permute-start.20) | collective-permute-done | bytes 860192 | tf_op jit(solution)/shard_map/ppermute | solution.py:122
  352.6 26.9 %feed.7 = (f32[1024,896]{1,0:T(8,128)}, f32[1024,896]{1,0:T(8,128)}, bf16[3,224,1024]{2,1,0:T(8,128)(2,1)}, bf16[3,224,1024]{2,1,0:T(8,128)(2,1)}, bf16[3,448,1024]{2,1,0:T(8,128)(2,1)}) custom-call(bf16[1024,896]{1,0:T(8,128)(2,1)} %get-tuple-element.103.refs_4_.refs_0_, bf16[896,1024]{1,0:T(8,128)(2,1)} %get-tuple-element.104.refs_1_, ...), custom_call_target="tpu_custom_call" | custom-call | flops 1 | bytes 1 | tf_op jit(solution)/shard_map/feed/pallas_call | solution.py:893
  390.1 14.8 %middle_back.1 = (bf16[1024,896]{1,0:T(8,128)(2,1)}, f32[1024,896]{1,0:T(8,128)}, bf16[1024,896]{1,0:T(8,128)(2,1)}, bf16[448,896]{1,0:T(8,128)(2,1)}, bf16[448,896]{1,0:T(8,128)(2,1)}, /*index=5*/f32[1,896]{1,0:T(1,128)}) custom-call(f32[1024,896]{1,0:T(8,128)} %get-tuple-element.102.refs_0_, f32[1024,896]{1,0:T(8,128)} %get-tuple-element.118.refs_3_.refs_2_.refs_1_, ...), custom_call_target="tpu_custom_call" | custom-call | flops 1 | bytes 1 | tf_op jit(solution)/shard_map/middle_back/pallas_call | solution.py:677
  416.9 31.1 %attend_back.1 = (bf16[2,512,896]{2,1,0:T(8,128)(2,1)}, f32[2,512,256]{2,1,0:T(8,128)}, bf16[2,512,256]{2,1,0:T(8,128)(2,1)}) custom-call(s32[2,4]{1,0:T(2,128)} %and_select_fusion.refs_0_, bf16[2,512,896]{2,1,0:T(8,128)(2,1)} %bitcast.52, bf16[2,512,128]{2,1,0:T(8,128)(2,1)} %bitcast.76, bf16[2,512,128]{2,1,0:T(8,128)(2,1)} %bitcast.70, ...), custom_call_target="tpu_custom_call" | custom-call | flops 1 | bytes 1 | tf_op jit(solution)/shard_map/attend_back/pallas_call | solution.py:569
  463.1 18.0 %project_back.1 = (f32[1024,896]{1,0:T(8,128)}, bf16[448,1152]{1,0:T(8,128)(2,1)}, bf16[448,1152]{1,0:T(8,128)(2,1)}, f32[1,896]{1,0:T(1,128)}, f32[1,1152]{1,0:T(1,128)}) custom-call(bf16[1024,896]{1,0:T(8,128)(2,1)} %bitcast.50, f32[1024,256]{1,0:T(8,128)} %bitcast.79, bf16[1024,256]{1,0:T(8,128)(2,1)} %bitcast.80, ...), custom_call_target="tpu_custom_call" | custom-call | flops 1 | bytes 1 | tf_op jit(solution)/shard_map/project_back/pallas_call | solution.py:982
  486.4 11.4 %collective-permute-start.46 = (bf16[1,448,1280]{2,1,0:T(8,128)(2,1)S(1)}, bf16[1,448,1280]{2,1,0:T(8,128)(2,1)S(1)}, u32[]{:S(2)}, u32[]{:S(2)}) collective-permute-start(bf16[1,448,1280]{2,1,0:T(8,128)(2,1)S(1)} %maximum_bitcast_fusion.1), channel_id=1, source_target_pairs={{0,2},{1,3},{2,0},{3,1},{4,6},{5,7},{6,4},{7,5},{8,10},{9,11},{10,... | collective-permute-start | bytes 3440648 | tf_op jit(solution)/shard_map/ppermute | solution.py:122
  500.5 5.3 collective-permute-start.30
  505.8 11.6 %collective-permute-start.31 = (bf16[3,28,1280]{2,1,0:T(8,128)(2,1)S(1)}, bf16[3,28,1280]{2,1,0:T(8,128)(2,1)S(1)}, u32[]{:S(2)}, u32[]{:S(2)}) collective-permute-start(bf16[3,28,1280]{2,1,0:T(8,128)(2,1)S(1)} %get-tuple-element.139), channel_id=1, source_target_pairs={{0,16},{1,17},{2,18},{3,19},{4,20},{5,21},{6,22},{7,23},{8,24},{9,... | collective-permute-start | bytes 645128 | tf_op jit(solution)/shard_map/ppermute | solution.py:122
  520.4 4.8 collective-permute-start.34
  525.3 12.3 %collective-permute-done.31.refs_2_ = bf16[3,28,1280]{2,1,0:T(8,128)(2,1)S(1)} collective-permute-done((bf16[3,28,1280]{2,1,0:T(8,128)(2,1)S(1)}, bf16[3,28,1280]{2,1,0:T(8,128)(2,1)S(1)}, u32[]{:S(2)}, u32[]{:S(2)}) %collective-permute-start.31) | collective-permute-done | bytes 215072 | tf_op jit(solution)/shard_map/ppermute | solution.py:122
  537.7 8.0 %collective-permute-start.35 = (bf16[3,28,1280]{2,1,0:T(8,128)(2,1)S(1)}, bf16[3,28,1280]{2,1,0:T(8,128)(2,1)S(1)}, u32[]{:S(2)}, u32[]{:S(2)}) collective-permute-start(bf16[3,28,1280]{2,1,0:T(8,128)(2,1)S(1)} %get-tuple-element.143), channel_id=1, source_target_pairs={{0,24},{1,25},{2,26},{3,27},{4,28},{5,29},{6,30},{7,31},{8,0},{9,1... | collective-permute-start | bytes 645128 | tf_op jit(solution)/shard_map/ppermute | solution.py:122
  548.6 11.5 %collective-permute-done.34.refs_6_ = bf16[3,28,1280]{2,1,0:T(8,128)(2,1)S(1)} collective-permute-done((bf16[3,28,1280]{2,1,0:T(8,128)(2,1)S(1)}, bf16[3,28,1280]{2,1,0:T(8,128)(2,1)S(1)}, u32[]{:S(2)}, u32[]{:S(2)}) %collective-permute-start.34) | collective-permute-done | bytes 215072 | tf_op jit(solution)/shard_map/ppermute | solution.py:122
  561.1 4.9 collective-permute-start.39
  570.7 7.6 %collective-permute-start.51 = (bf16[1,28,1280]{2,1,0:T(8,128)(2,1)S(1)}, bf16[1,28,1280]{2,1,0:T(8,128)(2,1)}, u32[]{:S(2)}, u32[]{:S(2)}) collective-permute-start(bf16[1,28,1280]{2,1,0:T(8,128)(2,1)S(1)} %get-tuple-element.162), channel_id=1, source_target_pairs={{0,24},{1,25},{2,26},{3,27},{4,28},{5,29},{6,30},{7,31},{8,0},{9,1... | collective-permute-start | bytes 215048 | tf_op jit(solution)/shard_map/ppermute | solution.py:122
  598.7 4.9 collective-permute-done.44.refs_18_
  615.0 4.9 packed.1
  619.9 9.6 %all-to-all-start = ((bf16[160,28,128]{2,1,0:T(8,128)(2,1)}), bf16[160,28,128]{2,1,0:T(8,128)(2,1)S(1)}, u32[]{:S(2)}, u32[]{:S(2)}) async-start(bf16[160,28,128]{2,1,0:T(8,128)(2,1)} %get-tuple-element.171), calls=%async_computation | async-start | bytes 2621440 | tf_op jit(solution)/shard_map/all_to_all | solution.py:1353
  630.7 30.7 %all-to-all-done = bf16[160,28,128]{2,1,0:T(8,128)(2,1)S(1)} async-done(((bf16[160,28,128]{2,1,0:T(8,128)(2,1)}), bf16[160,28,128]{2,1,0:T(8,128)(2,1)S(1)}, u32[]{:S(2)}, u32[]{:S(2)}) %all-to-all-start) | async-done | bytes 1146912 | tf_op jit(solution)/shard_map/all_to_all | solution.py:1353
  662.8 22.9 %rotated_adam.1 = (f32[5,896,128]{2,1,0:T(8,128)}, f32[5,896,128]{2,1,0:T(8,128)}, f32[5,896,128]{2,1,0:T(8,128)}) custom-call(s32[5]{0:T(128)} %dynamic_slice.3.block_ref, bf16[5,896,128]{2,1,0:T(8,128)(2,1)} %all_to_all.16.grad_ref, bf16[896,896]{1,0:T(8,128)(2,1)} %fusion.4.refs_1_.refs_5_.refs_8_.pi_ref, f32[5,896,128]{2,1,0:T(8,128)} %first_ref.1, ...), custom_call_target="tpu_custom_call" | custom-call | flops 1 | bytes 1 | tf_op jit(solution)/shard_map/rotated_adam/pallas_call | solution.py:1136
  (369 shorter events, 179.4 us)
Async XLA Ops:
  49.3 24.1 %collective-permute-start.4 = (bf16[3,28,1280]{2,1,0:T(8,128)(2,1)S(1)}, bf16[3,28,1280]{2,1,0:T(8,128)(2,1)}, u32[]{:S(2)}, u32[]{:S(2)}) collective-permute-start(bf16[3,28,1280]{2,1,0:T(8,128)(2,1)S(1)} %copy-done.45), channel_id=1, source_target_pairs={{0,16},{1,17},{2,18},{3,19},{4,20},{5,21},{6,22},{7,23},{8,24},{9,... | collective-permute-start | bytes 645128 | tf_op jit(solution)/shard_map/ppermute | solution.py:122
  50.7 22.7 %collective-permute-start.5 = (bf16[3,28,1280]{2,1,0:T(8,128)(2,1)S(1)}, bf16[3,28,1280]{2,1,0:T(8,128)(2,1)}, u32[]{:S(2)}, u32[]{:S(2)}) collective-permute-start(bf16[3,28,1280]{2,1,0:T(8,128)(2,1)S(1)} %copy-done.45), channel_id=1, source_target_pairs={{0,8},{1,9},{2,10},{3,11},{4,12},{5,13},{6,14},{7,15},{8,16},{9,17... | collective-permute-start | bytes 645128 | tf_op jit(solution)/shard_map/ppermute | solution.py:122
  56.9 34.1 %collective-permute-start.7 = (bf16[3,28,1280]{2,1,0:T(8,128)(2,1)}, bf16[3,28,1280]{2,1,0:T(8,128)(2,1)S(1)}, u32[]{:S(2)}, u32[]{:S(2)}) collective-permute-start(bf16[3,28,1280]{2,1,0:T(8,128)(2,1)} %copy-done.42), channel_id=1, source_target_pairs={{0,24},{1,25},{2,26},{3,27},{4,28},{5,29},{6,30},{7,31},{8,0},{9,1... | collective-permute-start | bytes 645128 | tf_op jit(solution)/shard_map/ppermute | solution.py:122
  58.9 35.2 %collective-permute-start.8 = (bf16[3,28,1280]{2,1,0:T(8,128)(2,1)}, bf16[3,28,1280]{2,1,0:T(8,128)(2,1)S(1)}, u32[]{:S(2)}, u32[]{:S(2)}) collective-permute-start(bf16[3,28,1280]{2,1,0:T(8,128)(2,1)} %copy-done.42), channel_id=1, source_target_pairs={{0,16},{1,17},{2,18},{3,19},{4,20},{5,21},{6,22},{7,23},{8,24},{9,... | collective-permute-start | bytes 645128 | tf_op jit(solution)/shard_map/ppermute | solution.py:122
  59.5 35.2 %collective-permute-start.9 = (bf16[3,28,1280]{2,1,0:T(8,128)(2,1)}, bf16[3,28,1280]{2,1,0:T(8,128)(2,1)S(1)}, u32[]{:S(2)}, u32[]{:S(2)}) collective-permute-start(bf16[3,28,1280]{2,1,0:T(8,128)(2,1)} %copy-done.42), channel_id=1, source_target_pairs={{0,8},{1,9},{2,10},{3,11},{4,12},{5,13},{6,14},{7,15},{8,16},{9,17... | collective-permute-start | bytes 645128 | tf_op jit(solution)/shard_map/ppermute | solution.py:122
  78.5 27.2 %collective-permute-start.10 = (bf16[3,112,1280]{2,1,0:T(8,128)(2,1)}, bf16[3,112,1280]{2,1,0:T(8,128)(2,1)}, u32[]{:S(2)}, u32[]{:S(2)}) collective-permute-start(bf16[3,112,1280]{2,1,0:T(8,128)(2,1)} %stacked_rows.5.refs_7_.refs_4_.refs_1_), channel_id=1, source_target_pairs={{0,1},{1,0},{2,6},{3,7},{4,5},{5,4},{6,2},{7,3},{8,9},{9,8},{10,14... | collective-permute-start | bytes 2580488 | tf_op jit(solution)/shard_map/ppermute | solution.py:122
  98.3 39.9 %collective-permute-start.11 = (bf16[3,112,1280]{2,1,0:T(8,128)(2,1)S(1)}, bf16[3,112,1280]{2,1,0:T(8,128)(2,1)}, u32[]{:S(2)}, u32[]{:S(2)}) collective-permute-start(bf16[3,112,1280]{2,1,0:T(8,128)(2,1)S(1)} %stacked_rows.6.refs_3_.refs_7_.refs_6_), channel_id=1, source_target_pairs={{0,1},{1,0},{2,6},{3,7},{4,5},{5,4},{6,2},{7,3},{8,9},{9,8},{10,14... | collective-permute-start | bytes 2580488 | tf_op jit(solution)/shard_map/ppermute | solution.py:122
  100.0 27.2 %collective-permute-start.6 = (bf16[1024,256]{1,0:T(8,128)(2,1)}, bf16[1024,256]{1,0:T(8,128)(2,1)}, u32[]{:S(2)}, u32[]{:S(2)}) collective-permute-start(bf16[1024,256]{1,0:T(8,128)(2,1)} %pad_maximum_fusion.2), channel_id=1, source_target_pairs={{0,1},{2,3},{4,5},{6,7},{8,9},{10,11},{12,13},{14,15},{16,17},{18,... | collective-permute-start | bytes 1572872 | tf_op jit(solution)/shard_map/ppermute | solution.py:122
  105.2 68.6 %collective-permute-start.12 = (bf16[3,112,1280]{2,1,0:T(8,128)(2,1)}, bf16[3,112,1280]{2,1,0:T(8,128)(2,1)}, u32[]{:S(2)}, u32[]{:S(2)}) collective-permute-start(bf16[3,112,1280]{2,1,0:T(8,128)(2,1)} %stacked_rows.5.refs_7_.refs_4_.refs_1_), channel_id=1, source_target_pairs={{0,4},{1,5},{2,3},{3,2},{4,0},{5,1},{6,7},{7,6},{8,12},{9,13},{10,... | collective-permute-start | bytes 2580488 | tf_op jit(solution)/shard_map/ppermute | solution.py:122
  105.7 68.1 %collective-permute-start.13 = (bf16[3,112,1280]{2,1,0:T(8,128)(2,1)}, bf16[3,112,1280]{2,1,0:T(8,128)(2,1)}, u32[]{:S(2)}, u32[]{:S(2)}) collective-permute-start(bf16[3,112,1280]{2,1,0:T(8,128)(2,1)} %collective-permute-done.10.refs_8_.refs_5_.refs_2_), channel_id=1, source_target_pairs={{0,4},{1,5},{2,3},{3,2},{4,0},{5,1},{6,7},{7,6},{8,12},{9,13},{10,... | collective-permute-start | bytes 2580488 | tf_op jit(solution)/shard_map/ppermute | solution.py:122
  114.7 56.0 %collective-permute-start.14 = (bf16[3,28,2304]{2,1,0:T(8,128)(2,1)S(1)}, bf16[3,28,2304]{2,1,0:T(8,128)(2,1)S(1)}, u32[]{:S(2)}, u32[]{:S(2)}) collective-permute-start(bf16[3,28,2304]{2,1,0:T(8,128)(2,1)S(1)} %rounded.7.refs_9_.refs_0_), channel_id=1, source_target_pairs={{0,24},{1,25},{2,26},{3,27},{4,28},{5,29},{6,30},{7,31},{8,0},{9,1... | collective-permute-start | bytes 1161224 | tf_op jit(solution)/shard_map/ppermute | solution.py:122
  127.2 43.5 %collective-permute-start.15 = (bf16[3,28,2304]{2,1,0:T(8,128)(2,1)S(1)}, bf16[3,28,2304]{2,1,0:T(8,128)(2,1)S(1)}, u32[]{:S(2)}, u32[]{:S(2)}) collective-permute-start(bf16[3,28,2304]{2,1,0:T(8,128)(2,1)S(1)} %rounded.7.refs_9_.refs_0_), channel_id=1, source_target_pairs={{0,16},{1,17},{2,18},{3,19},{4,20},{5,21},{6,22},{7,23},{8,24},{9,... | collective-permute-start | bytes 1161224 | tf_op jit(solution)/shard_map/ppermute | solution.py:122
  138.2 32.5 %collective-permute-start.16 = (bf16[3,28,2304]{2,1,0:T(8,128)(2,1)S(1)}, bf16[3,28,2304]{2,1,0:T(8,128)(2,1)S(1)}, u32[]{:S(2)}, u32[]{:S(2)}) collective-permute-start(bf16[3,28,2304]{2,1,0:T(8,128)(2,1)S(1)} %rounded.7.refs_9_.refs_0_), channel_id=1, source_target_pairs={{0,8},{1,9},{2,10},{3,11},{4,12},{5,13},{6,14},{7,15},{8,16},{9,17... | collective-permute-start | bytes 1161224 | tf_op jit(solution)/shard_map/ppermute | solution.py:122
  214.1 75.7 %collective-permute-start.19 = (bf16[3,224,1280]{2,1,0:T(8,128)(2,1)}, bf16[3,224,1280]{2,1,0:T(8,128)(2,1)S(1)}, u32[]{:S(2)}, u32[]{:S(2)}) collective-permute-start(bf16[3,224,1280]{2,1,0:T(8,128)(2,1)} %get-tuple-element.111), channel_id=1, source_target_pairs={{0,4},{1,5},{2,3},{3,2},{4,0},{5,1},{6,7},{7,6},{8,12},{9,13},{10,... | collective-permute-start | bytes 5160968 | tf_op jit(solution)/shard_map/ppermute | solution.py:122
  214.2 31.4 %collective-permute-start.17 = (bf16[3,112,1280]{2,1,0:T(8,128)(2,1)S(1)}, bf16[3,112,1280]{2,1,0:T(8,128)(2,1)S(1)}, u32[]{:S(2)}, u32[]{:S(2)}) collective-permute-start(bf16[3,112,1280]{2,1,0:T(8,128)(2,1)S(1)} %copy-done.13), channel_id=1, source_target_pairs={{0,4},{1,5},{2,3},{3,2},{4,0},{5,1},{6,7},{7,6},{8,12},{9,13},{10,... | collective-permute-start | bytes 2580488 | tf_op jit(solution)/shard_map/ppermute | solution.py:122
  216.2 38.6 %collective-permute-start.18 = (bf16[3,112,1280]{2,1,0:T(8,128)(2,1)}, bf16[3,112,1280]{2,1,0:T(8,128)(2,1)S(1)}, u32[]{:S(2)}, u32[]{:S(2)}) collective-permute-start(bf16[3,112,1280]{2,1,0:T(8,128)(2,1)} %collective-permute-done.11.refs_4_.refs_7_), channel_id=1, source_target_pairs={{0,4},{1,5},{2,3},{3,2},{4,0},{5,1},{6,7},{7,6},{8,12},{9,13},{10,... | collective-permute-start | bytes 2580488 | tf_op jit(solution)/shard_map/ppermute | solution.py:122
  288.8 40.9 %collective-permute-start.21 = (bf16[3,224,1280]{2,1,0:T(8,128)(2,1)}, bf16[3,224,1280]{2,1,0:T(8,128)(2,1)S(1)}, u32[]{:S(2)}, u32[]{:S(2)}) collective-permute-start(bf16[3,224,1280]{2,1,0:T(8,128)(2,1)} %get-tuple-element.117), channel_id=1, source_target_pairs={{0,4},{1,5},{2,3},{3,2},{4,0},{5,1},{6,7},{7,6},{8,12},{9,13},{10,... | collective-permute-start | bytes 5160968 | tf_op jit(solution)/shard_map/ppermute | solution.py:122
  327.7 52.8 %collective-permute-start.23 = (bf16[3,224,1280]{2,1,0:T(8,128)(2,1)}, bf16[3,224,1280]{2,1,0:T(8,128)(2,1)}, u32[]{:S(2)}, u32[]{:S(2)}) collective-permute-start(bf16[3,224,1280]{2,1,0:T(8,128)(2,1)} %get-tuple-element.122), channel_id=1, source_target_pairs={{0,4},{1,5},{2,3},{3,2},{4,0},{5,1},{6,7},{7,6},{8,12},{9,13},{10,... | collective-permute-start | bytes 5160968 | tf_op jit(solution)/shard_map/ppermute | solution.py:122
  336.7 52.0 %collective-permute-start.22 = (bf16[3,112,1280]{2,1,0:T(8,128)(2,1)S(1)}, bf16[3,112,1280]{2,1,0:T(8,128)(2,1)S(1)}, u32[]{:S(2)}, u32[]{:S(2)}) collective-permute-start(bf16[3,112,1280]{2,1,0:T(8,128)(2,1)S(1)} %fold.9.refs_8_), channel_id=1, source_target_pairs={{0,1},{1,0},{2,6},{3,7},{4,5},{5,4},{6,2},{7,3},{8,9},{9,8},{10,14... | collective-permute-start | bytes 2580488 | tf_op jit(solution)/shard_map/ppermute | solution.py:122
  379.5 26.2 %collective-permute-start.25 = (bf16[3,224,1024]{2,1,0:T(8,128)(2,1)}, bf16[3,224,1024]{2,1,0:T(8,128)(2,1)}, u32[]{:S(2)}, u32[]{:S(2)}) collective-permute-start(bf16[3,224,1024]{2,1,0:T(8,128)(2,1)} %get-tuple-element.129), channel_id=1, source_target_pairs={{0,4},{1,5},{2,3},{3,2},{4,0},{5,1},{6,7},{7,6},{8,12},{9,13},{10,... | collective-permute-start | bytes 4128776 | tf_op jit(solution)/shard_map/ppermute | solution.py:122
  387.7 24.2 %collective-permute-start.24 = (bf16[3,112,1280]{2,1,0:T(8,128)(2,1)}, bf16[3,112,1280]{2,1,0:T(8,128)(2,1)S(1)}, u32[]{:S(2)}, u32[]{:S(2)}) collective-permute-start(bf16[3,112,1280]{2,1,0:T(8,128)(2,1)} %fold.10.refs_9_), channel_id=1, source_target_pairs={{0,1},{1,0},{2,6},{3,7},{4,5},{5,4},{6,2},{7,3},{8,9},{9,8},{10,14... | collective-permute-start | bytes 2580488 | tf_op jit(solution)/shard_map/ppermute | solution.py:122
  410.3 43.1 %collective-permute-start.28 = (bf16[3,112,1024]{2,1,0:T(8,128)(2,1)S(1)}, bf16[3,112,1024]{2,1,0:T(8,128)(2,1)S(1)}, u32[]{:S(2)}, u32[]{:S(2)}) collective-permute-start(bf16[3,112,1024]{2,1,0:T(8,128)(2,1)S(1)} %fold.11.refs_11_), channel_id=1, source_target_pairs={{0,1},{1,0},{2,6},{3,7},{4,5},{5,4},{6,2},{7,3},{8,9},{9,8},{10,14... | collective-permute-start | bytes 2064392 | tf_op jit(solution)/shard_map/ppermute | solution.py:122
  500.5 24.8 %collective-permute-start.30 = (bf16[3,28,1280]{2,1,0:T(8,128)(2,1)S(1)}, bf16[3,28,1280]{2,1,0:T(8,128)(2,1)S(1)}, u32[]{:S(2)}, u32[]{:S(2)}) collective-permute-start(bf16[3,28,1280]{2,1,0:T(8,128)(2,1)S(1)} %get-tuple-element.138), channel_id=1, source_target_pairs={{0,8},{1,9},{2,10},{3,11},{4,12},{5,13},{6,14},{7,15},{8,16},{9,17... | collective-permute-start | bytes 645128 | tf_op jit(solution)/shard_map/ppermute | solution.py:122
  505.8 31.9 %collective-permute-start.31 = (bf16[3,28,1280]{2,1,0:T(8,128)(2,1)S(1)}, bf16[3,28,1280]{2,1,0:T(8,128)(2,1)S(1)}, u32[]{:S(2)}, u32[]{:S(2)}) collective-permute-start(bf16[3,28,1280]{2,1,0:T(8,128)(2,1)S(1)} %get-tuple-element.139), channel_id=1, source_target_pairs={{0,16},{1,17},{2,18},{3,19},{4,20},{5,21},{6,22},{7,23},{8,24},{9,... | collective-permute-start | bytes 645128 | tf_op jit(solution)/shard_map/ppermute | solution.py:122
  517.5 28.2 %collective-permute-start.32 = (bf16[3,28,1280]{2,1,0:T(8,128)(2,1)S(1)}, bf16[3,28,1280]{2,1,0:T(8,128)(2,1)S(1)}, u32[]{:S(2)}, u32[]{:S(2)}) collective-permute-start(bf16[3,28,1280]{2,1,0:T(8,128)(2,1)S(1)} %get-tuple-element.140), channel_id=1, source_target_pairs={{0,24},{1,25},{2,26},{3,27},{4,28},{5,29},{6,30},{7,31},{8,0},{9,1... | collective-permute-start | bytes 645128 | tf_op jit(solution)/shard_map/ppermute | solution.py:122
  520.4 27.1 %collective-permute-start.33 = (bf16[3,28,1280]{2,1,0:T(8,128)(2,1)S(1)}, bf16[3,28,1280]{2,1,0:T(8,128)(2,1)S(1)}, u32[]{:S(2)}, u32[]{:S(2)}) collective-permute-start(bf16[3,28,1280]{2,1,0:T(8,128)(2,1)S(1)} %get-tuple-element.141), channel_id=1, source_target_pairs={{0,8},{1,9},{2,10},{3,11},{4,12},{5,13},{6,14},{7,15},{8,16},{9,17... | collective-permute-start | bytes 645128 | tf_op jit(solution)/shard_map/ppermute | solution.py:122
  520.4 39.7 %collective-permute-start.34 = (bf16[3,28,1280]{2,1,0:T(8,128)(2,1)S(1)}, bf16[3,28,1280]{2,1,0:T(8,128)(2,1)S(1)}, u32[]{:S(2)}, u32[]{:S(2)}) collective-permute-start(bf16[3,28,1280]{2,1,0:T(8,128)(2,1)S(1)} %get-tuple-element.142), channel_id=1, source_target_pairs={{0,16},{1,17},{2,18},{3,19},{4,20},{5,21},{6,22},{7,23},{8,24},{9,... | collective-permute-start | bytes 645128 | tf_op jit(solution)/shard_map/ppermute | solution.py:122
  525.3 35.8 %collective-permute-start.48 = (bf16[1,112,1280]{2,1,0:T(8,128)(2,1)S(1)}, bf16[1,112,1280]{2,1,0:T(8,128)(2,1)S(1)}, u32[]{:S(2)}, u32[]{:S(2)}) collective-permute-start(bf16[1,112,1280]{2,1,0:T(8,128)(2,1)S(1)} %fold.15), channel_id=1, source_target_pairs={{0,1},{1,0},{2,6},{3,7},{4,5},{5,4},{6,2},{7,3},{8,9},{9,8},{10,14... | collective-permute-start | bytes 860168 | tf_op jit(solution)/shard_map/ppermute | solution.py:122
  537.7 23.4 %collective-permute-start.35 = (bf16[3,28,1280]{2,1,0:T(8,128)(2,1)S(1)}, bf16[3,28,1280]{2,1,0:T(8,128)(2,1)S(1)}, u32[]{:S(2)}, u32[]{:S(2)}) collective-permute-start(bf16[3,28,1280]{2,1,0:T(8,128)(2,1)S(1)} %get-tuple-element.143), channel_id=1, source_target_pairs={{0,24},{1,25},{2,26},{3,27},{4,28},{5,29},{6,30},{7,31},{8,0},{9,1... | collective-permute-start | bytes 645128 | tf_op jit(solution)/shard_map/ppermute | solution.py:122
  547.4 23.2 %collective-permute-start.37 = (bf16[3,28,1280]{2,1,0:T(8,128)(2,1)}, bf16[3,28,1280]{2,1,0:T(8,128)(2,1)S(1)}, u32[]{:S(2)}, u32[]{:S(2)}) collective-permute-start(bf16[3,28,1280]{2,1,0:T(8,128)(2,1)} %get-tuple-element.145), channel_id=1, source_target_pairs={{0,16},{1,17},{2,18},{3,19},{4,20},{5,21},{6,22},{7,23},{8,24},{9,... | collective-permute-start | bytes 645128 | tf_op jit(solution)/shard_map/ppermute | solution.py:122
  561.1 22.9 %collective-permute-start.39 = (bf16[3,28,1024]{2,1,0:T(8,128)(2,1)S(1)}, bf16[3,28,1024]{2,1,0:T(8,128)(2,1)S(1)}, u32[]{:S(2)}, u32[]{:S(2)}) collective-permute-start(bf16[3,28,1024]{2,1,0:T(8,128)(2,1)S(1)} %copy-done.93), channel_id=1, source_target_pairs={{0,8},{1,9},{2,10},{3,11},{4,12},{5,13},{6,14},{7,15},{8,16},{9,17... | collective-permute-start | bytes 516104 | tf_op jit(solution)/shard_map/ppermute | solution.py:122
  619.9 41.5 %all-to-all-start = ((bf16[160,28,128]{2,1,0:T(8,128)(2,1)}), bf16[160,28,128]{2,1,0:T(8,128)(2,1)S(1)}, u32[]{:S(2)}, u32[]{:S(2)}) async-start(bf16[160,28,128]{2,1,0:T(8,128)(2,1)} %get-tuple-element.171), calls=%async_computation | async-start | bytes 2621440 | tf_op jit(solution)/shard_map/all_to_all | solution.py:1353
  (126 other events, 1467.1 us)

commit v3 on v2

--- a/solution.py
+++ b/solution.py
@@ -84,6 +84,7 @@
         self.line = n_dp // 4
         self.rows = D // (n_dp * n_seq)
         self.n_dev = n_dp * n_seq
+        self.padded = -(-self.rows // 16) * 16
 
         def pairs(move):
             found = []
@@ -128,9 +129,9 @@
 
 def stack_kernel(count, *refs):
     ins, (out, scr) = refs[:count], refs[count:]
-    rows = ins[0].shape[1]
+    rows = QUARTER // count
     for k, ref in enumerate(ins):
-        scr[rows * k : rows * (k + 1), :] = ref[0].astype(F32)
+        scr[rows * k : rows * (k + 1), :] = ref[0, :rows].astype(F32)
     out[0] = scr[...].astype(BF16)
 
 
@@ -182,9 +183,67 @@
     return ref.at[:, pl.ds(QUARTER * k, QUARTER), :]
 
 
-def spread_kernel(own, out, sems, here_sem):
+def device_of(kind):
+    if isinstance(kind, str):
+        return dict(zip(("sibling", "long", "short"), neighbours()))[kind]
+    ahead, line = kind
+    dp = lax.axis_index("dp")
+    return (lax.rem(dp // 4 + ahead, line) * 4 + lax.rem(dp, 4), lax.axis_index("seq"))
+
+
+def greet_kinds(kinds):
+    found = []
+    for kind in kinds:
+        if kind not in found:
+            found.append(kind)
+    greet([device_of(kind) for kind in found])
+
+
+def carried(kinds, srcs, dsts, sems):
+    return [
+        push(src, dst, sems, n, device_of(kind))
+        for n, (kind, src, dst) in enumerate(zip(kinds, srcs, dsts))
+    ]
+
+
+def carrying(kernel, kinds, n_in, n_out):
+    count = len(kinds)
+
+    def wrapped(*refs):
+        ins, srcs = refs[:n_in], refs[n_in : n_in + count]
+        at = n_in + count
+        outs, dsts = refs[at : at + n_out], refs[at + n_out : at + n_out + count]
+        scratch, sems = refs[at + n_out + count : -1], refs[-1]
+
+        @pl.when(pl.program_id(0) == 0)
+        def _():
+            greet_kinds(kinds)
+            for move in carried(kinds, srcs, dsts, sems):
+                move.start()
+
+        kernel(*ins, *outs, *scratch)
+
+        @pl.when(pl.program_id(0) == pl.num_programs(0) - 1)
+        def _():
+            for move in carried(kinds, srcs, dsts, sems):
+                move.wait()
+
+    return wrapped
+
+
+def like(array):
+    return jax.ShapeDtypeStruct(array.shape, array.dtype)
+
+
+def spread_kernel(kinds, own, *refs):
+    count = len(kinds)
+    srcs, out, dsts, (sems, here_sem, more_sems) = (
+        refs[:count], refs[count], refs[count + 1 : 2 * count + 1], refs[2 * count + 1 :],
+    )
     sibling, long, short = neighbours()
-    greet((sibling, long, short))
+    greet_kinds(("sibling", "long", "short") + tuple(kinds))
+    for move in carried(kinds, srcs, dsts, more_sems):
+        move.start()
     here = pltpu.make_async_copy(own, quarter(out, 0), here_sem)
     moves = [
         push(own, quarter(out, 1), sems, 0, short),
@@ -206,19 +265,26 @@
         move.wait_send()
         if n not in (0, 1, 3):
             move.wait_recv()
-
-
-def spread(own, after=()):
+    for move in carried(kinds, srcs, dsts, more_sems):
+        move.wait()
+
+
+def spread(own, loads):
+    kinds = tuple(kind for kind, _ in loads)
     return pl.pallas_call(
-        following(spread_kernel, 1, after),
-        in_specs=[ANYWHERE] * (1 + len(after)),
-        out_specs=ANYWHERE,
-        out_shape=jax.ShapeDtypeStruct((1, D, own.shape[2]), BF16),
-        scratch_shapes=[pltpu.SemaphoreType.DMA((2, 7)), pltpu.SemaphoreType.DMA],
+        functools.partial(spread_kernel, kinds),
+        in_specs=[ANYWHERE] * (1 + len(loads)),
+        out_specs=[ANYWHERE] * (1 + len(loads)),
+        out_shape=[jax.ShapeDtypeStruct((1, D, own.shape[2]), BF16)] + [like(a) for _, a in loads],
+        scratch_shapes=[
+            pltpu.SemaphoreType.DMA((2, 7)),
+            pltpu.SemaphoreType.DMA,
+            pltpu.SemaphoreType.DMA((2, max(1, len(loads)))),
+        ],
         compiler_params=params(60, collective_id=8, has_side_effects=True),
         cost_estimate=TINY,
         name="spread",
-    )(own, *after)
+    )(own, *[array for _, array in loads])
 
 
 def fold_kernel(count, *refs):
@@ -254,20 +320,23 @@
         total = total + ref[0].astype(F32)
     scr[...] = total
     for k, ref in enumerate(outs):
-        ref[0] = scr[rows * k : rows * (k + 1), :].astype(ref.dtype)
-
-
-def share(terms, rows, line, after=()):
+        ref[0, :rows] = scr[rows * k : rows * (k + 1), :].astype(ref.dtype)
+
+
+def share(terms, rows, padded, line, after=()):
     pages, _, width = terms[0].shape
-    part = pl.BlockSpec((1, rows, width), lambda m: (m, 0, 0))
+    part = [
+        pl.BlockSpec((1, padded if k else rows, width), lambda m: (m, 0, 0)) for k in range(line)
+    ]
     return pl.pallas_call(
         following(functools.partial(share_kernel, len(terms), rows), len(terms), after),
         grid=(pages,),
         in_specs=[pl.BlockSpec((1, QUARTER, width), lambda m: (m, 0, 0))] * len(terms)
         + [ANYWHERE] * len(after),
-        out_specs=[part] * line,
+        out_specs=part,
         out_shape=[
-            jax.ShapeDtypeStruct((pages, rows, width), F32 if k == 0 else BF16) for k in range(line)
+            jax.ShapeDtypeStruct((pages, padded if k else rows, width), BF16 if k else F32)
+            for k in range(line)
         ],
         scratch_shapes=[pltpu.VMEM((QUARTER, width), F32)],
         compiler_params=params(32),
@@ -277,45 +346,111 @@
 
 
 class Reduce:
-    def __init__(self, places, terms, passed=None):
-        self.places, self.terms, self.passed = places, terms, passed
-
-    def second_step(self, after=()):
-        operand = self.passed
-        if operand is None:
-            operand = fold([(t, 1) for t in self.terms], 2 * QUARTER, after)
-        self.terms = self.terms + [send(operand, self.places.long)]
-        return operand
-
-    def third_step(self, after=()):
-        operand = fold([(t, 1) for t in self.terms], QUARTER, after)
-        self.terms = self.terms + [send(operand, self.places.short)]
-        return operand
-
-    def last_step(self, after=()):
-        mine, *parts = share(self.terms, self.places.rows, self.places.line, after)
-        self.parts = [mine] + [
-            send(part, self.places.ahead[k + 1]) for k, part in enumerate(parts)
-        ]
-        return mine
+    def __init__(self, places, kept, passed):
+        self.places, self.terms = places, [kept]
+        self.next = [("long", passed)]
+
+    def fold(self, arrived, after):
+        self.terms.append(arrived[0])
+        self.next = [("short", fold([(t, 1) for t in self.terms], QUARTER, after))]
+
+    def share(self, arrived, after):
+        self.terms.append(arrived[0])
+        line = self.places.line
+        mine, *parts = share(self.terms, self.places.rows, self.places.padded, line, after)
+        self.parts = [mine]
+        self.next = [((k + 1, line), part) for k, part in enumerate(parts)]
+
+    def end(self, arrived):
+        self.parts += list(arrived)
+
+
+def tail_kernel(line, rows, load_kinds, own, other, *refs):
+    count = len(load_kinds)
+    srcs, out, dsts = refs[:count], refs[count], refs[count + 1 : 2 * count + 1]
+    came, half, came_half, quart, came_quart, keep, parts, came_parts, sems, load_sems = refs[
+        2 * count + 1 :
+    ]
+    kinds = ["sibling", "long", "short"] + [(k, line) for k in range(1, line)]
+    greet_kinds(kinds)
+    for move in carried(load_kinds, srcs, dsts, load_sems):
+        move.start()
+    first = push(other, came, sems, 0, device_of("sibling"))
+    first.start()
+    first.wait_recv()
+    two = 2 * QUARTER
+    half[...] = (own[two:].astype(F32) + came[two:].astype(F32)).astype(BF16)
+    second = push(half, came_half, sems, 1, device_of("long"))
+    second.start()
+    keep[...] = own[:two].astype(F32) + came[:two].astype(F32)
+    second.wait_recv()
+    quart[...] = (keep[QUARTER:] + came_half[QUARTER:].astype(F32)).astype(BF16)
+    third = push(quart, came_quart, sems, 2, device_of("short"))
+    third.start()
+    keep[:QUARTER] = keep[:QUARTER] + came_half[:QUARTER].astype(F32)
+    third.wait_recv()
+    keep[:QUARTER] = keep[:QUARTER] + came_quart[...].astype(F32)
+    moves = [first, second, third]
+    for k in range(1, line):
+        parts[k - 1, :rows] = keep[rows * k : rows * (k + 1), :].astype(BF16)
+        moves.append(
+            push(parts.at[k - 1], came_parts.at[k - 1], sems, 2 + k, device_of((k, line)))
+        )
+        moves[-1].start()
+    total = keep[:rows]
+    for k in range(1, line):
+        moves[2 + k].wait_recv()
+        total = total + came_parts[k - 1, :rows].astype(F32)
+    out[0] = total
+    for move in moves:
+        move.wait_send()
+    for move in carried(load_kinds, srcs, dsts, load_sems):
+        move.wait()
+
+
+def reduce_tail(places, own, other, loads):
+    width, line, padded = own.shape[1], places.line, places.padded
+    vmem = pl.BlockSpec(memory_space=pltpu.VMEM)
+    return pl.pallas_call(
+        functools.partial(tail_kernel, line, places.rows, tuple(kind for kind, _ in loads)),
+        in_specs=[vmem, vmem] + [ANYWHERE] * len(loads),
+        out_specs=[vmem] + [ANYWHERE] * len(loads),
+        out_shape=[jax.ShapeDtypeStruct((1, places.rows, width), F32)] + [like(a) for _, a in loads],
+        scratch_shapes=[
+            pltpu.VMEM((HALF, width), BF16),
+            pltpu.VMEM((2 * QUARTER, width), BF16),
+            pltpu.VMEM((2 * QUARTER, width), BF16),
+            pltpu.VMEM((QUARTER, width), BF16),
+            pltpu.VMEM((QUARTER, width), BF16),
+            pltpu.VMEM((2 * QUARTER, width), F32),
+            pltpu.VMEM((line - 1, padded, width), BF16),
+            pltpu.VMEM((line - 1, padded, width), BF16),
+            pltpu.SemaphoreType.DMA((2, 2 + line)),
+            pltpu.SemaphoreType.DMA((2, max(1, len(loads)))),
+        ],
+        compiler_params=params(56, collective_id=11, has_side_effects=True),
+        cost_estimate=TINY,
+        name="reduce_tail",
+    )(own, other, *[array for _, array in loads])
 
 
 def round_kernel(spans, *refs):
     ins, out = refs[:-1], refs[-1]
     at = [0] * out.shape[0]
     for page, which, offset, width in spans:
-        out[page, :, at[page] : at[page] + width] = ins[which][:, offset : offset + width].astype(BF16)
+        piece = ins[which][:, offset : offset + width]
+        out[page, : piece.shape[0], at[page] : at[page] + width] = piece.astype(BF16)
         at[page] += width
 
 
-def rounded(parts, spans, after=()):
-    rows, pages = parts[0].shape[0], 1 + max(page for page, _, _, _ in spans)
+def rounded(parts, padded, spans, after=()):
+    pages = 1 + max(page for page, _, _, _ in spans)
     width = sum(width for page, _, _, width in spans if page == 0)
     return pl.pallas_call(
         following(functools.partial(round_kernel, spans), len(parts), after),
         in_specs=[pl.BlockSpec(memory_space=pltpu.VMEM)] * len(parts) + [ANYWHERE] * len(after),
         out_specs=pl.BlockSpec(memory_space=pltpu.VMEM),
-        out_shape=jax.ShapeDtypeStruct((pages, rows, width), BF16),
+        out_shape=jax.ShapeDtypeStruct((pages, padded, width), BF16),
         compiler_params=params(32),
         cost_estimate=TINY,
         name="rounded",
@@ -664,7 +799,7 @@
         sib_ref[...] = g_scr[HALF:].astype(BF16)
 
 
-def middle_back(residual, mlp, d_normed, cot, attended, pi, weights, gain, after=()):
+def middle_back(residual, mlp, d_normed, cot, attended, pi, weights, gain, loads):
     rows = residual.shape[0]
     width = weights.shape[1]
 
@@ -675,14 +810,15 @@
         return pl.BlockSpec((r, c), lambda t: (0, 0))
 
     return pl.pallas_call(
-        following(middle_back_kernel, 8, after),
+        carrying(middle_back_kernel, tuple(kind for kind, _ in loads), 8, 6),
         grid=(rows // TOKEN_TILE,),
         in_specs=[tile(D)] * 4
         + [tile(QW), whole(D, D)]
         + [whole(D, width)]
         + [whole(1, D)]
-        + [ANYWHERE] * len(after),
-        out_specs=[tile(D), tile(D), tile(QW), whole(HALF, QW), whole(HALF, QW), whole(1, D)],
+        + [ANYWHERE] * len(loads),
+        out_specs=[tile(D), tile(D), tile(QW), whole(HALF, QW), whole(HALF, QW), whole(1, D)]
+        + [ANYWHERE] * len(loads),
         out_shape=[
             jax.ShapeDtypeStruct((rows, D), BF16),
             jax.ShapeDtypeStruct((rows, D), F32),
@@ -690,15 +826,16 @@
             jax.ShapeDtypeStruct((HALF, QW), BF16),
             jax.ShapeDtypeStruct((HALF, QW), BF16),
             jax.ShapeDtypeStruct((1, D), F32),
-        ],
-        scratch_shapes=[pltpu.VMEM((D, QW), F32)],
-        compiler_params=params(56),
+        ]
+        + [like(array) for _, array in loads],
+        scratch_shapes=[pltpu.VMEM((D, QW), F32), pltpu.SemaphoreType.DMA((2, len(loads)))],
+        compiler_params=params(56, collective_id=9, has_side_effects=True),
         cost_estimate=TINY,
         name="middle_back",
-    )(residual, mlp, d_normed, cot, attended, pi, weights, gain, *after)
-
-
-def feed_kernel(wide, started, n_pieces, coming, *refs):
+    )(residual, mlp, d_normed, cot, attended, pi, weights, gain, *[array for _, array in loads])
+
+
+def feed_kernel(wide, started, n_pieces, coming, kinds, *refs):
     n_in = 4 + (2 if started else 0)
     n_hbm, nt_hbm, cot_hbm, cott_hbm = refs[:4]
     sums_in = refs[4:n_in]
@@ -707,14 +844,19 @@
     if coming:
         line_hbm = refs[n_in]
         n_in += 1
+    srcs = refs[n_in : n_in + len(kinds)]
+    n_in += len(kinds)
     mlp_hbm, dn_hbm, keep_hbm, pass_hbm, far_hbm = refs[n_in : n_in + 5]
     n_in += 5
     if coming:
         next_hbm = refs[n_in]
         n_in += 1
+    dsts = refs[n_in : n_in + len(kinds)]
+    n_in += len(kinds)
     (
         n_v, nt_v, cot_v, cott_v, w_v, mlp_v, dn_v, act_v, grad_v, came_v,
         in_sem, w_sem, w_send, w_recv, out_sem, g_sem, g_send, g_recv, next_sem, next_here,
+        carry_sem,
     ) = refs[n_in:]
     rows_all = n_v.shape[0]
     steps = wide // TILE
@@ -784,7 +926,7 @@
         )
     ]
     loads[0].start()
-    greet((sibling, long, short) if coming else (sibling,))
+    greet_kinds(("sibling",) + (("long", "short") if coming else ()) + kinds)
 
     def fetch(j, carry):
         for k in range(n_pieces):
@@ -810,6 +952,9 @@
         line_copy.start()
         moves[0].start()
         moves[1].start()
+
+    for move in carried(kinds, srcs, dsts, carry_sem):
+        move.start()
 
     for copy in loads[:4]:
         copy.wait()
@@ -880,20 +1025,24 @@
         moves[0].wait_send()
         moves[1].wait()
         moves[2].wait()
-
-
-def feed(number, wide, normed, normed_t, cot, cot_t, sums, pieces, line=None, coming=None, after=()):
+    for move in carried(kinds, srcs, dsts, carry_sem):
+        move.wait()
+
+
+def feed(number, wide, normed, normed_t, cot, cot_t, sums, pieces, line, coming, loads):
     rows = normed.shape[0]
     started = sums is not None
+    kinds = tuple(kind for kind, _ in loads)
     extra = (list(sums) if started else []) + list(pieces) + ([line] if coming else [])
+    extra += [array for _, array in loads]
     n_in = 4 + len(extra)
     steps = wide // TILE
     half = jax.ShapeDtypeStruct((3, HALF, wide), BF16)
     two_quarters = jax.ShapeDtypeStruct((3, 2 * QUARTER, wide), BF16)
     return pl.pallas_call(
-        following(functools.partial(feed_kernel, wide, started, len(pieces), coming), n_in, after),
-        in_specs=[ANYWHERE] * (n_in + len(after)),
-        out_specs=[ANYWHERE] * (6 if coming else 5),
+        functools.partial(feed_kernel, wide, started, len(pieces), coming, kinds),
+        in_specs=[ANYWHERE] * n_in,
+        out_specs=[ANYWHERE] * ((6 if coming else 5) + len(loads)),
         out_shape=[
             jax.ShapeDtypeStruct((rows, D), F32),
             jax.ShapeDtypeStruct((rows, D), F32),
@@ -901,7 +1050,8 @@
             two_quarters,
             half,
         ]
-        + ([jax.ShapeDtypeStruct((3, HALF, coming[1]), BF16)] if coming else []),
+        + ([jax.ShapeDtypeStruct((3, HALF, coming[1]), BF16)] if coming else [])
+        + [like(array) for _, array in loads],
         scratch_shapes=[
             pltpu.VMEM((rows, D), BF16),
             pltpu.VMEM((D, rows), BF16),
@@ -923,11 +1073,12 @@
             pltpu.SemaphoreType.DMA((steps,)),
             pltpu.SemaphoreType.DMA((2, 3)),
             pltpu.SemaphoreType.DMA,
+            pltpu.SemaphoreType.DMA((2, max(1, len(loads)))),
         ],
         compiler_params=params(56, collective_id=number, has_side_effects=True),
         cost_estimate=TINY,
         name="feed",
-    )(normed, normed_t, cot, cot_t, *extra, *after)
+    )(normed, normed_t, cot, cot_t, *extra)
 
 
 def project_back_kernel(dq_ref, own_kv_ref, recv_kv_ref, cos_ref, sin_ref, nl_ref, xp_ref, dres_ref, pi_ref, *refs):
@@ -969,7 +1120,7 @@
         sib_ref[...] = g_scr[HALF:].astype(BF16)
 
 
-def project_back(dq, own_kv, recv_kv, cos, sin, nl, xp, d_res, pi, weights, gain, after=()):
+def project_back(dq, own_kv, recv_kv, cos, sin, nl, xp, d_res, pi, weights, gain, loads):
     rows = xp.shape[0]
     width = weights.shape[1]
 
@@ -980,26 +1131,29 @@
         return pl.BlockSpec((r, c), lambda t: (0, 0))
 
     return pl.pallas_call(
-        following(project_back_kernel, 11, after),
+        carrying(project_back_kernel, tuple(kind for kind, _ in loads), 11, 5),
         grid=(rows // TOKEN_TILE,),
         in_specs=[tile(QW), tile(256), tile(256), tile(128), tile(128), tile(D), tile(D), tile(D)]
         + [whole(D, D)]
         + [whole(D, width)]
         + [whole(1, D)]
-        + [ANYWHERE] * len(after),
-        out_specs=[tile(D), whole(HALF, QKV), whole(HALF, QKV), whole(1, D), whole(1, QKV)],
+        + [ANYWHERE] * len(loads),
+        out_specs=[tile(D), whole(HALF, QKV), whole(HALF, QKV), whole(1, D), whole(1, QKV)]
+        + [ANYWHERE] * len(loads),
         out_shape=[
             jax.ShapeDtypeStruct((rows, D), F32),
             jax.ShapeDtypeStruct((HALF, QKV), BF16),
             jax.ShapeDtypeStruct((HALF, QKV), BF16),
             jax.ShapeDtypeStruct((1, D), F32),
             jax.ShapeDtypeStruct((1, QKV), F32),
-        ],
-        scratch_shapes=[pltpu.VMEM((D, QKV), F32)],
-        compiler_params=params(56),
+        ]
+        + [like(array) for _, array in loads],
+        scratch_shapes=[pltpu.VMEM((D, QKV), F32), pltpu.SemaphoreType.DMA((2, len(loads)))],
+        compiler_params=params(56, collective_id=10, has_side_effects=True),
         cost_estimate=TINY,
         name="project_back",
-    )(dq, own_kv, recv_kv, cos, sin, nl, xp, d_res, pi, weights, gain, *after)
+    )(dq, own_kv, recv_kv, cos, sin, nl, xp, d_res, pi, weights, gain,
+      *[array for _, array in loads])
 
 
 def step_of(first_new, second_new):
@@ -1027,42 +1181,62 @@
     return jnp.concatenate([value[:, BW * t : BW * (t + 1)] for t in range(D // BW)], axis=0)
 
 
-def adam_kernel(spans, n_arrays, block_ref, grad_ref, pi_ref, first_ref, second_ref, left_ref, right_ref, *refs):
+def pick_kernel(spans, counts, block_ref, pi_ref, *refs):
     arrays, at = [], 0
-    for count in n_arrays:
+    for count in counts:
         arrays.append(refs[at : at + count])
         at += count
-    first_out, second_out, block_out, w_scr, sem = refs[at:]
-    block = block_ref[pl.program_id(0)]
-    used = block >= 0
-    places = []
-    for n, pieces in enumerate(arrays):
-        for page, (low, high) in enumerate(spans[n]):
-            inside = used & (block >= low) & (block < high)
-            column = pl.multiple_of((block - low) * BW, BW)
-            places.append((inside, pieces, page, column))
-
-    def copies(pieces, page, column):
-        found, row = [], 0
-        for k, piece in enumerate(pieces):
-            count = piece.shape[1]
-            found.append(
-                pltpu.make_async_copy(
-                    piece.at[page, :, pl.ds(column, BW)], w_scr.at[pl.ds(row, count), :], sem.at[k]
-                )
-            )
-            row += count
-        return found
-
-    for inside, pieces, page, column in places:
-
-        @pl.when(inside)
-        def _(pieces=pieces, page=page, column=column):
-            found = copies(pieces, page, column)
-            for copy in found:
-                copy.start()
-            for copy in found:
-                copy.wait()
+    out_ref, w_scr, sem = refs[at:]
+    slots = out_ref.shape[0]
+
+    def each(slot, act):
+        block = block_ref[slot]
+        for n, pieces in enumerate(arrays):
+            for page, (low, high) in enumerate(spans[n]):
+
+                @pl.when((block >= low) & (block < high))
+                def _(pieces=pieces, page=page, low=low):
+                    column = pl.multiple_of((block - low) * BW, BW)
+                    row = 0
+                    for k, piece in enumerate(pieces):
+                        count = piece.shape[1]
+                        act(
+                            pltpu.make_async_copy(
+                                piece.at[page, :, pl.ds(column, BW)],
+                                w_scr.at[slot, pl.ds(row, count), :],
+                                sem.at[slot, k],
+                            )
+                        )
+                        row += count
+
+    for slot in range(slots):
+        each(slot, lambda copy: copy.start())
+    for slot in range(slots):
+        each(slot, lambda copy: copy.wait())
+        out_ref[slot] = dot_nn(pi_ref[...], w_scr[slot])
+
+
+def picked(slot_block, pi, arrays, spans, after=()):
+    capacity = slot_block.shape[0]
+    vmem = pl.BlockSpec(memory_space=pltpu.VMEM)
+    flat = [p for a in arrays for p in a]
+    return pl.pallas_call(
+        following(
+            functools.partial(pick_kernel, spans, [len(a) for a in arrays]), 2 + len(flat), after
+        ),
+        in_specs=[pl.BlockSpec(memory_space=pltpu.SMEM), vmem]
+        + [ANYWHERE] * (len(flat) + len(after)),
+        out_specs=vmem,
+        out_shape=jax.ShapeDtypeStruct((capacity, D, BW), F32),
+        scratch_shapes=[pltpu.VMEM((capacity, D, BW), BF16), pltpu.SemaphoreType.DMA((capacity, 8))],
+        compiler_params=params(60),
+        cost_estimate=TINY,
+        name="picked",
+    )(slot_block, pi, *flat, *after)
+
+
+def adam_kernel(block_ref, grad_ref, weight_ref, first_ref, second_ref, left_ref, right_ref, first_out, second_out, block_out):
+    used = block_ref[pl.program_id(0)] >= 0
 
     @pl.when(used)
     def _():
@@ -1077,7 +1251,7 @@
         step = split_two(step_of(first_new, second_new))
         back = split_two(side_by_side(product(dot_nt, step, right)))
         back = one_above_other(product(dot_nn, left, back))
-        weights = dot_nn(pi_ref[...], w_scr[...])
+        weights = weight_ref[0]
         block_out[0] = weights - rate_matrix * (back + weight_decay * weights)
 
     @pl.when(jnp.logical_not(used))
@@ -1094,7 +1268,7 @@
         for page, (width, target) in enumerate(found):
             total = ins[at][page, :, :width]
             for ref in ins[at + 1 : at + count]:
-                total = total + ref[page, :, :width].astype(F32)
+                total = total + ref[page, : total.shape[0], :width].astype(F32)
             all_scr[:, target : target + width] = total
         at += count
     for ref, start in zip(outs, targets):
@@ -1129,31 +1303,44 @@
     )(slot_block, *parts)
 
 
-def rotated_adam(slot_block, grads, pi, first_moment, second_moment, left, right, arrays, spans):
+def rotated_adam(slot_block, grads, weights, first_moment, second_moment, left, right):
     capacity = first_moment.shape[0]
     slab = pl.BlockSpec((1, D, BW), lambda s, b: (s, 0, 0))
     basis = pl.BlockSpec((1, BW, BW), lambda s, b: (s, 0, 0))
     return pl.pallas_call(
-        functools.partial(adam_kernel, spans, [len(a) for a in arrays]),
+        adam_kernel,
         grid_spec=pltpu.PrefetchScalarGridSpec(
             num_scalar_prefetch=1,
             grid=(capacity,),
-            in_specs=[slab, pl.BlockSpec((D, D), lambda s, b: (0, 0)), slab, slab, basis, basis]
-            + [ANYWHERE] * sum(len(a) for a in arrays),
+            in_specs=[slab, slab, slab, slab, basis, basis],
             out_specs=[slab] * 3,
-            scratch_shapes=[pltpu.VMEM((D, BW), BF16), pltpu.SemaphoreType.DMA((8,))],
         ),
         out_shape=[jax.ShapeDtypeStruct((capacity, D, BW), F32)] * 3,
-        compiler_params=params(60),
+        compiler_params=params(40),
         cost_estimate=TINY,
         name="rotated_adam",
-    )(slot_block, grads, pi, first_moment, second_moment, left, right, *[p for a in arrays for p in a])
+    )(slot_block, grads, weights, first_moment, second_moment, left, right)
 
 
 def vector_adam(vectors, grad_vectors, vector_first, vector_second):
     first_new = beta_first * vector_first + (1.0 - beta_first) * grad_vectors
     second_new = beta_second * vector_second + (1.0 - beta_second) * grad_vectors * grad_vectors
     return (second_new, vectors - rate_vector * step_of(first_new, second_new))
+
+
+def hand_out(moving, arrived, after=()):
+    at = 0
+    for r in moving:
+        came = arrived[at : at + len(r.next)]
+        at += len(r.next)
+        kind = r.next[0][0]
+        if kind == "long":
+            r.fold(came, after)
+        elif kind == "short":
+            r.share(came, after)
+        else:
+            r.end(came)
+            r.next = []
 
 
 def on_device(
@@ -1194,6 +1381,7 @@
             places,
             rounded(
                 [query_weight, key_weight, value_weight, out_t, vector_rows],
+                places.padded,
                 [(0, 0, 0, QW), (0, 1, 0, KW), (0, 2, 0, KW), (0, 3, 0, QW), (0, 4, 0, 128)],
             ),
         )
@@ -1202,11 +1390,12 @@
 
     def shard_of(chunks, after):
         spans = [(m, m, OFFSETS[n], CHUNKS[n]) for n in chunks for m in range(3)]
-        return rounded(feed_parts, spans, after=after)
-
-    shard_a = shard_of((0,), (attention_line,))
-    attention = spread(attention_line, after=(shard_a,))
-    line_a = stacked_rows(line_parts(places, shard_a), after=(attention,))
+        return rounded(feed_parts, places.padded, spans, after=after)
+
+    shard_a = shard_of((0,), ())
+    backwards = [(-k % places.line, places.line) for k in range(1, places.line)]
+    attention, *arrived = spread(attention_line, [(kind, shard_a) for kind in backwards])
+    line_a = stacked_rows([shard_a] + arrived)
     shard_b = shard_of((1,), (attention,))
     short_a, long_a = send(line_a, places.short), send(line_a, places.long)
     attention_pages, attention = attention, attention[0]
@@ -1275,46 +1464,50 @@
     sums = None
     reductions, feed_pieces = [], []
 
-    def advance(*steps, after=()):
-        return tuple(getattr(reductions[n], step)(after) for n, step in steps)
-
-    waits = [
-        lambda: (),
-        lambda: (),
-        lambda: advance((0, "third_step"), after=sums),
-        lambda: advance((0, "last_step"), (1, "third_step"), after=sums),
-    ]
     pieces = [[line_a, short_a, long_a, far_a], [line_b, short_b, long_b, far_b]]
     at = 0
-    for n, (wide, wait) in enumerate(zip(CHUNKS, waits)):
+    loads = []
+    for n, wide in enumerate(CHUNKS):
         coming = (at, CHUNKS[n + 2]) if n + 2 < len(CHUNKS) else None
+        moving = [r for r in reductions if r.next]
+        loads = [load for r in moving for load in r.next]
         mlp, d_normed, kept, passed, far, *arrived = feed(
-            n, wide, normed, normed_t, cot_p, cot_t, sums, pieces[n], line_c, coming, after=wait()
+            n, wide, normed, normed_t, cot_p, cot_t, sums, pieces[n], line_c, coming, loads
         )
         sums = (mlp, d_normed)
         feed_pieces.append(list(pieces[n]) + [far])
         if coming:
-            pieces.append(arrived)
+            pieces.append([arrived.pop(0)])
             at += coming[1]
-        reductions.append(Reduce(places, [kept], passed))
-        advance((n, "second_step"))
-
-    output, d_res, d_att, own_out, other_out, d_gain_mlp = middle_back(
+        hand_out(moving, arrived)
+        reductions.append(Reduce(places, kept, passed))
+
+    moving = [r for r in reductions if r.next]
+    output, d_res, d_att, own_out, other_out, d_gain_mlp, *arrived = middle_back(
         residual, sums[0], sums[1], cot_p, attended_flat, pi, attention, gain_mlp,
-        after=advance((1, "last_step"), (2, "third_step"), after=sums[:1]),
-    )
-    reductions.append(Reduce(places, [own_out[None], send(other_out[None], places.sibling)]))
+        [load for r in moving for load in r.next],
+    )
+    hand_out(moving, arrived)
+    moving = [r for r in reductions if r.next]
+    along = {"long": places.long, "short": places.short}
+    arrived = [
+        send(array, along[kind] if kind in along else places.ahead[kind[0]])
+        for r in moving
+        for kind, array in r.next
+    ]
     dq, dkv, dkv_recv = attend_back(
         *heads, attended, streams(d_att), lse,
-        after=advance((2, "last_step"), (3, "third_step"), (4, "second_step"), after=(d_res,)),
+        after=tuple(array for r in moving for _, array in r.next),
     )
     dkv_recv = send(dkv_recv, back)
-    input_grad, own_in, other_in, d_gain_attn, d_bias = project_back(
+    hand_out(moving, arrived, (dq,))
+    moving = [r for r in reductions if r.next]
+    input_grad, own_in, other_in, d_gain_attn, d_bias, *arrived = project_back(
         dq.reshape(-1, QW), dkv.reshape(-1, 2 * KW), dkv_recv.reshape(-1, 2 * KW),
-        cos, sin, nl, xp, d_res, pi,
-        attention, gain_attn,
-        after=advance((3, "last_step"), (4, "third_step"), after=(dq,)),
-    )
+        cos, sin, nl, xp, d_res, pi, attention, gain_attn,
+        [load for r in moving for load in r.next],
+    )
+    hand_out(moving, arrived)
 
     d_gains = jnp.concatenate([d_gain_attn, d_gain_mlp, jnp.zeros((6, D), F32)], axis=0)
     high, rest = split_two(d_gains)
@@ -1322,11 +1515,14 @@
     d_vectors = jnp.concatenate([d_gains[0], d_gains[1], d_bias[0]])
     d_vectors = jnp.pad(d_vectors.reshape(n_dev, vec_here), ((0, 0), (0, 128 - vec_here)))
     riders = dot_tn(riding, d_vectors.astype(BF16)).astype(BF16)
-    own_in = jnp.concatenate([own_in, riders[:HALF]], axis=1)[None]
-    other_in = jnp.concatenate([other_in, riders[HALF:]], axis=1)[None]
-    reductions.append(Reduce(places, [own_in, send(other_in, places.sibling)]))
-    advance((4, "last_step"), after=(own_in,))
-    advance((5, "second_step"), (5, "third_step"), (5, "last_step"))
+    moving = [r for r in reductions if r.next]
+    grad_in, *arrived = reduce_tail(
+        places,
+        jnp.concatenate([own_in, riders[:HALF], own_out], axis=1),
+        jnp.concatenate([other_in, riders[HALF:], other_out], axis=1),
+        [load for r in moving for load in r.next],
+    )
+    hand_out(moving, arrived)
 
     capacity = first_moment.shape[0]
     slot_count = n_dev * capacity
@@ -1337,11 +1533,11 @@
     )
     spots = [
         [(w, 2048 + m * FF + o) for m in range(3)] for o, w in zip(OFFSETS, CHUNKS)
-    ] + [[(QW, QKV)], [(QKV, 0)]]
+    ]
     groups = [r.parts for r in reductions]
-    rider_parts = [part[:, :, QKV:] for part in groups[-1]]
-    groups.append(rider_parts)
-    spots.append([(BW, 130 * BW)])
+    for start, width, target in ((0, QKV, 0), (QKV, BW, 130 * BW), (QKV + BW, QW, QKV)):
+        groups.append([grad_in[:, :, start : start + width]])
+        spots.append([(width, target)])
     targets = [
         (0, QW), (QW, KW), (QW + KW, KW), (QKV, QW),
         (2048, FF), (2048 + FF, FF), (2048 + 2 * FF, FF), (130 * BW, BW),
@@ -1366,9 +1562,11 @@
         spans.append(
             [(16 + 38 * m + first, 16 + 38 * m + first + count) for m in range(3)]
         )
+    owned_weights = picked(
+        local_block, pi, [[attention_pages]] + feed_pieces, spans, after=(slots,)
+    )
     new_first, new_second, new_blocks = rotated_adam(
-        local_block, owned_grads, pi, first_moment, second_moment, basis_left, basis_right,
-        [[attention_pages]] + feed_pieces, spans,
+        local_block, owned_grads, owned_weights, first_moment, second_moment, basis_left, basis_right
     )
     vector_second_new, vector_new = vector_adam(vectors, grad_vectors, vector_first, vector_second)
     return (

time: 697 us -> 578 us (0.83)
  waiting for transfers between devices: 157 us -> 56.3 us
  starting transfers between devices: 126 us -> 36.4 us
  Pallas kernels: 310 us -> 393 us
  local copies, waits for them, and re-layouts: 74.1 us -> 61.5 us
    ppermute x52 -> x21, waiting for transfers between devices: 126 us -> 34.2 us  [send(): return lax.ppermute(array, BOTH, pairs)]
    pallas_call x8 -> x10, Pallas kernels: 212 us -> 300 us  [the longest x4 149 us: feed(): pl.pallas_call(functools.partial(feed_kernel, wide, started, len(pieces),...]
    ppermute x52 -> x21, starting transfers between devices: 117 us -> 29.9 us  [send(): return lax.ppermute(array, BOTH, pairs)]
    unnamed x211 -> x171, local copies, waits for them, and re-layouts: 58.6 us -> 42.4 us
    all_to_all x1, waiting for transfers between devices: 30.7 us -> 22.1 us  [on_device(): lax.all_to_all(slots, BOTH, split_axis=0, concat_axis=1, tiled=True)]
    pallas_call x8 -> x4, Pallas kernels: 8.5 us -> 0.91 us  [fold(): pl.pallas_call(following(functools.partial(fold_kernel, len(terms)), len(...]
  transfers between devices with their start and end apart: 53 -> 22, of which waited for: 20 -> 5; matrix products, arithmetic and copies ran while one was open for 4% -> 6% of each run, Pallas kernels for 29% -> 36%
where the time goes in v3:
time: 578 us; the launch traced here: 569 us
  Pallas kernels  393 us (68%)
  local copies, waits for them, and re-layouts  61.5 us (11%)
  waiting for transfers between devices  56.3 us (10%)
  starting transfers between devices  36.4 us (6%)
  other arithmetic  12.7 us (2%)
  matrix products  7.38 us (1%)
    pallas_call x4, Pallas kernels, feed(): pl.pallas_call(functools.partial(feed_kernel, wide, started, len(pieces),...  149 us
    pallas_call x1, Pallas kernels, reduce_tail(): pl.pallas_call(functools.partial(tail_kernel, line, places.rows, tuple((k...  50.4 us
    unnamed x171, local copies, waits for them, and re-layouts  42.4 us
    ppermute x21, waiting for transfers between devices, send(): return lax.ppermute(array, BOTH, pairs)  34.2 us
    pallas_call x1, Pallas kernels, attend_back(): pl.pallas_call(following(attend_back_kernel, 10, after), grid_spec=pltpu....  33.8 us
    pallas_call x1, Pallas kernels, middle_back(): pl.pallas_call(carrying(middle_back_kernel, tuple((kind for kind, _ in lo...  33.7 us
    ppermute x21, starting transfers between devices, send(): return lax.ppermute(array, BOTH, pairs)  29.9 us
    pallas_call x1, Pallas kernels, spread(): pl.pallas_call(functools.partial(spread_kernel, kinds), in_specs=[ANYWHER...  25.7 us
  transfers between devices with their start and end apart: 22, of which 5 were waited for; matrix products, arithmetic and copies ran while one was open for 6% of the time, Pallas kernels for 36%

profile of v3, /device:TPU:0, one launch (start us, length us, event | category | flops | bytes accessed | tf_op | source)
XLA Modules:
  0.0 569.4 jit_solution(1233934094393299387)
XLA Ops:
  4.8 5.1 collective-permute-start
  18.2 3.7 collective-permute-done.1.refs_2_
  23.7 25.7 %spread.1 = (bf16[1,896,2176]{2,1,0:T(8,128)(2,1)}, bf16[3,32,1280]{2,1,0:T(8,128)(2,1)}, bf16[3,32,1280]{2,1,0:T(8,128)(2,1)}, bf16[3,32,1280]{2,1,0:T(8,128)(2,1)}) custom-call(bf16[1,112,2176]{2,1,0:T(8,128)(2,1)} %copy-done.36, bf16[3,32,1280]{2,1,0:T(8,128)(2,1)} %copy-done.16, bf16[3,32,1280]{2,1,0:T(8,128)(2,1)} %copy-done.16, ...), custom_call_target="tpu_custom_call" | custom-call | flops 1 | bytes 1 | tf_op jit(solution)/shard_map/spread/pallas_call | solution.py:274
  64.4 10.8 %project.1 = (bf16[1024,896]{1,0:T(8,128)(2,1)}, bf16[1024,896]{1,0:T(8,128)(2,1)}, bf16[1024,896]{1,0:T(8,128)(2,1)}, bf16[1024,128]{1,0:T(8,128)(2,1)}, bf16[1024,128]{1,0:T(8,128)(2,1)}) custom-call(bf16[1024,896]{1,0:T(8,128)(2,1)} %bitcast.68, bf16[896,896]{1,0:T(8,128)(2,1)} %fusion.4.refs_1_.refs_5_.refs_8_, bf16[896,2176]{1,0:T(8,128)(2,1)} %bitcast.39, ...), custom_call_target="tpu_custom_call" | custom-call | flops 1 | bytes 1 | tf_op jit(solution)/shard_map/project/pallas_call | solution.py:495
  81.0 2.1 stacked_rows.6.refs_3_.refs_7_.refs_6_.refs_8_
  84.6 4.2 collective-permute-start.3
  89.9 2.1 collective-permute-start.12
  93.2 16.6 %collective-permute-done.3 = bf16[1024,256]{1,0:T(8,128)(2,1)} collective-permute-done((bf16[1024,256]{1,0:T(8,128)(2,1)}, bf16[1024,256]{1,0:T(8,128)(2,1)}, u32[]{:S(2)}, u32[]{:S(2)}) %collective-permute-start.3) | collective-permute-done | bytes 524320 | tf_op jit(solution)/shard_map/ppermute | solution.py:123
  113.8 3.5 fusion.5
  117.4 3.8 copy.69.refs_3_
  121.2 2.3 collective-permute-start.13
  125.9 22.5 %attend.1 = (bf16[2,512,896]{2,1,0:T(8,128)(2,1)}, f32[2,512,128]{2,1,0:T(8,128)}) custom-call(s32[2,4]{1,0:T(2,128)} %and_select_fusion.refs_0_, bf16[2,512,896]{2,1,0:T(8,128)(2,1)} %bitcast.44, bf16[2,512,128]{2,1,0:T(8,128)(2,1)} %bitcast.66, bf16[2,512,128]{2,1,0:T(8,128)(2,1)} %bitcast.60, bf16[2,512,128]{2,1,0:T(8,128)(2,1)} %bitcast.64, ...), custom_call_target="tpu_custom_call" | custom-call | flops 1 | bytes 1 | tf_op jit(solution)/shard_map/attend/pallas_call | solution.py:607
  148.4 8.4 %middle.1 = (f32[1024,896]{1,0:T(8,128)}, bf16[1024,896]{1,0:T(8,128)(2,1)}, bf16[896,1024]{1,0:T(8,128)(2,1)}) custom-call(bf16[1024,896]{1,0:T(8,128)(2,1)} %bitcast.56, bf16[1024,896]{1,0:T(8,128)(2,1)} %get-tuple-element.117.refs_1_.refs_6_, bf16[896,2176]{1,0:T(8,128)(2,1)} %bitcast.40, f32[1,896]{1,0:T(1,128)} %get-tuple-element.272.refs_3_.refs_7_, ...), custom_call_target="tpu_custom_call" | custom-call | flops 1 | bytes 1 | tf_op jit(solution)/shard_map/middle/pallas_call | solution.py:753
  158.3 2.2 stacked_rows.7.refs_8_.refs_10_
  161.7 37.6 %feed.4 = (f32[1024,896]{1,0:T(8,128)}, f32[1024,896]{1,0:T(8,128)}, bf16[3,224,1280]{2,1,0:T(8,128)(2,1)}, bf16[3,224,1280]{2,1,0:T(8,128)(2,1)}, bf16[3,448,12...) custom-call(bf16[1024,896]{1,0:T(8,128)(2,1)} %get-tuple-element.119.refs_4_.refs_0_, ...), custom_call_target="tpu_custom_call" | custom-call | flops 1 | bytes 1 | tf_op jit(solution)/shard_map/feed/pallas_call | solution.py:1042
  199.4 44.8 %feed.5 = (f32[1024,896]{1,0:T(8,128)}, f32[1024,896]{1,0:T(8,128)}, bf16[3,224,1280]{2,1,0:T(8,128)(2,1)}, bf16[3,224,1280]{2,1,0:T(8,128)(2,1)}, bf16[3,448,12...) custom-call(bf16[1024,896]{1,0:T(8,128)(2,1)} %get-tuple-element.119.refs_4_.refs_0_, ...), custom_call_target="tpu_custom_call" | custom-call | flops 1 | bytes 1 | tf_op jit(solution)/shard_map/feed/pallas_call | solution.py:1042
  246.8 31.9 %feed.6 = (f32[1024,896]{1,0:T(8,128)}, f32[1024,896]{1,0:T(8,128)}, bf16[3,224,1280]{2,1,0:T(8,128)(2,1)}, bf16[3,224,1280]{2,1,0:T(8,128)(2,1)}, bf16[3,448,12...) custom-call(bf16[1024,896]{1,0:T(8,128)(2,1)} %get-tuple-element.119.refs_4_.refs_0_, ...), custom_call_target="tpu_custom_call" | custom-call | flops 1 | bytes 1 | tf_op jit(solution)/shard_map/feed/pallas_call | solution.py:1042
  282.3 34.7 %feed.7 = (f32[1024,896]{1,0:T(8,128)}, f32[1024,896]{1,0:T(8,128)}, bf16[3,224,1024]{2,1,0:T(8,128)(2,1)}, bf16[3,224,1024]{2,1,0:T(8,128)(2,1)}, bf16[3,448,10...) custom-call(bf16[1024,896]{1,0:T(8,128)(2,1)} %get-tuple-element.119, ...), custom_call_target="tpu_custom_call" | custom-call | flops 1 | bytes 1 | tf_op jit(solution)/shard_map/feed/pallas_call | solution.py:1042
  320.4 33.7 %middle_back.1 = (bf16[1024,896]{1,0:T(8,128)(2,1)}, f32[1024,896]{1,0:T(8,128)}, bf16[1024,896]{1,0:T(8,128)(2,1)}, bf16[448,896]{1,0:T(8,128)(2,1)}, bf16[448,...) custom-call(f32[1024,896]{1,0:T(8,128)} %get-tuple-element.118.refs_, ...), custom_call_target="tpu_custom_call" | custom-call | flops 1 | bytes 1 | tf_op jit(solution)/shard_map/middle_back/pallas_call | solution.py:812
  359.1 33.8 %attend_back.1 = (bf16[2,512,896]{2,1,0:T(8,128)(2,1)}, f32[2,512,256]{2,1,0:T(8,128)}, bf16[2,512,256]{2,1,0:T(8,128)(2,1)}) custom-call(s32[2,4]{1,0:T(2,128)} %and_select_fusion.refs_0_, bf16[2,512,896]{2,1,0:T(8,128)(2,1)} %bitcast.45, bf16[2,512,128]{2,1,0:T(8,128)(2,1)} %bitcast.67, bf16[2,512,128]{2,1,0:T(8,128)(2,1)} %bitcast.61, ...), custom_call_target="tpu_custom_call" | custom-call | flops 1 | bytes 1 | tf_op jit(solution)/shard_map/attend_back/pallas_call | solution.py:704
  394.4 3.6 collective-permute-start.20
  402.1 12.2 %collective-permute-done.16 = bf16[2,512,256]{2,1,0:T(8,128)(2,1)S(1)} collective-permute-done((bf16[2,512,256]{2,1,0:T(8,128)(2,1)}, bf16[2,512,256]{2,1,0:T(8,128)(2,1)S(1)}, u32[]{:S(2)}, u32[]{:S(2)}) %collective-permute-start.16) | collective-permute-done | bytes 524320 | tf_op jit(solution)/shard_map/ppermute | solution.py:123
  415.0 22.1 %project_back.1 = (f32[1024,896]{1,0:T(8,128)}, bf16[448,1152]{1,0:T(8,128)(2,1)}, bf16[448,1152]{1,0:T(8,128)(2,1)}, f32[1,896]{1,0:T(1,128)}, f32[1,1152]{1,0:...) custom-call(bf16[1024,896]{1,0:T(8,128)(2,1)} %bitcast.46, ...), custom_call_target="tpu_custom_call" | custom-call | flops 1 | bytes 1 | tf_op jit(solution)/shard_map/project_back/pallas_call | solution.py:1133
  441.1 3.0 pad_maximum_fusion.own
  446.6 50.4 %reduce_tail.1 = f32[1,28,2176]{2,1,0:T(8,128)} custom-call(bf16[448,2176]{1,0:T(8,128)(2,1)} %pad_maximum_fusion.own, bf16[448,2176]{1,0:T(8,128)(2,1)} %pad_maximum_fusion.1.other), custom_call_target="tpu_custom_call" | custom-call | flops 1 | bytes 1 | tf_op jit(solution)/shard_map/reduce_tail/pallas_call | solution.py:414
  499.7 5.1 packed.1
  504.8 6.5 %all-to-all-start = ((bf16[160,28,128]{2,1,0:T(8,128)(2,1)}), bf16[160,28,128]{2,1,0:T(8,128)(2,1)}, u32[]{:S(2)}, u32[]{:S(2)}) async-start(bf16[160,28,128]{2,1,0:T(8,128)(2,1)} %get-tuple-element.195.refs_17_), calls=%async_computation | async-start | bytes 2621440 | tf_op jit(solution)/shard_map/all_to_all | solution.py:1549
  511.9 8.5 %picked.1.weight_ref = f32[5,896,128]{2,1,0:T(8,128)} custom-call(s32[5]{0:T(128)} %dynamic_slice.3.refs_0_.block_ref, bf16[896,896]{1,0:T(8,128)(2,1)} %fusion.4.refs_1_.refs_5_.refs_8_, bf16[1,896,2176]{2,1,0:T(8,128)(2,1)} %get-tuple-element.109.refs_3_.refs_2_, bf16[3,112,1280]{2,1,0:T(8,128)(2,1)} %stacked_rows.5.refs_7_.refs_4_.refs_3_, ...), custom_call_target="tpu_custom_call" | custom-call | flops 1 | bytes 1 | tf_op jit(solution)/shard_map/picked/pallas_call | solution.py:1223
  521.0 22.1 %all-to-all-done = bf16[160,28,128]{2,1,0:T(8,128)(2,1)} async-done(((bf16[160,28,128]{2,1,0:T(8,128)(2,1)}), bf16[160,28,128]{2,1,0:T(8,128)(2,1)}, u32[]{:S(2)}, u32[]{:S(2)}) %all-to-all-start) | async-done | bytes 1146912 | tf_op jit(solution)/shard_map/all_to_all | solution.py:1549
  543.2 2.8 copy.77
  546.0 2.1 all_to_all.16.grad_ref
  553.4 11.0 %rotated_adam.1 = (f32[5,896,128]{2,1,0:T(8,128)}, f32[5,896,128]{2,1,0:T(8,128)}, f32[5,896,128]{2,1,0:T(8,128)}) custom-call(s32[5]{0:T(128)S(1)} %copy-done.71, bf16[5,896,128]{2,1,0:T(8,128)(2,1)S(1)} %all_to_all.16.grad_ref, f32[5,896,128]{2,1,0:T(8,128)S(1)} %copy-done.7, f32[5,896,128]{2,1,0:T(8,128)S(1)} %copy-done.32, ...), custom_call_target="tpu_custom_call" | custom-call | flops 1 | bytes 1 | tf_op jit(solution)/shard_map/rotated_adam/pallas_call | solution.py:1310
  (262 shorter events, 88.4 us)
Async XLA Ops:
  0.6 113.2 %copy-start = (bf16[2,1,512,896]{3,2,1,0:T(8,128)(2,1)S(1)}, bf16[2,1,512,896]{3,2,1,0:T(8,128)(2,1)}, u32[]{:S(2)}) copy-start(bf16[2,1,512,896]{3,2,1,0:T(8,128)(2,1)} %param.19) | copy-start | bytes 5505028
  4.8 13.4 %collective-permute-start = (bf16[1,32,2176]{2,1,0:T(8,128)(2,1)S(1)}, bf16[1,32,2176]{2,1,0:T(8,128)(2,1)S(1)}, u32[]{:S(2)}, u32[]{:S(2)}) collective-permute-start(bf16[1,32,2176]{2,1,0:T(8,128)(2,1)S(1)} %rounded.4.refs_0_), channel_id=1, source_target_pairs={{0,24},{1,25},{2,26},{3,27},{4,28},{5,29},{6,30},{7,31},{8,0},{9,1... | collective-permute-start | bytes 417800 | tf_op jit(solution)/shard_map/ppermute | solution.py:123
  9.9 11.9 %collective-permute-start.1 = (bf16[1,32,2176]{2,1,0:T(8,128)(2,1)S(1)}, bf16[1,32,2176]{2,1,0:T(8,128)(2,1)}, u32[]{:S(2)}, u32[]{:S(2)}) collective-permute-start(bf16[1,32,2176]{2,1,0:T(8,128)(2,1)S(1)} %rounded.4.refs_0_), channel_id=1, source_target_pairs={{0,16},{1,17},{2,18},{3,19},{4,20},{5,21},{6,22},{7,23},{8,24},{9,... | collective-permute-start | bytes 417800 | tf_op jit(solution)/shard_map/ppermute | solution.py:123
  9.9 11.9 %collective-permute-start.2 = (bf16[1,32,2176]{2,1,0:T(8,128)(2,1)S(1)}, bf16[1,32,2176]{2,1,0:T(8,128)(2,1)}, u32[]{:S(2)}, u32[]{:S(2)}) collective-permute-start(bf16[1,32,2176]{2,1,0:T(8,128)(2,1)S(1)} %rounded.4.refs_0_), channel_id=1, source_target_pairs={{0,8},{1,9},{2,10},{3,11},{4,12},{5,13},{6,14},{7,15},{8,16},{9,17... | collective-permute-start | bytes 417800 | tf_op jit(solution)/shard_map/ppermute | solution.py:123
  53.7 21.5 %collective-permute-start.4 = (bf16[3,32,1280]{2,1,0:T(8,128)(2,1)S(1)}, bf16[3,32,1280]{2,1,0:T(8,128)(2,1)S(1)}, u32[]{:S(2)}, u32[]{:S(2)}) collective-permute-start(bf16[3,32,1280]{2,1,0:T(8,128)(2,1)S(1)} %rounded.6.refs_8_.refs_0_), channel_id=1, source_target_pairs={{0,24},{1,25},{2,26},{3,27},{4,28},{5,29},{6,30},{7,31},{8,0},{9,1... | collective-permute-start | bytes 737288 | tf_op jit(solution)/shard_map/ppermute | solution.py:123
  55.0 22.7 %collective-permute-start.5 = (bf16[3,32,1280]{2,1,0:T(8,128)(2,1)S(1)}, bf16[3,32,1280]{2,1,0:T(8,128)(2,1)}, u32[]{:S(2)}, u32[]{:S(2)}) collective-permute-start(bf16[3,32,1280]{2,1,0:T(8,128)(2,1)S(1)} %rounded.6.refs_8_.refs_0_), channel_id=1, source_target_pairs={{0,16},{1,17},{2,18},{3,19},{4,20},{5,21},{6,22},{7,23},{8,24},{9,... | collective-permute-start | bytes 737288 | tf_op jit(solution)/shard_map/ppermute | solution.py:123
  55.5 22.1 %collective-permute-start.6 = (bf16[3,32,1280]{2,1,0:T(8,128)(2,1)S(1)}, bf16[3,32,1280]{2,1,0:T(8,128)(2,1)}, u32[]{:S(2)}, u32[]{:S(2)}) collective-permute-start(bf16[3,32,1280]{2,1,0:T(8,128)(2,1)S(1)} %rounded.6.refs_8_.refs_0_), channel_id=1, source_target_pairs={{0,8},{1,9},{2,10},{3,11},{4,12},{5,13},{6,14},{7,15},{8,16},{9,17... | collective-permute-start | bytes 737288 | tf_op jit(solution)/shard_map/ppermute | solution.py:123
  63.1 48.7 %collective-permute-start.7 = (bf16[3,112,1280]{2,1,0:T(8,128)(2,1)}, bf16[3,112,1280]{2,1,0:T(8,128)(2,1)}, u32[]{:S(2)}, u32[]{:S(2)}) collective-permute-start(bf16[3,112,1280]{2,1,0:T(8,128)(2,1)} %stacked_rows.5.refs_7_.refs_4_.refs_3_), channel_id=1, source_target_pairs={{0,1},{1,0},{2,6},{3,7},{4,5},{5,4},{6,2},{7,3},{8,9},{9,8},{10,14... | collective-permute-start | bytes 2580488 | tf_op jit(solution)/shard_map/ppermute | solution.py:123
  83.2 28.7 %collective-permute-start.8 = (bf16[3,112,1280]{2,1,0:T(8,128)(2,1)S(1)}, bf16[3,112,1280]{2,1,0:T(8,128)(2,1)}, u32[]{:S(2)}, u32[]{:S(2)}) collective-permute-start(bf16[3,112,1280]{2,1,0:T(8,128)(2,1)S(1)} %stacked_rows.6.refs_3_.refs_7_.refs_6_.refs_8_), channel_id=1, source_target_pairs={{0,1},{1,0},{2,6},{3,7},{4,5},{5,4},{6,2},{7,3},{8,9},{9,8},{10,14... | collective-permute-start | bytes 2580488 | tf_op jit(solution)/shard_map/ppermute | solution.py:123
  84.6 25.2 %collective-permute-start.3 = (bf16[1024,256]{1,0:T(8,128)(2,1)}, bf16[1024,256]{1,0:T(8,128)(2,1)}, u32[]{:S(2)}, u32[]{:S(2)}) collective-permute-start(bf16[1024,256]{1,0:T(8,128)(2,1)} %pad_maximum_fusion.4), channel_id=1, source_target_pairs={{0,1},{2,3},{4,5},{6,7},{8,9},{10,11},{12,13},{14,15},{16,17},{18,... | collective-permute-start | bytes 1572872 | tf_op jit(solution)/shard_map/ppermute | solution.py:123
  89.7 20.1 %collective-permute-start.11 = (bf16[3,32,2304]{2,1,0:T(8,128)(2,1)}, bf16[3,32,2304]{2,1,0:T(8,128)(2,1)S(1)}, u32[]{:S(2)}, u32[]{:S(2)}) collective-permute-start(bf16[3,32,2304]{2,1,0:T(8,128)(2,1)} %rounded.7.refs_9_.refs_0_), channel_id=1, source_target_pairs={{0,24},{1,25},{2,26},{3,27},{4,28},{5,29},{6,30},{7,31},{8,0},{9,1... | collective-permute-start | bytes 1327112 | tf_op jit(solution)/shard_map/ppermute | solution.py:123
  89.9 31.2 %collective-permute-start.12 = (bf16[3,32,2304]{2,1,0:T(8,128)(2,1)}, bf16[3,32,2304]{2,1,0:T(8,128)(2,1)}, u32[]{:S(2)}, u32[]{:S(2)}) collective-permute-start(bf16[3,32,2304]{2,1,0:T(8,128)(2,1)} %rounded.7.refs_9_.refs_0_), channel_id=1, source_target_pairs={{0,16},{1,17},{2,18},{3,19},{4,20},{5,21},{6,22},{7,23},{8,24},{9,... | collective-permute-start | bytes 1327112 | tf_op jit(solution)/shard_map/ppermute | solution.py:123
  109.8 52.0 %collective-permute-start.9 = (bf16[3,112,1280]{2,1,0:T(8,128)(2,1)}, bf16[3,112,1280]{2,1,0:T(8,128)(2,1)}, u32[]{:S(2)}, u32[]{:S(2)}) collective-permute-start(bf16[3,112,1280]{2,1,0:T(8,128)(2,1)} %stacked_rows.5.refs_7_.refs_4_.refs_3_), channel_id=1, source_target_pairs={{0,4},{1,5},{2,3},{3,2},{4,0},{5,1},{6,7},{7,6},{8,12},{9,13},{10,... | collective-permute-start | bytes 2580488 | tf_op jit(solution)/shard_map/ppermute | solution.py:123
  109.8 89.6 %collective-permute-start.14 = (bf16[3,112,1280]{2,1,0:T(8,128)(2,1)S(1)}, bf16[3,112,1280]{2,1,0:T(8,128)(2,1)}, u32[]{:S(2)}, u32[]{:S(2)}) collective-permute-start(bf16[3,112,1280]{2,1,0:T(8,128)(2,1)S(1)} %stacked_rows.6.refs_3_.refs_7_.refs_6_.refs_8_), channel_id=1, source_target_pairs={{0,4},{1,5},{2,3},{3,2},{4,0},{5,1},{6,7},{7,6},{8,12},{9,13},{10,... | collective-permute-start | bytes 2580488 | tf_op jit(solution)/shard_map/ppermute | solution.py:123
  111.8 49.9 %collective-permute-start.10 = (bf16[3,112,1280]{2,1,0:T(8,128)(2,1)}, bf16[3,112,1280]{2,1,0:T(8,128)(2,1)}, u32[]{:S(2)}, u32[]{:S(2)}) collective-permute-start(bf16[3,112,1280]{2,1,0:T(8,128)(2,1)} %collective-permute-done.7.refs_8_.refs_5_.refs_4_), channel_id=1, source_target_pairs={{0,4},{1,5},{2,3},{3,2},{4,0},{5,1},{6,7},{7,6},{8,12},{9,13},{10,... | collective-permute-start | bytes 2580488 | tf_op jit(solution)/shard_map/ppermute | solution.py:123
  111.9 87.5 %collective-permute-start.15 = (bf16[3,112,1280]{2,1,0:T(8,128)(2,1)}, bf16[3,112,1280]{2,1,0:T(8,128)(2,1)}, u32[]{:S(2)}, u32[]{:S(2)}) collective-permute-start(bf16[3,112,1280]{2,1,0:T(8,128)(2,1)} %collective-permute-done.8.refs_4_.refs_7_.refs_9_), channel_id=1, source_target_pairs={{0,4},{1,5},{2,3},{3,2},{4,0},{5,1},{6,7},{7,6},{8,12},{9,13},{10,... | collective-permute-start | bytes 2580488 | tf_op jit(solution)/shard_map/ppermute | solution.py:123
  121.2 35.7 %collective-permute-start.13 = (bf16[3,32,2304]{2,1,0:T(8,128)(2,1)}, bf16[3,32,2304]{2,1,0:T(8,128)(2,1)S(1)}, u32[]{:S(2)}, u32[]{:S(2)}) collective-permute-start(bf16[3,32,2304]{2,1,0:T(8,128)(2,1)} %rounded.7.refs_9_.refs_0_), channel_id=1, source_target_pairs={{0,8},{1,9},{2,10},{3,11},{4,12},{5,13},{6,14},{7,15},{8,16},{9,17... | collective-permute-start | bytes 1327112 | tf_op jit(solution)/shard_map/ppermute | solution.py:123
  355.7 42.4 %collective-permute-start.17 = (bf16[3,112,1024]{2,1,0:T(8,128)(2,1)S(1)}, bf16[3,112,1024]{2,1,0:T(8,128)(2,1)S(1)}, u32[]{:S(2)}, u32[]{:S(2)}) collective-permute-start(bf16[3,112,1024]{2,1,0:T(8,128)(2,1)S(1)} %fold.7.refs_13_), channel_id=1, source_target_pairs={{0,1},{1,0},{2,6},{3,7},{4,5},{5,4},{6,2},{7,3},{8,9},{9,8},{10,14... | collective-permute-start | bytes 2064392 | tf_op jit(solution)/shard_map/ppermute | solution.py:123
  392.8 21.4 %collective-permute-start.16 = (bf16[2,512,256]{2,1,0:T(8,128)(2,1)}, bf16[2,512,256]{2,1,0:T(8,128)(2,1)S(1)}, u32[]{:S(2)}, u32[]{:S(2)}) collective-permute-start(bf16[2,512,256]{2,1,0:T(8,128)(2,1)} %get-tuple-element.160), channel_id=1, source_target_pairs={{1,0},{3,2},{5,4},{7,6},{9,8},{11,10},{13,12},{15,14},{17,16},{19,... | collective-permute-start | bytes 1572872 | tf_op jit(solution)/shard_map/ppermute | solution.py:123
  394.2 105.4 %collective-permute-start.18 = (bf16[3,32,1280]{2,1,0:T(8,128)(2,1)}, bf16[3,32,1280]{2,1,0:T(8,128)(2,1)}, u32[]{:S(2)}, u32[]{:S(2)}) collective-permute-start(bf16[3,32,1280]{2,1,0:T(8,128)(2,1)} %get-tuple-element.153.refs_10_), channel_id=1, source_target_pairs={{0,8},{1,9},{2,10},{3,11},{4,12},{5,13},{6,14},{7,15},{8,16},{9,17... | collective-permute-start | bytes 737288 | tf_op jit(solution)/shard_map/ppermute | solution.py:123
  394.2 105.4 %collective-permute-start.19 = (bf16[3,32,1280]{2,1,0:T(8,128)(2,1)}, bf16[3,32,1280]{2,1,0:T(8,128)(2,1)}, u32[]{:S(2)}, u32[]{:S(2)}) collective-permute-start(bf16[3,32,1280]{2,1,0:T(8,128)(2,1)} %get-tuple-element.154.refs_11_), channel_id=1, source_target_pairs={{0,16},{1,17},{2,18},{3,19},{4,20},{5,21},{6,22},{7,23},{8,24},{9,... | collective-permute-start | bytes 737288 | tf_op jit(solution)/shard_map/ppermute | solution.py:123
  394.4 105.2 %collective-permute-start.20 = (bf16[3,32,1280]{2,1,0:T(8,128)(2,1)S(1)}, bf16[3,32,1280]{2,1,0:T(8,128)(2,1)}, u32[]{:S(2)}, u32[]{:S(2)}) collective-permute-start(bf16[3,32,1280]{2,1,0:T(8,128)(2,1)S(1)} %copy-done.51), channel_id=1, source_target_pairs={{0,24},{1,25},{2,26},{3,27},{4,28},{5,29},{6,30},{7,31},{8,0},{9,1... | collective-permute-start | bytes 737288 | tf_op jit(solution)/shard_map/ppermute | solution.py:123
  446.5 53.1 %copy-start.52 = (bf16[3,32,1280]{2,1,0:T(8,128)(2,1)S(1)}, bf16[3,32,1280]{2,1,0:T(8,128)(2,1)}, u32[]{:S(2)}) copy-start(bf16[3,32,1280]{2,1,0:T(8,128)(2,1)} %get-tuple-element.168.refs_1_) | copy-start | bytes 737284
  446.5 53.1 %copy-start.53 = (bf16[3,32,1280]{2,1,0:T(8,128)(2,1)S(1)}, bf16[3,32,1280]{2,1,0:T(8,128)(2,1)}, u32[]{:S(2)}) copy-start(bf16[3,32,1280]{2,1,0:T(8,128)(2,1)} %get-tuple-element.169.refs_2_) | copy-start | bytes 737284
  446.6 53.1 %copy-start.54 = (bf16[3,32,1280]{2,1,0:T(8,128)(2,1)S(1)}, bf16[3,32,1280]{2,1,0:T(8,128)(2,1)}, u32[]{:S(2)}) copy-start(bf16[3,32,1280]{2,1,0:T(8,128)(2,1)} %get-tuple-element.170.refs_3_) | copy-start | bytes 737284
  446.6 53.1 %copy-start.55 = (bf16[3,32,1280]{2,1,0:T(8,128)(2,1)S(1)}, bf16[3,32,1280]{2,1,0:T(8,128)(2,1)}, u32[]{:S(2)}) copy-start(bf16[3,32,1280]{2,1,0:T(8,128)(2,1)} %get-tuple-element.172.refs_5_) | copy-start | bytes 737284
  446.6 53.1 %copy-start.56 = (bf16[3,32,1280]{2,1,0:T(8,128)(2,1)S(1)}, bf16[3,32,1280]{2,1,0:T(8,128)(2,1)}, u32[]{:S(2)}) copy-start(bf16[3,32,1280]{2,1,0:T(8,128)(2,1)} %get-tuple-element.173.refs_6_) | copy-start | bytes 737284
  446.6 53.1 %copy-start.57 = (bf16[3,32,1280]{2,1,0:T(8,128)(2,1)S(1)}, bf16[3,32,1280]{2,1,0:T(8,128)(2,1)}, u32[]{:S(2)}) copy-start(bf16[3,32,1280]{2,1,0:T(8,128)(2,1)} %get-tuple-element.174.refs_7_) | copy-start | bytes 737284
  446.6 53.1 %copy-start.64 = (bf16[3,32,1024]{2,1,0:T(8,128)(2,1)S(1)}, bf16[3,32,1024]{2,1,0:T(8,128)(2,1)}, u32[]{:S(2)}) copy-start(bf16[3,32,1024]{2,1,0:T(8,128)(2,1)} %get-tuple-element.177.refs_13_) | copy-start | bytes 589828
  446.6 53.1 %copy-start.65 = (bf16[3,32,1024]{2,1,0:T(8,128)(2,1)S(1)}, bf16[3,32,1024]{2,1,0:T(8,128)(2,1)}, u32[]{:S(2)}) copy-start(bf16[3,32,1024]{2,1,0:T(8,128)(2,1)} %get-tuple-element.178.refs_14_) | copy-start | bytes 589828
  446.6 53.1 %copy-start.66 = (bf16[3,32,1024]{2,1,0:T(8,128)(2,1)S(1)}, bf16[3,32,1024]{2,1,0:T(8,128)(2,1)}, u32[]{:S(2)}) copy-start(bf16[3,32,1024]{2,1,0:T(8,128)(2,1)} %get-tuple-element.179.refs_15_) | copy-start | bytes 589828
  504.8 38.3 %all-to-all-start = ((bf16[160,28,128]{2,1,0:T(8,128)(2,1)}), bf16[160,28,128]{2,1,0:T(8,128)(2,1)}, u32[]{:S(2)}, u32[]{:S(2)}) async-start(bf16[160,28,128]{2,1,0:T(8,128)(2,1)} %get-tuple-element.195.refs_17_), calls=%async_computation | async-start | bytes 2621440 | tf_op jit(solution)/shard_map/all_to_all | solution.py:1549
  (74 other events, 458.1 us)

commit v4 on v3

--- a/solution.py
+++ b/solution.py
@@ -123,8 +123,12 @@
     return lax.ppermute(array, BOTH, pairs)
 
 
-def line_parts(places, shard):
-    return [shard] + [send(shard, places.ahead[-k % places.line]) for k in range(1, places.line)]
+def line_parts(places, shard, last=None):
+    count = places.line
+    return [shard] + [
+        send(shard if last is None or k < count - 1 else last, places.ahead[-k % count])
+        for k in range(1, count)
+    ]
 
 
 def stack_kernel(count, *refs):
@@ -145,7 +149,7 @@
         out_specs=pl.BlockSpec((1, QUARTER, width), lambda m: (m, 0, 0)),
         out_shape=jax.ShapeDtypeStruct((pages, QUARTER, width), BF16),
         scratch_shapes=[pltpu.VMEM((QUARTER, width), F32)],
-        compiler_params=params(32),
+        compiler_params=params(60),
         cost_estimate=TINY,
         name="stacked_rows",
     )(*parts, *after)
@@ -306,7 +310,7 @@
         in_specs=[spec(block) for _, block in terms] + [ANYWHERE] * len(after),
         out_specs=spec(0),
         out_shape=jax.ShapeDtypeStruct((pages, rows, width), BF16),
-        compiler_params=params(32),
+        compiler_params=params(60),
         cost_estimate=TINY,
         name="fold",
     )(*[array for array, _ in terms], *after)
@@ -339,7 +343,7 @@
             for k in range(line)
         ],
         scratch_shapes=[pltpu.VMEM((QUARTER, width), F32)],
-        compiler_params=params(32),
+        compiler_params=params(60),
         cost_estimate=TINY,
         name="share",
     )(*terms, *after)
@@ -365,55 +369,70 @@
         self.parts += list(arrived)
 
 
-def tail_kernel(line, rows, load_kinds, own, other, *refs):
-    count = len(load_kinds)
-    srcs, out, dsts = refs[:count], refs[count], refs[count + 1 : 2 * count + 1]
+def tail_kernel(line, rows, widths, load_kinds, *refs):
+    parts_n, count = len(widths), len(load_kinds)
+    owns, others = refs[:parts_n], refs[parts_n : 2 * parts_n]
+    at = 2 * parts_n
+    srcs, out, dsts = refs[at : at + count], refs[at + count], refs[at + count + 1 : at + 2 * count + 1]
     came, half, came_half, quart, came_quart, keep, parts, came_parts, sems, load_sems = refs[
-        2 * count + 1 :
+        at + 2 * count + 1 :
     ]
-    kinds = ["sibling", "long", "short"] + [(k, line) for k in range(1, line)]
-    greet_kinds(kinds)
+    starts = [sum(widths[:n]) for n in range(parts_n)]
+    spans = [slice(start, start + width) for start, width in zip(starts, widths)]
+    sibling, long, short = neighbours()
+    greet_kinds(["sibling", "long", "short"] + [(k, line) for k in range(1, line)])
+    moves = []
+
+    def go(src, dst, device):
+        moves.append(push(src, dst, sems, len(moves), device))
+        moves[-1].start()
+        return moves[-1]
+
+    first = [go(others[n], came.at[:, span], sibling) for n, span in enumerate(spans)]
     for move in carried(load_kinds, srcs, dsts, load_sems):
         move.start()
-    first = push(other, came, sems, 0, device_of("sibling"))
-    first.start()
-    first.wait_recv()
     two = 2 * QUARTER
-    half[...] = (own[two:].astype(F32) + came[two:].astype(F32)).astype(BF16)
-    second = push(half, came_half, sems, 1, device_of("long"))
-    second.start()
-    keep[...] = own[:two].astype(F32) + came[:two].astype(F32)
-    second.wait_recv()
-    quart[...] = (keep[QUARTER:] + came_half[QUARTER:].astype(F32)).astype(BF16)
-    third = push(quart, came_quart, sems, 2, device_of("short"))
-    third.start()
-    keep[:QUARTER] = keep[:QUARTER] + came_half[:QUARTER].astype(F32)
-    third.wait_recv()
-    keep[:QUARTER] = keep[:QUARTER] + came_quart[...].astype(F32)
-    moves = [first, second, third]
-    for k in range(1, line):
-        parts[k - 1, :rows] = keep[rows * k : rows * (k + 1), :].astype(BF16)
-        moves.append(
-            push(parts.at[k - 1], came_parts.at[k - 1], sems, 2 + k, device_of((k, line)))
-        )
-        moves[-1].start()
-    total = keep[:rows]
-    for k in range(1, line):
-        moves[2 + k].wait_recv()
-        total = total + came_parts[k - 1, :rows].astype(F32)
-    out[0] = total
+    second, third, last = [], [], []
+    for n, span in enumerate(spans):
+        first[n].wait_recv()
+        half[:, span] = (owns[n][two:].astype(F32) + came[two:, span].astype(F32)).astype(BF16)
+        second.append(go(half.at[:, span], came_half.at[:, span], long))
+        keep[:, span] = owns[n][:two].astype(F32) + came[:two, span].astype(F32)
+    for n, span in enumerate(spans):
+        second[n].wait_recv()
+        total = keep[QUARTER:, span] + came_half[QUARTER:, span].astype(F32)
+        quart[:, span] = total.astype(BF16)
+        third.append(go(quart.at[:, span], came_quart.at[:, span], short))
+        keep[:QUARTER, span] = keep[:QUARTER, span] + came_half[:QUARTER, span].astype(F32)
+    for n, span in enumerate(spans):
+        third[n].wait_recv()
+        keep[:QUARTER, span] = keep[:QUARTER, span] + came_quart[:, span].astype(F32)
+        for k in range(1, line):
+            parts[k - 1, :rows, span] = keep[rows * k : rows * (k + 1), span].astype(BF16)
+            last.append(
+                go(parts.at[k - 1, :, span], came_parts.at[k - 1, :, span], device_of((k, line)))
+            )
+    for n, span in enumerate(spans):
+        total = keep[:rows, span]
+        for k in range(1, line):
+            last[n * (line - 1) + k - 1].wait_recv()
+            total = total + came_parts[k - 1, :rows, span].astype(F32)
+        out[0, :, span] = total
     for move in moves:
         move.wait_send()
     for move in carried(load_kinds, srcs, dsts, load_sems):
         move.wait()
 
 
-def reduce_tail(places, own, other, loads):
-    width, line, padded = own.shape[1], places.line, places.padded
+def reduce_tail(places, owns, others, loads):
+    widths, line, padded = [a.shape[1] for a in owns], places.line, places.padded
+    width = sum(widths)
     vmem = pl.BlockSpec(memory_space=pltpu.VMEM)
     return pl.pallas_call(
-        functools.partial(tail_kernel, line, places.rows, tuple(kind for kind, _ in loads)),
-        in_specs=[vmem, vmem] + [ANYWHERE] * len(loads),
+        functools.partial(
+            tail_kernel, line, places.rows, widths, tuple(kind for kind, _ in loads)
+        ),
+        in_specs=[vmem] * (2 * len(owns)) + [ANYWHERE] * len(loads),
         out_specs=[vmem] + [ANYWHERE] * len(loads),
         out_shape=[jax.ShapeDtypeStruct((1, places.rows, width), F32)] + [like(a) for _, a in loads],
         scratch_shapes=[
@@ -425,13 +444,13 @@
             pltpu.VMEM((2 * QUARTER, width), F32),
             pltpu.VMEM((line - 1, padded, width), BF16),
             pltpu.VMEM((line - 1, padded, width), BF16),
-            pltpu.SemaphoreType.DMA((2, 2 + line)),
+            pltpu.SemaphoreType.DMA((2, len(owns) * (2 + line))),
             pltpu.SemaphoreType.DMA((2, max(1, len(loads)))),
         ],
         compiler_params=params(56, collective_id=11, has_side_effects=True),
         cost_estimate=TINY,
         name="reduce_tail",
-    )(own, other, *[array for _, array in loads])
+    )(*owns, *others, *[array for _, array in loads])
 
 
 def round_kernel(spans, *refs):
@@ -451,7 +470,7 @@
         in_specs=[pl.BlockSpec(memory_space=pltpu.VMEM)] * len(parts) + [ANYWHERE] * len(after),
         out_specs=pl.BlockSpec(memory_space=pltpu.VMEM),
         out_shape=jax.ShapeDtypeStruct((pages, padded, width), BF16),
-        compiler_params=params(32),
+        compiler_params=params(60),
         cost_estimate=TINY,
         name="rounded",
     )(*parts, *after)
@@ -462,7 +481,22 @@
 
 
 def project_kernel(x_ref, pi_ref, *refs):
-    w_ref, gain_ref, bias_ref, cos_ref, sin_ref, xp_ref, nl_ref, q_ref, k_ref, v_ref = refs
+    (
+        w_ref, gain_ref, bias_ref, cos_ref, sin_ref, xp_ref, nl_ref, q_ref, k_ref, v_ref, came_hbm,
+        kv_scr, sems,
+    ) = refs
+    step, steps = pl.program_id(0), kv_scr.shape[0] // TOKEN_TILE
+    seq = lax.axis_index("seq")
+    other = (lax.axis_index("dp"), 1 - seq)
+
+    def hand_on(n):
+        rows = pl.ds(pl.multiple_of(n * TOKEN_TILE, TOKEN_TILE), TOKEN_TILE)
+        return push(kv_scr.at[rows, :], came_hbm.at[rows, :], sems, n, other)
+
+    @pl.when(step == 0)
+    def _():
+        greet([other])
+
     xp = dot_nn(x_ref[...], pi_ref[...])
     inv = lax.rsqrt(jnp.sum(xp * xp, axis=1, keepdims=True) * (1.0 / D) + norm_epsilon)
     nl = (xp * inv * gain_ref[...]).astype(BF16)
@@ -478,7 +512,24 @@
             q_ref[:, 128 * t : 128 * (t + 1)] = (turned.astype(F32) * 0.125).astype(BF16)
         else:
             k_ref[...] = turned
-    v_ref[...] = lin[:, QW + KW :].astype(BF16)
+            kv_scr[pl.ds(pl.multiple_of(step * TOKEN_TILE, TOKEN_TILE), TOKEN_TILE), :KW] = turned
+    value = lin[:, QW + KW :].astype(BF16)
+    v_ref[...] = value
+    kv_scr[pl.ds(pl.multiple_of(step * TOKEN_TILE, TOKEN_TILE), TOKEN_TILE), KW:] = value
+
+    @pl.when(seq == 0)
+    def _():
+        hand_on(step).start()
+
+    @pl.when((step == steps - 1) & (seq == 0))
+    def _():
+        for n in range(steps):
+            hand_on(n).wait_send()
+
+    @pl.when((step == steps - 1) & (seq == 1))
+    def _():
+        for n in range(steps):
+            hand_on(n).wait_recv()
 
 
 def project(x, pi, weights, gain, bias, cos, sin, after=()):
@@ -499,32 +550,43 @@
         + [whole(D, width)]
         + [whole(1, D), whole(1, QKV), tile(128), tile(128)]
         + [ANYWHERE] * len(after),
-        out_specs=[tile(c) for c, _ in shapes],
-        out_shape=[jax.ShapeDtypeStruct((rows, c), t) for c, t in shapes],
-        compiler_params=params(56),
+        out_specs=[tile(c) for c, _ in shapes] + [ANYWHERE],
+        out_shape=[jax.ShapeDtypeStruct((rows, c), t) for c, t in shapes + [(2 * KW, BF16)]],
+        scratch_shapes=[
+            pltpu.VMEM((rows, 2 * KW), BF16),
+            pltpu.SemaphoreType.DMA((2, rows // TOKEN_TILE)),
+        ],
+        compiler_params=params(56, collective_id=12, has_side_effects=True),
         cost_estimate=TINY,
         name="project",
     )(x, pi, weights, gain, bias, cos, sin, *after)
 
 
-def padded_heads(recv, own, out):
-    lane = lax.broadcasted_iota(jnp.int32, (512, 128), 1)
+def padded_heads(recv, own, out, turned):
     for part, ref in enumerate((recv, own)):
-        if ref is None:
-            continue
         natural = ref[0].astype(F32)
-        crossed = pltpu.roll(natural, 64, 1)
-        rows = pl.ds(512 * part, 512)
-        for s, (_, half, head) in enumerate(HEAD_SETS):
-            source = natural if half == head else crossed
-            keep = (lane >= 64) if half else (lane < 64)
-            out[s, rows, :] = jnp.where(keep, source, 0.0).astype(BF16)
+        span = pl.ds(512 * part, 512)
+        if out is not None:
+            lane = lax.broadcasted_iota(jnp.int32, (512, 128), 1)
+            crossed = pltpu.roll(natural, 64, 1)
+            for s, (_, half, head) in enumerate(HEAD_SETS):
+                source = natural if half == head else crossed
+                keep = (lane >= 64) if half else (lane < 64)
+                out[s, span, :] = jnp.where(keep, source, 0.0).astype(BF16)
+        if turned is not None:
+            flat = natural.T
+            other = jnp.concatenate([flat[64:], flat[:64]], axis=0)
+            row = lax.broadcasted_iota(jnp.int32, (128, 512), 0)
+            for s, (_, half, head) in enumerate(HEAD_SETS):
+                source = flat if half == head else other
+                keep = (row >= 64) if half else (row < 64)
+                turned[s, :, span] = jnp.where(keep, source, 0.0).astype(BF16)
 
 
 def block_bias(kb, i, begin):
     shape = (128, 128)
-    key = kb * 128 + lax.broadcasted_iota(jnp.int32, shape, 1)
-    query = 512 + i * 128 + lax.broadcasted_iota(jnp.int32, shape, 0)
+    key = kb * 128 + lax.broadcasted_iota(jnp.int32, shape, 0)
+    query = 512 + i * 128 + lax.broadcasted_iota(jnp.int32, shape, 1)
     return jnp.where((key >= begin) & (key <= query), 0.0, masked_value)
 
 
@@ -532,18 +594,41 @@
     return jnp.concatenate([tile_of(p) for p in pairs], axis=0)
 
 
+def turned_block(ref, out):
+    for p in range(7):
+        cols = slice(128 * p, 128 * (p + 1))
+        out[:, cols] = ref[0, :, cols].astype(F32).T.astype(BF16)
+
+
+def pair_columns(s):
+    pairs = HEAD_SETS[s][0]
+    return slice(128 * pairs[0], 128 * (pairs[-1] + 1))
+
+
+def columns_of(s, n=None):
+    pairs = HEAD_SETS[s][0]
+    if n is None:
+        return slice(SET_ROWS[s], SET_ROWS[s] + 128 * len(pairs))
+    return slice(SET_ROWS[s] + 128 * n, SET_ROWS[s] + 128 * (n + 1))
+
+
+def eights(value):
+    return value.reshape(value.shape[0] // 8, 8, value.shape[1])
+
+
 def attend_kernel(
-    lo_ref, q_ref, kr_ref, ko_ref, vr_ref, vo_ref, ds_ref, o_ref, lse_ref, kp, vp, s_scr, m_scr, l_scr, acc
+    lo_ref, q_ref, kr_ref, ko_ref, vr_ref, vo_ref, ds_ref, o_ref, lse_ref, kp, vt, qt, s_scr, m_scr, l_scr, acc
 ):
     b, i = pl.program_id(0), pl.program_id(1)
 
     @pl.when(i == 0)
     def _():
-        padded_heads(kr_ref, ko_ref, kp)
-        padded_heads(vr_ref, vo_ref, vp)
+        padded_heads(kr_ref, ko_ref, kp, None)
+        padded_heads(vr_ref, vo_ref, None, vt)
 
     lo, hi = lo_ref[b, i], i + 5
     begin = ds_ref[0]
+    turned_block(q_ref, qt)
     m_scr[...] = jnp.full(m_scr.shape, masked_value, F32)
     l_scr[...] = jnp.zeros(l_scr.shape, F32)
     acc[...] = jnp.zeros(acc.shape, F32)
@@ -551,78 +636,78 @@
     def scores(kb, carry):
         bias = block_bias(kb, i, begin)
         keys = pl.ds(pl.multiple_of(kb * 128, 128), 128)
+        raws = [dot_nn(kp[s, keys, :], qt[:, pair_columns(s)]) for s in range(4)]
         for s, (pairs, _, _) in enumerate(HEAD_SETS):
-            x = stacked(lambda p: q_ref[0, :, 128 * p : 128 * (p + 1)], pairs)
-            raw = dot_nt(x, kp[s, keys, :])
-            for n in range(len(pairs)):
-                rows = slice(SET_ROWS[s] + 128 * n, SET_ROWS[s] + 128 * (n + 1))
-                value = raw[128 * n : 128 * (n + 1)] + bias
-                s_scr[kb, rows, :] = value
-                m_scr[rows, :] = jnp.maximum(m_scr[rows, :], value)
+            cols = columns_of(s)
+            value = raws[s] + jnp.concatenate([bias] * len(pairs), axis=1)
+            s_scr[kb, :, cols] = value
+            m_scr[:, cols] = jnp.maximum(m_scr[:, cols], jnp.max(eights(value), axis=0))
         return carry
 
     lax.fori_loop(lo, hi, scores, 0)
-    top = jnp.max(m_scr[...], axis=1, keepdims=True)
-    m_scr[...] = jnp.broadcast_to(top, m_scr.shape)
+    top = jnp.max(m_scr[...], axis=0, keepdims=True)
 
     def weigh(kb, carry):
         keys = pl.ds(pl.multiple_of(kb * 128, 128), 128)
-        for s, (pairs, _, _) in enumerate(HEAD_SETS):
-            rows = slice(SET_ROWS[s], SET_ROWS[s] + 128 * len(pairs))
-            p = jnp.exp(s_scr[kb, rows, :] - m_scr[rows, :])
-            l_scr[rows, :] += p
-            acc[rows, :] += dot_nn(p.astype(BF16), vp[s, keys, :])
+        probs = [jnp.exp(s_scr[kb, :, columns_of(s)] - top[:, columns_of(s)]) for s in range(4)]
+        parts = [dot_nn(vt[s, :, keys], probs[s].astype(BF16)) for s in range(4)]
+        for s in range(4):
+            cols = columns_of(s)
+            l_scr[:, cols] += jnp.sum(eights(probs[s]), axis=0)
+            acc[:, cols] += parts[s]
         return carry
 
     lax.fori_loop(lo, hi, weigh, 0)
-    total = jnp.sum(l_scr[...], axis=1, keepdims=True)
-    lse = m_scr[:, :1] + jnp.log(total)
+    total = jnp.sum(l_scr[...], axis=0, keepdims=True)
+    lse = top + jnp.log(total)
     share = 1.0 / total
-    lane = lax.broadcasted_iota(jnp.int32, (128, 128), 1)
-    lanes = jnp.zeros((128, 128), F32)
     outs = [None] * 7
     for s, (pairs, half, _) in enumerate(HEAD_SETS):
         for n, p in enumerate(pairs):
-            rows = slice(SET_ROWS[s] + 128 * n, SET_ROWS[s] + 128 * (n + 1))
-            part = acc[rows, :] * share[rows]
+            cols = columns_of(s, n)
+            part = acc[:, cols] * share[:, cols]
             outs[p] = part if outs[p] is None else outs[p] + part
-            lanes = jnp.where(lane == 2 * p + half, lse[rows], lanes)
+            head = 2 * p + half
+            lse_ref[0, head : head + 1, :] = lse[:, cols]
     for p in range(7):
-        o_ref[0, :, 128 * p : 128 * (p + 1)] = outs[p].astype(BF16)
-    lse_ref[0] = lanes
+        o_ref[0, :, 128 * p : 128 * (p + 1)] = outs[p].T.astype(BF16)
 
 
 def attend_specs():
     def block(cols):
         return pl.BlockSpec((1, 128, cols), lambda b, i, lo: (b, i, 0))
 
+    def lanes(rows):
+        return pl.BlockSpec((1, rows, 128), lambda b, i, lo: (b, 0, i))
+
     def stream(cols):
         return pl.BlockSpec((1, 512, cols), lambda b, i, lo: (b, 0, 0))
 
-    return block, stream
+    return block, lanes, stream
 
 
 def attend(lo, q, k_recv, k_own, v_recv, v_own, begin, after=()):
-    block, stream = attend_specs()
+    block, lanes, stream = attend_specs()
     return pl.pallas_call(
         following(attend_kernel, 7, after),
         grid_spec=pltpu.PrefetchScalarGridSpec(
             num_scalar_prefetch=1,
             grid=(MICRO, 4),
-            in_specs=[block(QW)] + [stream(KW)] * 4 + [block(1)] + [ANYWHERE] * len(after),
-            out_specs=[block(QW), block(128)],
+            in_specs=[block(QW)] + [stream(KW)] * 4 + [lanes(1)] + [ANYWHERE] * len(after),
+            out_specs=[block(QW), lanes(16)],
             scratch_shapes=[
                 pltpu.VMEM((4, 1024, 128), BF16),
-                pltpu.VMEM((4, 1024, 128), BF16),
-                pltpu.VMEM((8, ALL_ROWS, 128), F32),
-                pltpu.VMEM((ALL_ROWS, 128), F32),
-                pltpu.VMEM((ALL_ROWS, 128), F32),
-                pltpu.VMEM((ALL_ROWS, 128), F32),
+                pltpu.VMEM((4, 128, 1024), BF16),
+                pltpu.VMEM((128, QW), BF16),
+                pltpu.VMEM((8, 128, ALL_ROWS), F32),
+                pltpu.VMEM((8, ALL_ROWS), F32),
+                pltpu.VMEM((8, ALL_ROWS), F32),
+                pltpu.VMEM((128, ALL_ROWS), F32),
             ],
         ),
         out_shape=[
             jax.ShapeDtypeStruct((MICRO, 512, QW), BF16),
-            jax.ShapeDtypeStruct((MICRO, 512, 128), F32),
+            jax.ShapeDtypeStruct((MICRO, 16, 512), F32),
         ],
         compiler_params=params(56),
         cost_estimate=TINY,
@@ -632,60 +717,71 @@
 
 def attend_back_kernel(
     lo_ref, q_ref, kr_ref, ko_ref, vr_ref, vo_ref, ds_ref, o_ref, do_ref, lse_ref,
-    dq_ref, own_ref, recv_ref, kp, vp, dk, dv, dq_acc,
+    dq_ref, own_ref, recv_ref, kp, vp, kt, qt, dot_t, dk, dv, dq_acc,
 ):
     b, i = pl.program_id(0), pl.program_id(1)
 
     @pl.when(i == 0)
     def _():
-        padded_heads(kr_ref, ko_ref, kp)
-        padded_heads(vr_ref, vo_ref, vp)
+        padded_heads(kr_ref, ko_ref, kp, kt)
+        padded_heads(vr_ref, vo_ref, vp, None)
         dk[...] = jnp.zeros(dk.shape, F32)
         dv[...] = jnp.zeros(dv.shape, F32)
 
     lo, hi = lo_ref[b, i], i + 5
     begin = ds_ref[0]
-    lane = lax.broadcasted_iota(jnp.int32, (128, 128), 1)
     dq_acc[...] = jnp.zeros(dq_acc.shape, F32)
-    lse_all = lse_ref[0]
+    turned_block(q_ref, qt)
+    turned_block(do_ref, dot_t)
+    pick = lax.broadcasted_iota(jnp.int32, (8, 128), 1) // 64 == lax.broadcasted_iota(
+        jnp.int32, (8, 128), 0
+    )
+    pick = pick.astype(F32).astype(BF16)
+    halves = []
+    for p in range(7):
+        cols = slice(128 * p, 128 * (p + 1))
+        high, rest = split_two(o_ref[0, :, cols].astype(F32) * do_ref[0, :, cols].astype(F32))
+        halves.append(dot_nt(pick, high) + dot_nt(pick, rest))
     lse, dots = [], []
-    for s, (pairs, half, _) in enumerate(HEAD_SETS):
-        for p in pairs:
-            cols = slice(128 * p, 128 * (p + 1))
-            product = o_ref[0, :, cols].astype(F32) * do_ref[0, :, cols].astype(F32)
-            keep = (lane >= 64) if half else (lane < 64)
-            dots.append(jnp.sum(jnp.where(keep, product, 0.0), axis=1, keepdims=True))
-            head = 2 * p + half
-            lse.append(lse_all[:, head : head + 1])
+    for pairs, half, _ in HEAD_SETS:
+        heads = [2 * p + half for p in pairs]
+        lse.append(jnp.concatenate([lse_ref[0, h : h + 1, :] for h in heads], axis=1))
+        dots.append(jnp.concatenate([halves[p][half : half + 1] for p in pairs], axis=1))
 
     def one_block(kb, carry):
         bias = block_bias(kb, i, begin)
         keys = pl.ds(pl.multiple_of(kb * 128, 128), 128)
-        at = 0
+        work = []
         for s, (pairs, _, _) in enumerate(HEAD_SETS):
+            cols = columns_of(s)
             x = stacked(lambda p: q_ref[0, :, 128 * p : 128 * (p + 1)], pairs)
             y = stacked(lambda p: do_ref[0, :, 128 * p : 128 * (p + 1)], pairs)
-            raw = dot_nt(x, kp[s, keys, :])
-            d_prob = dot_nt(y, vp[s, keys, :])
-            probs, d_scores = [], []
-            for n in range(len(pairs)):
-                rows = slice(128 * n, 128 * (n + 1))
-                p = jnp.exp(raw[rows] + bias - lse[at + n])
-                probs.append(p.astype(BF16))
-                d_scores.append((p * (d_prob[rows] - dots[at + n])).astype(BF16))
-            at += len(pairs)
-            prob = jnp.concatenate(probs, axis=0)
-            d_score = jnp.concatenate(d_scores, axis=0)
-            d_query = dot_nn(d_score, kp[s, keys, :])
-            for n, p in enumerate(pairs):
-                dq_acc[p] += d_query[128 * n : 128 * (n + 1)]
-            dk[s, keys, :] += dot_tn(d_score, x)
-            dv[s, keys, :] += dot_tn(prob, y)
+            raw = dot_nn(kp[s, keys, :], qt[:, pair_columns(s)]) + jnp.concatenate([bias] * len(pairs), axis=1)
+            d_prob = dot_nn(vp[s, keys, :], dot_t[:, pair_columns(s)])
+            work.append((s, cols, x, y, raw, d_prob))
+        parts = []
+        for s, cols, x, y, raw, d_prob in work:
+            p = jnp.exp(raw - lse[s])
+            d_score = (p * (d_prob - dots[s])).astype(BF16)
+            parts.append((s, cols, x, y, p.astype(BF16), d_score))
+        sums = [
+            (s, cols, dot_nn(kt[s, :, keys], d_score), dot_nn(d_score, x), dot_nn(p, y))
+            for s, cols, x, y, p, d_score in parts
+        ]
+        for s, cols, d_query, d_key, d_value in sums:
+            dq_acc[:, cols] += d_query
+            dk[s, keys, :] += d_key
+            dv[s, keys, :] += d_value
         return carry
 
     lax.fori_loop(lo, hi, one_block, 0)
+    sums = [None] * 7
+    for s, (pairs, _, _) in enumerate(HEAD_SETS):
+        for n, p in enumerate(pairs):
+            part = dq_acc[:, columns_of(s, n)]
+            sums[p] = part if sums[p] is None else sums[p] + part
     for p in range(7):
-        dq_ref[0, :, 128 * p : 128 * (p + 1)] = (dq_acc[p] * 0.125).astype(BF16)
+        dq_ref[0, :, 128 * p : 128 * (p + 1)] = (sums[p] * 0.125).T.astype(BF16)
 
     @pl.when(i == 3)
     def _():
@@ -700,7 +796,7 @@
 
 
 def attend_back(lo, q, k_recv, k_own, v_recv, v_own, begin, out, d_out, lse, after=()):
-    block, stream = attend_specs()
+    block, lanes, stream = attend_specs()
     return pl.pallas_call(
         following(attend_back_kernel, 10, after),
         grid_spec=pltpu.PrefetchScalarGridSpec(
@@ -708,15 +804,18 @@
             grid=(MICRO, 4),
             in_specs=[block(QW)]
             + [stream(KW)] * 4
-            + [block(1), block(QW), block(QW), block(128)]
+            + [lanes(1), block(QW), block(QW), lanes(16)]
             + [ANYWHERE] * len(after),
             out_specs=[block(QW), stream(256), stream(256)],
             scratch_shapes=[
                 pltpu.VMEM((4, 1024, 128), BF16),
                 pltpu.VMEM((4, 1024, 128), BF16),
+                pltpu.VMEM((4, 128, 1024), BF16),
+                pltpu.VMEM((128, QW), BF16),
+                pltpu.VMEM((128, QW), BF16),
                 pltpu.VMEM((4, 1024, 128), F32),
                 pltpu.VMEM((4, 1024, 128), F32),
-                pltpu.VMEM((7, 128, 128), F32),
+                pltpu.VMEM((128, ALL_ROWS), F32),
             ],
         ),
         out_shape=[
@@ -799,7 +898,7 @@
         sib_ref[...] = g_scr[HALF:].astype(BF16)
 
 
-def middle_back(residual, mlp, d_normed, cot, attended, pi, weights, gain, loads):
+def middle_back(residual, mlp, d_normed, cot, attended, pi, weights, gain, after=()):
     rows = residual.shape[0]
     width = weights.shape[1]
 
@@ -810,15 +909,14 @@
         return pl.BlockSpec((r, c), lambda t: (0, 0))
 
     return pl.pallas_call(
-        carrying(middle_back_kernel, tuple(kind for kind, _ in loads), 8, 6),
+        following(middle_back_kernel, 8, after),
         grid=(rows // TOKEN_TILE,),
         in_specs=[tile(D)] * 4
         + [tile(QW), whole(D, D)]
         + [whole(D, width)]
         + [whole(1, D)]
-        + [ANYWHERE] * len(loads),
-        out_specs=[tile(D), tile(D), tile(QW), whole(HALF, QW), whole(HALF, QW), whole(1, D)]
-        + [ANYWHERE] * len(loads),
+        + [ANYWHERE] * len(after),
+        out_specs=[tile(D), tile(D), tile(QW), whole(HALF, QW), whole(HALF, QW), whole(1, D)],
         out_shape=[
             jax.ShapeDtypeStruct((rows, D), BF16),
             jax.ShapeDtypeStruct((rows, D), F32),
@@ -826,13 +924,12 @@
             jax.ShapeDtypeStruct((HALF, QW), BF16),
             jax.ShapeDtypeStruct((HALF, QW), BF16),
             jax.ShapeDtypeStruct((1, D), F32),
-        ]
-        + [like(array) for _, array in loads],
-        scratch_shapes=[pltpu.VMEM((D, QW), F32), pltpu.SemaphoreType.DMA((2, len(loads)))],
-        compiler_params=params(56, collective_id=9, has_side_effects=True),
+        ],
+        scratch_shapes=[pltpu.VMEM((D, QW), F32)],
+        compiler_params=params(56),
         cost_estimate=TINY,
         name="middle_back",
-    )(residual, mlp, d_normed, cot, attended, pi, weights, gain, *[array for _, array in loads])
+    )(residual, mlp, d_normed, cot, attended, pi, weights, gain, *after)
 
 
 def feed_kernel(wide, started, n_pieces, coming, kinds, *refs):
@@ -1297,7 +1394,7 @@
         out_shape=[jax.ShapeDtypeStruct((rows, width), F32) for _, width in targets]
         + [jax.ShapeDtypeStruct((slot_block.shape[0], rows, BW), BF16)],
         scratch_shapes=[pltpu.VMEM((rows, total), F32)],
-        compiler_params=params(48),
+        compiler_params=params(60),
         cost_estimate=TINY,
         name="packed",
     )(slot_block, *parts)
@@ -1316,7 +1413,7 @@
             out_specs=[slab] * 3,
         ),
         out_shape=[jax.ShapeDtypeStruct((capacity, D, BW), F32)] * 3,
-        compiler_params=params(40),
+        compiler_params=params(60),
         cost_estimate=TINY,
         name="rotated_adam",
     )(slot_block, grads, weights, first_moment, second_moment, left, right)
@@ -1376,6 +1473,11 @@
         jnp.arange(n_dev, dtype=jnp.int32)[:, None] * shard_rows == natural[None, :]
     ).astype(BF16)
     vector_rows = jnp.pad(vectors.reshape(1, vec_here), ((0, shard_rows - 1), (0, 128 - vec_here)))
+    cot = cotangent[:, 0].reshape(-1, D)
+    cot_p = dot_nn(cot, pi).astype(BF16)
+    cot_t = lax.dot_general(
+        pi, cot, (((0,), (1,)), ((), ())), preferred_element_type=F32
+    ).astype(BF16)
     attention_line = stacked_rows(
         line_parts(
             places,
@@ -1384,7 +1486,8 @@
                 places.padded,
                 [(0, 0, 0, QW), (0, 1, 0, KW), (0, 2, 0, KW), (0, 3, 0, QW), (0, 4, 0, 128)],
             ),
-        )
+        ),
+        after=(cot_p, cot_t),
     )
     feed_parts = [gate_weight, up_weight, down_t]
 
@@ -1420,26 +1523,18 @@
     sin = jnp.concatenate([-sin, sin, -sin, sin], axis=1)
     begin = doc_begin + here - seq_index * here
     lo = begin[:, ::128] // 128
-    begin = begin[:, :, None]
+    begin = begin[:, None, :]
 
     x = inputs[:, 0].reshape(-1, D)
-    cot = cotangent[:, 0].reshape(-1, D)
-    cot_p = dot_nn(cot, pi).astype(BF16)
-    cot_t = lax.dot_general(
-        pi, cot, (((0,), (1,)), ((), ())), preferred_element_type=F32
-    ).astype(BF16)
-
-    xp, nl, q, k, v = project(
+    xp, nl, q, k, v, kv = project(
         x, pi, attention, gain_attn, bias, cos, sin, after=(line_a, shard_b)
     )
     line_b = stacked_rows(line_parts(places, shard_b), after=(q,))
     far_a = send(short_a, places.long)
     short_b, long_b = send(line_b, places.short), send(line_b, places.long)
-    shard_c = shard_of((2, 3), (line_b,))
-
-    forth = [(2 * n, 2 * n + 1) for n in range(n_dev // 2)]
+    shard_c = shard_of((2,), (line_b,))
+
     back = [(2 * n + 1, 2 * n) for n in range(n_dev // 2)]
-    kv = send(jnp.concatenate([k, v], axis=1), forth)
 
     def streams(array):
         return array.reshape(MICRO, here, array.shape[-1])
@@ -1459,47 +1554,61 @@
         attended_flat, xp, attention, gain_mlp, after=(short_b,)
     )
     far_b = send(short_b, places.long)
-    line_c = stacked_rows(line_parts(places, shard_c), after=(normed,))
+    shard_last = shard_of((2,), (attended,))
+    line_c = stacked_rows(line_parts(places, shard_c, shard_last), after=(normed,))
+    shard_d = shard_of((3,), (line_b,))
 
     sums = None
     reductions, feed_pieces = [], []
 
     pieces = [[line_a, short_a, long_a, far_a], [line_b, short_b, long_b, far_b]]
-    at = 0
-    loads = []
+    lines = [line_c]
     for n, wide in enumerate(CHUNKS):
-        coming = (at, CHUNKS[n + 2]) if n + 2 < len(CHUNKS) else None
+        coming = (0, CHUNKS[n + 2]) if n + 2 < len(CHUNKS) else None
         moving = [r for r in reductions if r.next]
         loads = [load for r in moving for load in r.next]
+        if n == 0:
+            loads = [(kind, shard_d) for kind in backwards]
         mlp, d_normed, kept, passed, far, *arrived = feed(
-            n, wide, normed, normed_t, cot_p, cot_t, sums, pieces[n], line_c, coming, loads
+            n, wide, normed, normed_t, cot_p, cot_t, sums, pieces[n],
+            lines[n] if coming else None, coming, loads,
         )
         sums = (mlp, d_normed)
         feed_pieces.append(list(pieces[n]) + [far])
         if coming:
             pieces.append([arrived.pop(0)])
-            at += coming[1]
+        if n == 0:
+            lines.append(stacked_rows([shard_d] + arrived))
         hand_out(moving, arrived)
         reductions.append(Reduce(places, kept, passed))
 
-    moving = [r for r in reductions if r.next]
-    output, d_res, d_att, own_out, other_out, d_gain_mlp, *arrived = middle_back(
+    along = {"long": places.long, "short": places.short}
+
+    def set_off(moving):
+        return [
+            send(array, along[kind] if kind in along else places.ahead[kind[0]])
+            for r in moving
+            for kind, array in r.next
+        ]
+
+    def operands(moving):
+        return tuple(array for r in moving for _, array in r.next)
+
+    moving, newest = [r for r in reductions[:-1] if r.next], reductions[-1:]
+    arrived, arrived_late = set_off(moving), set_off(newest)
+    output, d_res, d_att, own_out, other_out, d_gain_mlp = middle_back(
         residual, sums[0], sums[1], cot_p, attended_flat, pi, attention, gain_mlp,
-        [load for r in moving for load in r.next],
-    )
-    hand_out(moving, arrived)
-    moving = [r for r in reductions if r.next]
-    along = {"long": places.long, "short": places.short}
-    arrived = [
-        send(array, along[kind] if kind in along else places.ahead[kind[0]])
-        for r in moving
-        for kind, array in r.next
-    ]
+        after=operands(moving + newest),
+    )
+    ended = tuple(arrived[: places.line - 1])
+    hand_out(moving, arrived, (d_att,))
+    moving = [r for r in reductions[:-1] if r.next]
+    arrived = set_off(moving)
     dq, dkv, dkv_recv = attend_back(
-        *heads, attended, streams(d_att), lse,
-        after=tuple(array for r in moving for _, array in r.next),
+        *heads, attended, streams(d_att), lse, after=operands(moving) + ended
     )
     dkv_recv = send(dkv_recv, back)
+    hand_out(newest, arrived_late, (dq,))
     hand_out(moving, arrived, (dq,))
     moving = [r for r in reductions if r.next]
     input_grad, own_in, other_in, d_gain_attn, d_bias, *arrived = project_back(
@@ -1518,8 +1627,8 @@
     moving = [r for r in reductions if r.next]
     grad_in, *arrived = reduce_tail(
         places,
-        jnp.concatenate([own_in, riders[:HALF], own_out], axis=1),
-        jnp.concatenate([other_in, riders[HALF:], other_out], axis=1),
+        [own_out, own_in, riders[:HALF]],
+        [other_out, other_in, riders[HALF:]],
         [load for r in moving for load in r.next],
     )
     hand_out(moving, arrived)
@@ -1535,7 +1644,7 @@
         [(w, 2048 + m * FF + o) for m in range(3)] for o, w in zip(OFFSETS, CHUNKS)
     ]
     groups = [r.parts for r in reductions]
-    for start, width, target in ((0, QKV, 0), (QKV, BW, 130 * BW), (QKV + BW, QW, QKV)):
+    for start, width, target in ((0, QW, QKV), (QW, QKV, 0), (QW + QKV, BW, 130 * BW)):
         groups.append([grad_in[:, :, start : start + width]])
         spots.append([(width, target)])
     targets = [

time: 578 us -> 535 us (0.926)
  local copies, waits for them, and re-layouts: 61.5 us -> 26.6 us
  waiting for transfers between devices: 56.3 us -> 38.2 us
  Pallas kernels: 393 us -> 406 us
    unnamed x171 -> x60, local copies, waits for them, and re-layouts: 42.4 us -> 9.12 us
    pallas_call x2, Pallas kernels: 84.1 us -> 54.6 us  [the longest x1 39.7 us: reduce_tail(): pl.pallas_call(functools.partial(tail_kernel, line, places.rows, widths,...]
    ppermute x21 -> x24, waiting for transfers between devices: 34.2 us -> 16.8 us  [send(): return lax.ppermute(array, BOTH, pairs)]
    pallas_call x4, Pallas kernels: 0.91 us -> 13 us  [fold(): pl.pallas_call(following(functools.partial(fold_kernel, len(terms)), len(...]
    pallas_call x4 -> x6, Pallas kernels: 0.9 us -> 12.5 us  [rounded(): pl.pallas_call(following(functools.partial(round_kernel, spans), len(part...]
    pallas_call x1, Pallas kernels: 10.8 us -> 22.3 us  [project(): pl.pallas_call(following(project_kernel, 7, after), grid=(rows // TOKEN_T...]
    pallas_call x4, Pallas kernels: 3.28 us -> 14.1 us  [share(): pl.pallas_call(following(functools.partial(share_kernel, len(terms), rows...]
    pallas_call x1, Pallas kernels: 33.8 us -> 25.6 us  [attend_back(): pl.pallas_call(following(attend_back_kernel, 10, after), grid_spec=pltpu....]
  transfers between devices with their start and end apart: 22 -> 25, of which waited for: 5 -> 3; matrix products, arithmetic and copies ran while one was open for 6% -> 6% of each run, Pallas kernels for 36% -> 44%
where the time goes in v4:
time: 535 us; the launch traced here: 527 us
  Pallas kernels  406 us (76%)
  waiting for transfers between devices  38.2 us (7%)
  starting transfers between devices  37.4 us (7%)
  local copies, waits for them, and re-layouts  26.6 us (5%)
  other arithmetic  8.77 us (2%)
  matrix products  8.35 us (2%)
    pallas_call x4, Pallas kernels, feed(): pl.pallas_call(functools.partial(feed_kernel, wide, started, len(pieces),...  149 us
    pallas_call x1, Pallas kernels, reduce_tail(): pl.pallas_call(functools.partial(tail_kernel, line, places.rows, widths,...  39.7 us
    ppermute x24, starting transfers between devices, send(): return lax.ppermute(array, BOTH, pairs)  33.2 us
    pallas_call x1, Pallas kernels, spread(): pl.pallas_call(functools.partial(spread_kernel, kinds), in_specs=[ANYWHER...  25.6 us
    pallas_call x1, Pallas kernels, attend_back(): pl.pallas_call(following(attend_back_kernel, 10, after), grid_spec=pltpu....  25.6 us
    pallas_call x1, Pallas kernels, project(): pl.pallas_call(following(project_kernel, 7, after), grid=(rows // TOKEN_T...  22.3 us
    all_to_all x1, waiting for transfers between devices, on_device(): lax.all_to_all(slots, BOTH, split_axis=0, concat_axis=1, tiled=True)  21.4 us
    pallas_call x1, Pallas kernels, project_back(): pl.pallas_call(carrying(project_back_kernel, tuple((kind for kind, _ in l...  21.2 us
  transfers between devices with their start and end apart: 25, of which 3 were waited for; matrix products, arithmetic and copies ran while one was open for 6% of the time, Pallas kernels for 44%

profile of v4, /device:TPU:0, one launch (start us, length us, event | category | flops | bytes accessed | tf_op | source)
XLA Modules:
  0.0 526.5 jit_solution(1722435415827686634)
XLA Ops:
  3.7 5.0 collective-permute-start
  13.0 3.5 fusion.5
  27.6 25.6 %spread.1 = (bf16[1,896,2176]{2,1,0:T(8,128)(2,1)}, bf16[3,32,1280]{2,1,0:T(8,128)(2,1)}, bf16[3,32,1280]{2,1,0:T(8,128)(2,1)}, bf16[3,32,1280]{2,1,0:T(8,128)(2,1)}) custom-call(bf16[1,112,2176]{2,1,0:T(8,128)(2,1)} %stacked_rows.5.own, bf16[3,32,1280]{2,1,0:T(8,128)(2,1)} %rounded.7.refs_0_.refs_1_.refs_2_, ...), custom_call_target="tpu_custom_call" | custom-call | flops 1 | bytes 1 | tf_op jit(solution)/shard_map/spread/pallas_call | solution.py:278
  66.5 22.3 %project.1 = (bf16[1024,896]{1,0:T(8,128)(2,1)}, bf16[1024,896]{1,0:T(8,128)(2,1)}, bf16[1024,896]{1,0:T(8,128)(2,1)}, bf16[1024,128]{1,0:T(8,128)(2,1)}, bf16[1...) custom-call(bf16[1024,896]{1,0:T(8,128)(2,1)} %bitcast.67, bf16[896,896]{1,0:T(8,128)(2,1)} %fusion.4.refs_1_.refs_5_.refs_8_, ...), custom_call_target="tpu_custom_call" | custom-call | flops 1 | bytes 1 | tf_op jit(solution)/shard_map/project/pallas_call | solution.py:546
  102.9 12.7 %collective-permute-done.7.refs_4_.refs_7_.refs_9_ = bf16[3,112,1280]{2,1,0:T(8,128)(2,1)S(1)} collective-permute-done((bf16[3,112,1280]{2,1,0:T(8,128)(2,1)}, bf16[3,112,1280]{2,1,0:T(8,128)(2,1)S(1)}, u32[]{:S(2)}, u32[]{:S(2)}) %collective-permute-start.7) | collective-permute-done | bytes 860192 | tf_op jit(solution)/shard_map/ppermute | solution.py:123
  121.4 17.9 %attend.1 = (bf16[2,512,896]{2,1,0:T(8,128)(2,1)}, f32[2,16,512]{2,1,0:T(8,128)}) custom-call(s32[2,4]{1,0:T(2,128)} %and_select_fusion.refs_0_, bf16[2,512,896]{2,1,0:T(8,128)(2,1)} %bitcast.51, bf16[2,512,128]{2,1,0:T(8,128)(2,1)} %bitcast.65, bf16[2,512,128]{2,1,0:T(8,128)(2,1)} %bitcast.69, bf16[2,512,128]{2,1,0:T(8,128)(2,1)} %bitcast.63, ...), custom_call_target="tpu_custom_call" | custom-call | flops 1 | bytes 1 | tf_op jit(solution)/shard_map/attend/pallas_call | solution.py:691
  143.8 8.4 %middle.1 = (f32[1024,896]{1,0:T(8,128)}, bf16[1024,896]{1,0:T(8,128)(2,1)}, bf16[896,1024]{1,0:T(8,128)(2,1)}) custom-call(bf16[1024,896]{1,0:T(8,128)(2,1)} %bitcast.49, bf16[1024,896]{1,0:T(8,128)(2,1)} %get-tuple-element.119.refs_1_.refs_6_, bf16[896,2176]{1,0:T(8,128)(2,1)} %bitcast.40, f32[1,896]{1,0:T(1,128)} %get-tuple-element.274.refs_3_.refs_7_, ...), custom_call_target="tpu_custom_call" | custom-call | flops 1 | bytes 1 | tf_op jit(solution)/shard_map/middle/pallas_call | solution.py:852
  152.9 3.1 stacked_rows.8.refs_8_
  156.0 39.1 %feed.4 = (f32[1024,896]{1,0:T(8,128)}, f32[1024,896]{1,0:T(8,128)}, bf16[3,224,1280]{2,1,0:T(8,128)(2,1)}, bf16[3,224,1280]{2,1,0:T(8,128)(2,1)}, bf16[3,448,12...) custom-call(bf16[1024,896]{1,0:T(8,128)(2,1)} %get-tuple-element.121, ...), custom_call_target="tpu_custom_call" | custom-call | flops 1 | bytes 1 | tf_op jit(solution)/shard_map/feed/pallas_call | solution.py:1139
  198.0 45.2 %feed.5 = (f32[1024,896]{1,0:T(8,128)}, f32[1024,896]{1,0:T(8,128)}, bf16[3,224,1280]{2,1,0:T(8,128)(2,1)}, bf16[3,224,1280]{2,1,0:T(8,128)(2,1)}, bf16[3,448,12...) custom-call(bf16[1024,896]{1,0:T(8,128)(2,1)} %get-tuple-element.121.refs_4_.refs_0_, ...), custom_call_target="tpu_custom_call" | custom-call | flops 1 | bytes 1 | tf_op jit(solution)/shard_map/feed/pallas_call | solution.py:1139
  243.3 3.2 fold.4.refs_7_
  246.5 31.8 %feed.6 = (f32[1024,896]{1,0:T(8,128)}, f32[1024,896]{1,0:T(8,128)}, bf16[3,224,1280]{2,1,0:T(8,128)(2,1)}, bf16[3,224,1280]{2,1,0:T(8,128)(2,1)}, bf16[3,448,12...) custom-call(bf16[1024,896]{1,0:T(8,128)(2,1)} %get-tuple-element.121.refs_4_.refs_0_, ...), custom_call_target="tpu_custom_call" | custom-call | flops 1 | bytes 1 | tf_op jit(solution)/shard_map/feed/pallas_call | solution.py:1139
  278.2 3.6 share.4
  281.8 3.2 fold.5.refs_10_
  285.0 32.7 %feed.7 = (f32[1024,896]{1,0:T(8,128)}, f32[1024,896]{1,0:T(8,128)}, bf16[3,224,1024]{2,1,0:T(8,128)(2,1)}, bf16[3,224,1024]{2,1,0:T(8,128)(2,1)}, bf16[3,448,10...) custom-call(bf16[1024,896]{1,0:T(8,128)(2,1)} %get-tuple-element.121, ...), custom_call_target="tpu_custom_call" | custom-call | flops 1 | bytes 1 | tf_op jit(solution)/shard_map/feed/pallas_call | solution.py:1139
  317.7 3.3 fold.6.refs_11_
  323.4 3.5 share.5
  330.8 14.9 %middle_back.1 = (bf16[1024,896]{1,0:T(8,128)(2,1)}, f32[1024,896]{1,0:T(8,128)}, bf16[1024,896]{1,0:T(8,128)(2,1)}, bf16[448,896]{1,0:T(8,128)(2,1)}, bf16[448,896]{1,0:T(8,128)(2,1)}, /*index=5*/f32[1,896]{1,0:T(1,128)}) custom-call(f32[1024,896]{1,0:T(8,128)} %get-tuple-element.120.refs_0_, f32[1024,896]{1,0:T(8,128)} %get-tuple-element.145.refs_1_, ...), custom_call_target="tpu_custom_call" | custom-call | flops 1 | bytes 1 | tf_op jit(solution)/shard_map/middle_back/pallas_call | solution.py:911
  345.7 3.6 share.6
  350.2 25.6 %attend_back.1 = (bf16[2,512,896]{2,1,0:T(8,128)(2,1)}, f32[2,512,256]{2,1,0:T(8,128)}, bf16[2,512,256]{2,1,0:T(8,128)(2,1)}) custom-call(s32[2,4]{1,0:T(2,128)} %and_select_fusion.refs_0_, bf16[2,512,896]{2,1,0:T(8,128)(2,1)} %bitcast.52, bf16[2,512,128]{2,1,0:T(8,128)(2,1)} %bitcast.66, bf16[2,512,128]{2,1,0:T(8,128)(2,1)} %bitcast.70, ...), custom_call_target="tpu_custom_call" | custom-call | flops 1 | bytes 1 | tf_op jit(solution)/shard_map/attend_back/pallas_call | solution.py:800
  379.0 3.5 collective-permute-start.23
  383.6 3.3 fold.7.refs_11_
  386.9 4.1 collective-permute-done.19
  391.1 21.2 %project_back.1 = (f32[1024,896]{1,0:T(8,128)}, bf16[448,1152]{1,0:T(8,128)(2,1)}, bf16[448,1152]{1,0:T(8,128)(2,1)}, f32[1,896]{1,0:T(1,128)}, f32[1,1152]{1,0:T(1,128)}, /*index=5*/bf16[3,112,1024]{2,1,0:T(8,128)(2,1)}) custom-call(bf16[1024,896]{1,0:T(8,128)(2,1)} %bitcast.58, f32[1024,256]{1,0:T(8,128)} %bitcast.68, bf16[1024,256]{1,0:T(8,128)(2,1)} %bitcast.19.refs_2_, ...), custom_call_target="tpu_custom_call" | custom-call | flops 1 | bytes 1 | tf_op jit(solution)/shard_map/project_back/pallas_call | solution.py:1230
  416.2 3.4 share.7
  420.3 39.7 %reduce_tail.1 = (f32[1,28,2176]{2,1,0:T(8,128)}, bf16[3,32,1024]{2,1,0:T(8,128)(2,1)}, bf16[3,32,1024]{2,1,0:T(8,128)(2,1)}, bf16[3,32,1024]{2,1,0:T(8,128)(2,1)}) custom-call(bf16[448,896]{1,0:T(8,128)(2,1)} %get-tuple-element.175.refs_0_, bf16[448,1152]{1,0:T(8,128)(2,1)} %get-tuple-element.176.refs_1_, bf16[448,128]{1,0:T(8,128)(2,1)} %get-tuple-element.273.refs_2_, ...), custom_call_target="tpu_custom_call" | custom-call | flops 1 | bytes 1 | tf_op jit(solution)/shard_map/reduce_tail/pallas_call | solution.py:431
  465.3 6.4 %packed.1 = (f32[28,896]{1,0:T(8,128)}, f32[28,128]{1,0:T(8,128)}, f32[28,128]{1,0:T(8,128)}, f32[28,896]{1,0:T(8,128)}, f32[28,4864]{1,0:T(8,128)}, /*index=5*/...) custom-call(s32[160]{0:T(256)} %scatter_custom_fusion.block_ref, ...), custom_call_target="tpu_custom_call" | custom-call | flops 1 | bytes 1 | tf_op jit(solution)/shard_map/packed/pallas_call | solution.py:1388
  471.7 4.2 all-to-all-start
  476.6 8.5 %picked.1.weight_ref = f32[5,896,128]{2,1,0:T(8,128)} custom-call(s32[5]{0:T(128)} %dynamic_slice.3.refs_0_.block_ref, bf16[896,896]{1,0:T(8,128)(2,1)} %fusion.4.refs_1_.refs_5_.refs_8_, bf16[1,896,2176]{2,1,0:T(8,128)(2,1)} %get-tuple-element.110.refs_3_.refs_2_, bf16[3,112,1280]{2,1,0:T(8,128)(2,1)} %stacked_rows.6.refs_7_.refs_4_.refs_3_, ...), custom_call_target="tpu_custom_call" | custom-call | flops 1 | bytes 1 | tf_op jit(solution)/shard_map/picked/pallas_call | solution.py:1320
  486.4 21.4 %all-to-all-done = bf16[160,28,128]{2,1,0:T(8,128)(2,1)S(1)} async-done(((bf16[160,28,128]{2,1,0:T(8,128)(2,1)}), bf16[160,28,128]{2,1,0:T(8,128)(2,1)S(1)}, u32[]{:S(2)}, u32[]{:S(2)}) %all-to-all-start) | async-done | bytes 1146912 | tf_op jit(solution)/shard_map/all_to_all | solution.py:1658
  509.2 12.5 %rotated_adam.1 = (f32[5,896,128]{2,1,0:T(8,128)}, f32[5,896,128]{2,1,0:T(8,128)}, f32[5,896,128]{2,1,0:T(8,128)}) custom-call(s32[5]{0:T(128)} %dynamic_slice.3.refs_0_.block_ref, bf16[5,896,128]{2,1,0:T(8,128)(2,1)} %all_to_all.16.grad_ref, f32[5,896,128]{2,1,0:T(8,128)} %picked.1.weight_ref, f32[5,896,128]{2,1,0:T(8,128)} %first_ref.1, ...), custom_call_target="tpu_custom_call" | custom-call | flops 1 | bytes 1 | tf_op jit(solution)/shard_map/rotated_adam/pallas_call | solution.py:1407
  521.7 4.2 copy.77
  (157 shorter events, 84.1 us)
Async XLA Ops:
  3.7 21.2 %collective-permute-start = (bf16[1,32,2176]{2,1,0:T(8,128)(2,1)}, bf16[1,32,2176]{2,1,0:T(8,128)(2,1)S(1)}, u32[]{:S(2)}, u32[]{:S(2)}) collective-permute-start(bf16[1,32,2176]{2,1,0:T(8,128)(2,1)} %rounded.6.refs_0_), channel_id=1, source_target_pairs={{0,24},{1,25},{2,26},{3,27},{4,28},{5,29},{6,30},{7,31},{8,0},{9,1... | collective-permute-start | bytes 417800 | tf_op jit(solution)/shard_map/ppermute | solution.py:123
  8.8 16.1 %collective-permute-start.1 = (bf16[1,32,2176]{2,1,0:T(8,128)(2,1)}, bf16[1,32,2176]{2,1,0:T(8,128)(2,1)}, u32[]{:S(2)}, u32[]{:S(2)}) collective-permute-start(bf16[1,32,2176]{2,1,0:T(8,128)(2,1)} %rounded.6.refs_0_), channel_id=1, source_target_pairs={{0,16},{1,17},{2,18},{3,19},{4,20},{5,21},{6,22},{7,23},{8,24},{9,... | collective-permute-start | bytes 417800 | tf_op jit(solution)/shard_map/ppermute | solution.py:123
  8.8 16.1 %collective-permute-start.2 = (bf16[1,32,2176]{2,1,0:T(8,128)(2,1)}, bf16[1,32,2176]{2,1,0:T(8,128)(2,1)}, u32[]{:S(2)}, u32[]{:S(2)}) collective-permute-start(bf16[1,32,2176]{2,1,0:T(8,128)(2,1)} %rounded.6.refs_0_), channel_id=1, source_target_pairs={{0,8},{1,9},{2,10},{3,11},{4,12},{5,13},{6,14},{7,15},{8,16},{9,17... | collective-permute-start | bytes 417800 | tf_op jit(solution)/shard_map/ppermute | solution.py:123
  11.3 48.7 %copy-start.20 = (s32[896]{0:T(1024)}, s32[896]{0:T(1024)S(1)}, u32[]{:S(2)}) copy-start(s32[896]{0:T(1024)S(1)} %fusion.41) | copy-start | bytes 10756
  55.3 33.5 %collective-permute-start.3 = (bf16[3,32,1280]{2,1,0:T(8,128)(2,1)}, bf16[3,32,1280]{2,1,0:T(8,128)(2,1)S(1)}, u32[]{:S(2)}, u32[]{:S(2)}) collective-permute-start(bf16[3,32,1280]{2,1,0:T(8,128)(2,1)} %rounded.8.refs_8_.refs_0_), channel_id=1, source_target_pairs={{0,24},{1,25},{2,26},{3,27},{4,28},{5,29},{6,30},{7,31},{8,0},{9,1... | collective-permute-start | bytes 737288 | tf_op jit(solution)/shard_map/ppermute | solution.py:123
  57.3 31.6 %collective-permute-start.4 = (bf16[3,32,1280]{2,1,0:T(8,128)(2,1)}, bf16[3,32,1280]{2,1,0:T(8,128)(2,1)S(1)}, u32[]{:S(2)}, u32[]{:S(2)}) collective-permute-start(bf16[3,32,1280]{2,1,0:T(8,128)(2,1)} %rounded.8.refs_8_.refs_0_), channel_id=1, source_target_pairs={{0,16},{1,17},{2,18},{3,19},{4,20},{5,21},{6,22},{7,23},{8,24},{9,... | collective-permute-start | bytes 737288 | tf_op jit(solution)/shard_map/ppermute | solution.py:123
  58.0 30.9 %collective-permute-start.5 = (bf16[3,32,1280]{2,1,0:T(8,128)(2,1)}, bf16[3,32,1280]{2,1,0:T(8,128)(2,1)S(1)}, u32[]{:S(2)}, u32[]{:S(2)}) collective-permute-start(bf16[3,32,1280]{2,1,0:T(8,128)(2,1)} %rounded.8.refs_8_.refs_0_), channel_id=1, source_target_pairs={{0,8},{1,9},{2,10},{3,11},{4,12},{5,13},{6,14},{7,15},{8,16},{9,17... | collective-permute-start | bytes 737288 | tf_op jit(solution)/shard_map/ppermute | solution.py:123
  64.3 36.5 %collective-permute-start.6 = (bf16[3,112,1280]{2,1,0:T(8,128)(2,1)}, bf16[3,112,1280]{2,1,0:T(8,128)(2,1)S(1)}, u32[]{:S(2)}, u32[]{:S(2)}) collective-permute-start(bf16[3,112,1280]{2,1,0:T(8,128)(2,1)} %stacked_rows.6.refs_7_.refs_4_.refs_3_), channel_id=1, source_target_pairs={{0,1},{1,0},{2,6},{3,7},{4,5},{5,4},{6,2},{7,3},{8,9},{9,8},{10,14... | collective-permute-start | bytes 2580488 | tf_op jit(solution)/shard_map/ppermute | solution.py:123
  92.8 24.4 %copy-start.22 = (s32[2,512]{1,0:T(2,128)S(1)}, s32[2,512]{1,0:T(2,128)}, u32[]{:S(2)}) copy-start(s32[2,512]{1,0:T(2,128)} %get-tuple-element.280) | copy-start | bytes 12292
  92.8 22.8 %collective-permute-start.7 = (bf16[3,112,1280]{2,1,0:T(8,128)(2,1)}, bf16[3,112,1280]{2,1,0:T(8,128)(2,1)S(1)}, u32[]{:S(2)}, u32[]{:S(2)}) collective-permute-start(bf16[3,112,1280]{2,1,0:T(8,128)(2,1)} %stacked_rows.7.refs_3_.refs_7_.refs_6_.refs_8_), channel_id=1, source_target_pairs={{0,1},{1,0},{2,6},{3,7},{4,5},{5,4},{6,2},{7,3},{8,9},{9,8},{10,14... | collective-permute-start | bytes 2580488 | tf_op jit(solution)/shard_map/ppermute | solution.py:123
  97.6 19.7 %collective-permute-start.10 = (bf16[3,32,1280]{2,1,0:T(8,128)(2,1)}, bf16[3,32,1280]{2,1,0:T(8,128)(2,1)}, u32[]{:S(2)}, u32[]{:S(2)}) collective-permute-start(bf16[3,32,1280]{2,1,0:T(8,128)(2,1)} %rounded.9.refs_9_.refs_0_), channel_id=1, source_target_pairs={{0,24},{1,25},{2,26},{3,27},{4,28},{5,29},{6,30},{7,31},{8,0},{9,1... | collective-permute-start | bytes 737288 | tf_op jit(solution)/shard_map/ppermute | solution.py:123
  99.6 56.3 %collective-permute-start.8 = (bf16[3,112,1280]{2,1,0:T(8,128)(2,1)S(1)}, bf16[3,112,1280]{2,1,0:T(8,128)(2,1)}, u32[]{:S(2)}, u32[]{:S(2)}) collective-permute-start(bf16[3,112,1280]{2,1,0:T(8,128)(2,1)S(1)} %copy-done.4), channel_id=1, source_target_pairs={{0,4},{1,5},{2,3},{3,2},{4,0},{5,1},{6,7},{7,6},{8,12},{9,13},{10,... | collective-permute-start | bytes 2580488 | tf_op jit(solution)/shard_map/ppermute | solution.py:123
  100.9 20.5 %copy-start.5 = (bf16[3,112,1280]{2,1,0:T(8,128)(2,1)}, bf16[3,112,1280]{2,1,0:T(8,128)(2,1)S(1)}, u32[]{:S(2)}) copy-start(bf16[3,112,1280]{2,1,0:T(8,128)(2,1)S(1)} %collective-permute-done.6.refs_8_.refs_5_.refs_4_) | copy-start | bytes 2580484
  100.9 55.1 %collective-permute-start.9 = (bf16[3,112,1280]{2,1,0:T(8,128)(2,1)S(1)}, bf16[3,112,1280]{2,1,0:T(8,128)(2,1)}, u32[]{:S(2)}, u32[]{:S(2)}) collective-permute-start(bf16[3,112,1280]{2,1,0:T(8,128)(2,1)S(1)} %collective-permute-done.6.refs_8_.refs_5_.refs_4_), channel_id=1, source_target_pairs={{0,4},{1,5},{2,3},{3,2},{4,0},{5,1},{6,7},{7,6},{8,12},{9,13},{10,... | collective-permute-start | bytes 2580488 | tf_op jit(solution)/shard_map/ppermute | solution.py:123
  101.7 96.3 %collective-permute-start.13 = (bf16[3,112,1280]{2,1,0:T(8,128)(2,1)S(1)}, bf16[3,112,1280]{2,1,0:T(8,128)(2,1)}, u32[]{:S(2)}, u32[]{:S(2)}) collective-permute-start(bf16[3,112,1280]{2,1,0:T(8,128)(2,1)S(1)} %copy-done.3), channel_id=1, source_target_pairs={{0,4},{1,5},{2,3},{3,2},{4,0},{5,1},{6,7},{7,6},{8,12},{9,13},{10,... | collective-permute-start | bytes 2580488 | tf_op jit(solution)/shard_map/ppermute | solution.py:123
  115.6 23.7 %copy-start.6 = (bf16[3,112,1280]{2,1,0:T(8,128)(2,1)}, bf16[3,112,1280]{2,1,0:T(8,128)(2,1)S(1)}, u32[]{:S(2)}) copy-start(bf16[3,112,1280]{2,1,0:T(8,128)(2,1)S(1)} %collective-permute-done.7.refs_4_.refs_7_.refs_9_) | copy-start | bytes 2580484
  115.6 82.4 %collective-permute-start.14 = (bf16[3,112,1280]{2,1,0:T(8,128)(2,1)S(1)}, bf16[3,112,1280]{2,1,0:T(8,128)(2,1)}, u32[]{:S(2)}, u32[]{:S(2)}) collective-permute-start(bf16[3,112,1280]{2,1,0:T(8,128)(2,1)S(1)} %collective-permute-done.7.refs_4_.refs_7_.refs_9_), channel_id=1, source_target_pairs={{0,4},{1,5},{2,3},{3,2},{4,0},{5,1},{6,7},{7,6},{8,12},{9,13},{10,... | collective-permute-start | bytes 2580488 | tf_op jit(solution)/shard_map/ppermute | solution.py:123
  117.3 24.2 %collective-permute-start.11 = (bf16[3,32,1280]{2,1,0:T(8,128)(2,1)}, bf16[3,32,1280]{2,1,0:T(8,128)(2,1)S(1)}, u32[]{:S(2)}, u32[]{:S(2)}) collective-permute-start(bf16[3,32,1280]{2,1,0:T(8,128)(2,1)} %rounded.9.refs_9_.refs_0_), channel_id=1, source_target_pairs={{0,16},{1,17},{2,18},{3,19},{4,20},{5,21},{6,22},{7,23},{8,24},{9,... | collective-permute-start | bytes 737288 | tf_op jit(solution)/shard_map/ppermute | solution.py:123
  141.5 10.7 %collective-permute-start.12 = (bf16[3,32,1280]{2,1,0:T(8,128)(2,1)}, bf16[3,32,1280]{2,1,0:T(8,128)(2,1)S(1)}, u32[]{:S(2)}, u32[]{:S(2)}) collective-permute-start(bf16[3,32,1280]{2,1,0:T(8,128)(2,1)} %rounded.10), channel_id=1, source_target_pairs={{0,8},{1,9},{2,10},{3,11},{4,12},{5,13},{6,14},{7,15},{8,16},{9,17... | collective-permute-start | bytes 737288 | tf_op jit(solution)/shard_map/ppermute | solution.py:123
  321.0 24.8 %collective-permute-start.15 = (bf16[3,112,1280]{2,1,0:T(8,128)(2,1)}, bf16[3,112,1280]{2,1,0:T(8,128)(2,1)}, u32[]{:S(2)}, u32[]{:S(2)}) collective-permute-start(bf16[3,112,1280]{2,1,0:T(8,128)(2,1)} %fold.6.refs_11_), channel_id=1, source_target_pairs={{0,1},{1,0},{2,6},{3,7},{4,5},{5,4},{6,2},{7,3},{8,9},{9,8},{10,14... | collective-permute-start | bytes 2580488 | tf_op jit(solution)/shard_map/ppermute | solution.py:123
  322.8 59.7 %collective-permute-start.20 = (bf16[3,224,1024]{2,1,0:T(8,128)(2,1)S(1)}, bf16[3,224,1024]{2,1,0:T(8,128)(2,1)S(1)}, u32[]{:S(2)}, u32[]{:S(2)}) collective-permute-start(bf16[3,224,1024]{2,1,0:T(8,128)(2,1)S(1)} %copy-done.8), channel_id=1, source_target_pairs={{0,4},{1,5},{2,3},{3,2},{4,0},{5,1},{6,7},{7,6},{8,12},{9,13},{10,... | collective-permute-start | bytes 4128776 | tf_op jit(solution)/shard_map/ppermute | solution.py:123
  326.9 22.4 %collective-permute-start.16 = (bf16[3,32,1280]{2,1,0:T(8,128)(2,1)}, bf16[3,32,1280]{2,1,0:T(8,128)(2,1)S(1)}, u32[]{:S(2)}, u32[]{:S(2)}) collective-permute-start(bf16[3,32,1280]{2,1,0:T(8,128)(2,1)} %get-tuple-element.148.refs_8_), channel_id=1, source_target_pairs={{0,8},{1,9},{2,10},{3,11},{4,12},{5,13},{6,14},{7,15},{8,16},{9,17... | collective-permute-start | bytes 737288 | tf_op jit(solution)/shard_map/ppermute | solution.py:123
  327.5 21.8 %collective-permute-start.17 = (bf16[3,32,1280]{2,1,0:T(8,128)(2,1)}, bf16[3,32,1280]{2,1,0:T(8,128)(2,1)S(1)}, u32[]{:S(2)}, u32[]{:S(2)}) collective-permute-start(bf16[3,32,1280]{2,1,0:T(8,128)(2,1)} %get-tuple-element.149.refs_9_), channel_id=1, source_target_pairs={{0,16},{1,17},{2,18},{3,19},{4,20},{5,21},{6,22},{7,23},{8,24},{9,... | collective-permute-start | bytes 737288 | tf_op jit(solution)/shard_map/ppermute | solution.py:123
  329.3 20.0 %collective-permute-start.18 = (bf16[3,32,1280]{2,1,0:T(8,128)(2,1)}, bf16[3,32,1280]{2,1,0:T(8,128)(2,1)S(1)}, u32[]{:S(2)}, u32[]{:S(2)}) collective-permute-start(bf16[3,32,1280]{2,1,0:T(8,128)(2,1)} %get-tuple-element.150.refs_10_), channel_id=1, source_target_pairs={{0,24},{1,25},{2,26},{3,27},{4,28},{5,29},{6,30},{7,31},{8,0},{9,1... | collective-permute-start | bytes 737288 | tf_op jit(solution)/shard_map/ppermute | solution.py:123
  350.2 26.8 %copy-start.24 = (s32[130]{0:T(256)S(1)}, s32[130]{0:T(256)}, u32[]{:S(2)}) copy-start(s32[130]{0:T(256)} %param.29) | copy-start | bytes 1564
  375.7 15.3 %collective-permute-start.19 = (bf16[2,512,256]{2,1,0:T(8,128)(2,1)}, bf16[2,512,256]{2,1,0:T(8,128)(2,1)}, u32[]{:S(2)}, u32[]{:S(2)}) collective-permute-start(bf16[2,512,256]{2,1,0:T(8,128)(2,1)} %get-tuple-element.162), channel_id=1, source_target_pairs={{1,0},{3,2},{5,4},{7,6},{9,8},{11,10},{13,12},{15,14},{17,16},{19,... | collective-permute-start | bytes 1572872 | tf_op jit(solution)/shard_map/ppermute | solution.py:123
  378.7 85.8 %collective-permute-start.21 = (bf16[3,32,1280]{2,1,0:T(8,128)(2,1)}, bf16[3,32,1280]{2,1,0:T(8,128)(2,1)S(1)}, u32[]{:S(2)}, u32[]{:S(2)}) collective-permute-start(bf16[3,32,1280]{2,1,0:T(8,128)(2,1)} %get-tuple-element.157.refs_10_), channel_id=1, source_target_pairs={{0,8},{1,9},{2,10},{3,11},{4,12},{5,13},{6,14},{7,15},{8,16},{9,17... | collective-permute-start | bytes 737288 | tf_op jit(solution)/shard_map/ppermute | solution.py:123
  378.7 85.8 %collective-permute-start.22 = (bf16[3,32,1280]{2,1,0:T(8,128)(2,1)}, bf16[3,32,1280]{2,1,0:T(8,128)(2,1)S(1)}, u32[]{:S(2)}, u32[]{:S(2)}) collective-permute-start(bf16[3,32,1280]{2,1,0:T(8,128)(2,1)} %get-tuple-element.158.refs_11_), channel_id=1, source_target_pairs={{0,16},{1,17},{2,18},{3,19},{4,20},{5,21},{6,22},{7,23},{8,24},{9,... | collective-permute-start | bytes 737288 | tf_op jit(solution)/shard_map/ppermute | solution.py:123
  379.0 85.5 %collective-permute-start.23 = (bf16[3,32,1280]{2,1,0:T(8,128)(2,1)}, bf16[3,32,1280]{2,1,0:T(8,128)(2,1)}, u32[]{:S(2)}, u32[]{:S(2)}) collective-permute-start(bf16[3,32,1280]{2,1,0:T(8,128)(2,1)} %get-tuple-element.159.refs_12_), channel_id=1, source_target_pairs={{0,24},{1,25},{2,26},{3,27},{4,28},{5,29},{6,30},{7,31},{8,0},{9,1... | collective-permute-start | bytes 737288 | tf_op jit(solution)/shard_map/ppermute | solution.py:123
  391.1 21.9 %copy-start.21 = (s32[896]{0:T(1024)S(1)}, s32[896]{0:T(1024)}, u32[]{:S(2)}) copy-start(s32[896]{0:T(1024)} %copy-done.20) | copy-start | bytes 10756
  391.1 21.9 %copy-start.28 = (f32[1,896]{1,0:T(1,128)S(1)}, f32[1,896]{1,0:T(1,128)}, u32[]{:S(2)}) copy-start(f32[1,896]{1,0:T(1,128)} %get-tuple-element.178) | copy-start | bytes 10756
  471.7 36.1 %all-to-all-start = ((bf16[160,28,128]{2,1,0:T(8,128)(2,1)}), bf16[160,28,128]{2,1,0:T(8,128)(2,1)S(1)}, u32[]{:S(2)}, u32[]{:S(2)}) async-start(bf16[160,28,128]{2,1,0:T(8,128)(2,1)} %get-tuple-element.197.refs_17_), calls=%async_computation | async-start | bytes 2621440 | tf_op jit(solution)/shard_map/all_to_all | solution.py:1658
  (22 other events, 90.8 us)
